TPU v7x, 256 devices: a whole 4x4x8 slice. The times are simulated.
256 devices in a mesh: gz: 32 (over y_lo, z, core), gy: 8 (over x, y_hi).
Axes of the slice: x: 4, y: 4 (y_hi: 2, y_lo: 2; y = y_hi * 2 + y_lo), z: 8, core: 2. Of those that a mesh axis runs over, the one named last changes fastest.
Arguments:
- wave_now: float32 [128, 256, 512], P('gz', 'gy'), may hold values from -6 to 6
- wave_later: float32 [128, 256, 512], P('gz', 'gy'), may hold values from -6 to 6
- adjoint_now: float32 [128, 256, 512], P('gz', 'gy'), may hold values from -6 to 6
- adjoint_later: float32 [128, 256, 512], P('gz', 'gy'), may hold values from -6 to 6
- velocity: float32 [128, 256, 512], P('gz', 'gy'), may hold values from 1.5 to 4.5
- observed: float32 [2, 4096], P(None, ('gz', 'gy')), may hold values from -6 to 6
- receivers: int32 [3, 4096], replicated, may hold values from 0 to 511, as said below
- sources: int32 [3, 4], replicated, may hold values from 0 to 511, as said below
- wavelet: float32 [2, 4], replicated, may hold values from -40 to 40
Outputs:
- wave_first: float32 [128, 256, 512], P('gz', 'gy')
- wave_second: float32 [128, 256, 512], P('gz', 'gy')
- adjoint_first: float32 [128, 256, 512], P('gz', 'gy')
- adjoint_second: float32 [128, 256, 512], P('gz', 'gy')
- gradient: float32 [128, 256, 512], P('gz', 'gy')
Inputs may be any that keep to these rules, and one draw needn't show every extreme that they name: `receivers`: row 0 holds depth indices below 128, row 1 y indices below 256, row 2 x indices below 512. `sources`: row 0 holds depth indices below 128, row 1 y indices below 256, row 2 x indices below 512.
All inputs are finite; a program needn't handle non-finite values.
Results may differ from a plain program's by a relative error of at most 0.00015.
Values sent between devices are 32-bit elements; how exact they have to be, the bound alone decides.
No kernel may reach another device: no remote copies, remote signals or barrier semaphores. Data moves between devices by JAX's collectives and lax.ppermute only.
A program may use at most 64 MiB of HBM per device.

v0:
```python
import math

import jax
import jax.numpy as jnp
from jax import lax
from jax.sharding import PartitionSpec as P

STEPS = 2


centre_coef = -7.5
near_coef = 4.0 / 3.0
far_coef = -1.0 / 12.0
time_ratio = 0.1
damp_peak = 0.3


def padded_2(value, sides, width, wrap):
    for axis, dim in sides:
        size, length = (lax.axis_size(axis), value.shape[dim])
        up = [(i, (i + 1) % size) for i in range(size if wrap else size - 1)]
        down = [(j, i) for i, j in up]
        last = lax.slice_in_dim(value, length - width, length, axis=dim)
        initial = lax.slice_in_dim(value, 0, width, axis=dim)
        before = lax.ppermute(last, axis, up)
        after = lax.ppermute(initial, axis, down)
        value = jnp.concatenate([before, value, after], axis=dim)
    return value


def laplace(padded):
    centre = padded[..., 2:-2, 2:-2, :]
    widths = [(0, 0)] * (centre.ndim - 1) + [(2, 2)]
    x_padded = jnp.pad(centre, widths)
    near_sum = (
        padded[..., 3:-1, 2:-2, :]
        + padded[..., 1:-3, 2:-2, :]
        + padded[..., 2:-2, 3:-1, :]
        + padded[..., 2:-2, 1:-3, :]
        + x_padded[..., 3:-1]
        + x_padded[..., 1:-3]
    )
    far_sum = (
        padded[..., 4:, 2:-2, :]
        + padded[..., :-4, 2:-2, :]
        + padded[..., 2:-2, 4:, :]
        + padded[..., 2:-2, :-4, :]
        + x_padded[..., 4:]
        + x_padded[..., :-4]
    )
    return centre_coef * centre + near_coef * near_sum + far_coef * far_sum


def damping(z_index, z_total, sponge):
    z_float = jnp.clip(z_index, 0, z_total - 1).astype(jnp.float32)
    near_low = jnp.maximum(sponge - z_float, 0.0) / sponge
    near_high = jnp.maximum(z_float - (z_total - 1 - sponge), 0.0) / sponge
    return damp_peak * (near_low * near_low + near_high * near_high)


def update(
    wave_cur,
    adjoint_cur,
    wave_after,
    adjoint_after,
    lap_wave,
    lap_adjoint,
    speed_field,
    absorb,
    source,
    inject,
):
    courant = (speed_field * time_ratio) ** 2
    wave_before = (2.0 * wave_cur - (1.0 + absorb) * wave_after + courant * (lap_wave + source)) / (
        1.0 - absorb
    )
    adjoint_before = (
        2.0 * adjoint_cur - (1.0 - absorb) * adjoint_after + courant * lap_adjoint + inject
    ) / (1.0 + absorb)
    grad_term = 2.0 / speed_field * adjoint_cur * (wave_after - 2.0 * wave_cur + wave_before)
    return (wave_before, adjoint_before, grad_term)


def cell_codes(points, z_first, y_first, z_count, y_count, y_total):
    loc_z = points[0] - z_first
    loc_y = jnp.mod(points[1] - y_first, y_total)
    inside = (loc_z >= 0) & (loc_z < z_count) & (loc_y < y_count)
    row_code = jnp.where(inside, loc_z * y_count + loc_y, -1)
    return (row_code, points[2], inside)


def block_count(total):
    return total // math.gcd(total, 2048)


def sample_cells(field, row_code, column):
    z_count, y_count, x_total = field.shape
    rows = z_count * y_count
    flat = field.reshape(rows, x_total)
    total = row_code.shape[0]
    blocks = block_count(total)
    row_iota = jnp.arange(rows, dtype=jnp.int32)
    x_iota = jnp.arange(x_total, dtype=jnp.int32)

    def one_block(pair):
        codes, columns = pair
        pick_rows = (codes[:, None] == row_iota[None, :]).astype(jnp.float32)
        picked = jnp.dot(
            pick_rows, flat, precision=lax.Precision.HIGHEST, preferred_element_type=jnp.float32
        )
        return jnp.sum(jnp.where(columns[:, None] == x_iota[None, :], picked, 0.0), axis=1)

    values = lax.map(
        one_block,
        (row_code.reshape(blocks, total // blocks), column.reshape(blocks, total // blocks)),
    )
    return values.reshape(total)


def place_cells(values, row_code, column, z_count, y_count, x_total):
    rows = z_count * y_count
    total = row_code.shape[0]
    blocks = block_count(total)
    row_iota = jnp.arange(rows, dtype=jnp.int32)
    x_iota = jnp.arange(x_total, dtype=jnp.int32)

    def add_block(grid, triple):
        codes, columns, amounts = triple
        pick_rows = (codes[:, None] == row_iota[None, :]).astype(jnp.float32)
        spread = jnp.where(columns[:, None] == x_iota[None, :], amounts[:, None], 0.0)
        added = lax.dot_general(
            pick_rows,
            spread,
            (((0,), (0,)), ((), ())),
            precision=lax.Precision.HIGHEST,
            preferred_element_type=jnp.float32,
        )
        return (grid + added, None)

    width = total // blocks
    grid, unused = lax.scan(
        add_block,
        jnp.zeros((rows, x_total), jnp.float32),
        (
            row_code.reshape(blocks, width),
            column.reshape(blocks, width),
            values.reshape(blocks, width),
        ),
    )
    return grid.reshape(z_count, y_count, x_total)


def shards(
    wave_now,
    wave_later,
    adjoint_now,
    adjoint_later,
    velocity,
    observed,
    receivers,
    sources,
    wavelet,
):
    slab_z, slab_y, x_total = wave_now.shape
    z_total = slab_z * lax.axis_size("gz")
    y_total = slab_y * lax.axis_size("gy")
    z_start = lax.axis_index("gz") * slab_z
    y_start = lax.axis_index("gy") * slab_y
    gradient = jnp.zeros(wave_now.shape, jnp.float32)
    wave_cur, wave_after = (wave_now, wave_later)
    adjoint_cur, adjoint_after = (adjoint_now, adjoint_later)
    for step_index in range(STEPS):
        row_code, column, inside = cell_codes(
            receivers, z_start, y_start, wave_cur.shape[0], wave_cur.shape[1], y_total
        )
        sampled = sample_cells(wave_cur, row_code, column)
        predicted = lax.psum_scatter(sampled, ("gz", "gy"), scatter_dimension=0, tiled=True)
        owned = predicted - observed[step_index]
        residual = lax.all_gather(owned, ("gz", "gy"), axis=0, tiled=True)
        stacked = jnp.stack([wave_cur, adjoint_cur])
        rimmed_y = padded_2(stacked, (("gy", 2),), 2, True)
        padded = padded_2(rimmed_y, (("gz", 1),), 2, False)
        z_count = wave_after.shape[0]
        y_count = wave_after.shape[1]
        z_global = z_start + jnp.arange(z_count, dtype=jnp.int32)
        inside_z = ((z_global >= 0) & (z_global < z_total))[:, None, None]
        absorb = damping(z_global, z_total, slab_z)[:, None, None]
        speed_safe = jnp.where(inside_z, velocity, 1.0)
        lapped = laplace(padded)
        centre = padded[:, 2:-2, 2:-2, :]
        source_rows, source_columns, source_inside = cell_codes(
            sources, z_start, y_start, z_count, y_count, y_total
        )
        source = place_cells(
            wavelet[step_index], source_rows, source_columns, z_count, y_count, x_total
        )
        receiver_rows, receiver_columns, receiver_inside = cell_codes(
            receivers, z_start, y_start, z_count, y_count, y_total
        )
        inject = place_cells(residual, receiver_rows, receiver_columns, z_count, y_count, x_total)
        wave_before, adjoint_before, grad_term = update(
            centre[0],
            centre[1],
            wave_after,
            adjoint_after,
            lapped[0],
            lapped[1],
            speed_safe,
            absorb,
            source,
            inject,
        )
        wave_before, adjoint_before, grad_term = (
            jnp.where(inside_z, wave_before, 0.0),
            jnp.where(inside_z, adjoint_before, 0.0),
            grad_term,
        )
        gradient = gradient + grad_term
        wave_after, wave_cur = (wave_cur, wave_before)
        adjoint_after, adjoint_cur = (adjoint_cur, adjoint_before)
    return (wave_cur, wave_after, adjoint_cur, adjoint_after, gradient)


def solution(mesh):
    return jax.shard_map(
        shards,
        mesh=mesh,
        in_specs=(
            P("gz", "gy", None),
            P("gz", "gy", None),
            P("gz", "gy", None),
            P("gz", "gy", None),
            P("gz", "gy", None),
            P(None, ("gz", "gy")),
            P(),
            P(),
            P(),
        ),
        out_specs=(
            P("gz", "gy", None),
            P("gz", "gy", None),
            P("gz", "gy", None),
            P("gz", "gy", None),
            P("gz", "gy", None),
        ),
        check_vma=False,
    )
```

profile of v0, /device:TPU:1, one launch (start us, length us, event | category | flops | bytes accessed | tf_op | source)
XLA Modules:
  0.0 222.6 jit_solution(16481008250022961365)
XLA Ops:
  0.6 1.0 fusion.75
  1.6 3.8 %collective-permute-start = (f32[2,4,2,512]{3,2,1,0:T(2,128)S(1)}, f32[2,4,2,512]{3,2,1,0:T(2,128)S(1)}, u32[]{:S(2)}, u32[]{:S(2)}) collective-permute-start(f32[2,4,2,512]{3,2,1,0:T(2,128)S(1)} %get-tuple-element.344), channel_id=1, source_target_pairs={{0,1},{1,2},{2,3},{3,4},{4,5},{5,6},{6,7},{7,0},{8,9},{9,10},{10,1... | collective-permute-start | bytes 98312 | tf_op jit(solution)/shard_map/ppermute | solution.py:25
  5.4 2.3 %collective-permute-start.1 = (f32[2,4,2,512]{3,2,1,0:T(2,128)S(1)}, f32[2,4,2,512]{3,2,1,0:T(2,128)S(1)}, u32[]{:S(2)}, u32[]{:S(2)}) collective-permute-start(f32[2,4,2,512]{3,2,1,0:T(2,128)S(1)} %get-tuple-element.343), channel_id=1, source_target_pairs={{1,0},{2,1},{3,2},{4,3},{5,4},{6,5},{7,6},{0,7},{9,8},{10,9},{11,1... | collective-permute-start | bytes 98312 | tf_op jit(solution)/shard_map/ppermute | solution.py:26
  9.2 1.1 slice_reduce_fusion
  10.3 0.9 and_reduce_fusion
  12.1 7.5 %while.52 = (s32[]{:T(128)}, f32[2,2048]{1,0:T(2,128)S(1)}, s32[2,2048]{1,0:T(2,128)S(1)}, s32[2,2048]{1,0:T(2,128)S(1)}, f32[128,512]{1,0:T(8,128)}, /*index=5*/s32[]{:T(128)}, s32[]{:T(128)}) while((s32[]{:T(128)}, f32[2,2048]{1,0:T(2,128)S(1)}, s32[2,2048]{1,0:T(2,128)S(1)}, s32[2,2048]{1,0:T(2,128)S(1)}, f32[128,512]{1,0:T(8,128)}, ...), condition=%wide.region_2.3_spmd.clone, body=%wide.region_0.2_spmd.clone.sunk | while | flops 1614018560 | bytes 335957 | solution.py:113
  12.1 3.6 %select_reduce_fusion.4 = f32[2048]{0:T(1024)S(1)} fusion(f32[128,512]{1,0:T(8,128)} %get-tuple-element.507, s32[2048]{0:T(1024)S(1)} %bitcast.161, s32[2048]{0:T(1024)S(1)} %bitcast.160), kind=kOutput, calls=%fused_computation.9.clone.1 | convolution fusion | flops 1614018560 | bytes 286720 | tf_op jit(solution)/shard_map/while/body/eval_jaxpr/dot_general | solution.py:108
  15.9 3.6 %select_reduce_fusion.4 = f32[2048]{0:T(1024)S(1)} fusion(f32[128,512]{1,0:T(8,128)} %get-tuple-element.507, s32[2048]{0:T(1024)S(1)} %bitcast.161, s32[2048]{0:T(1024)S(1)} %bitcast.160), kind=kOutput, calls=%fused_computation.9.clone.1 | convolution fusion | flops 1614018560 | bytes 286720 | tf_op jit(solution)/shard_map/while/body/eval_jaxpr/dot_general | solution.py:108
  20.0 1.0 pad_maximum_fusion.4
  21.1 4.9 %collective-permute-start.2 = (f32[2,2,36,512]{3,2,1,0:T(8,128)S(1)}, f32[2,2,36,512]{3,2,1,0:T(8,128)S(1)}, u32[]{:S(2)}, u32[]{:S(2)}) collective-permute-start(f32[2,2,36,512]{3,2,1,0:T(8,128)S(1)} %get-tuple-element.331), channel_id=1, source_target_pairs={{8,0},{16,8},{24,16},{32,24},{40,32},{48,40},{56,48},{64,56},{72,6... | collective-permute-start | bytes 884744 | tf_op jit(solution)/shard_map/ppermute | solution.py:26
  26.0 1.9 collective-permute-start.3
  28.2 2.3 %collective-permute-done.2 = f32[2,2,36,512]{3,2,1,0:T(8,128)S(1)} collective-permute-done((f32[2,2,36,512]{3,2,1,0:T(8,128)S(1)}, f32[2,2,36,512]{3,2,1,0:T(8,128)S(1)}, u32[]{:S(2)}, u32[]{:S(2)}) %collective-permute-start.2) | collective-permute-done | bytes 294944 | tf_op jit(solution)/shard_map/ppermute | solution.py:26
  30.6 1.4 collective-permute-done.3
  33.5 5.6 %while.53 = (s32[]{:T(128)}, f32[2,2048]{1,0:T(2,128)S(1)}, s32[2,2048]{1,0:T(2,128)S(1)}, s32[2,2048]{1,0:T(2,128)S(1)}, f32[128,512]{1,0:T(8,128)S(1)}, /*index=5*/s32[]{:T(128)}, s32[]{:T(128)}) while((s32[]{:T(128)}, f32[2,2048]{1,0:T(2,128)S(1)}, s32[2,2048]{1,0:T(2,128)S(1)}, s32[2,2048]{1,0:T(2,128)S(1)}, ...), condition=%wide.region_8.9_spmd.clone, body=%wide.region_6.8_spmd.clone.sunk | while | flops 1614018560 | bytes 335957 | solution.py:113
  33.5 2.6 %select_reduce_fusion.5 = f32[2048]{0:T(1024)S(1)} fusion(f32[128,512]{1,0:T(8,128)S(1)} %get-tuple-element.528, s32[2048]{0:T(1024)S(1)} %bitcast.163, s32[2048]{0:T(1024)S(1)} %bitcast.162), kind=kOutput, calls=%fused_computation.15.clone.1 | convolution fusion | flops 1614018560 | bytes 286720 | tf_op jit(solution)/shard_map/while/body/eval_jaxpr/dot_general | solution.py:108
  36.3 2.6 %select_reduce_fusion.5 = f32[2048]{0:T(1024)S(1)} fusion(f32[128,512]{1,0:T(8,128)S(1)} %get-tuple-element.528, s32[2048]{0:T(1024)S(1)} %bitcast.163, s32[2048]{0:T(1024)S(1)} %bitcast.162), kind=kOutput, calls=%fused_computation.15.clone.1 | convolution fusion | flops 1614018560 | bytes 286720 | tf_op jit(solution)/shard_map/while/body/eval_jaxpr/dot_general | solution.py:108
  39.1 79.9 %all-reduce.7 = (f32[4096]{0:T(1024)S(1)}, f32[4096]{0:T(1024)S(1)}) all-reduce(f32[4096]{0:T(1024)S(1)} %bitcast.164, f32[4096]{0:T(1024)S(1)} %bitcast.167), channel_id=2, replica_groups=mesh['gz'=32,'gy'=8] {'gz','gy'}, use_global_device_ids=true, to_apply=%region_3.4.clone | all-reduce | flops 8192 | bytes 65536
  119.3 73.8 %all-reduce.6 = (f32[4096]{0:T(1024)S(1)}, f32[4096]{0:T(1024)S(1)}) all-reduce(f32[4096]{0:T(1024)S(1)} %fusion.92, f32[4096]{0:T(1024)S(1)} %fusion.91), channel_id=1, replica_groups=mesh['gz'=32,'gy'=8] {'gz','gy'}, use_global_device_ids=true, to_apply=%add.2 | all-reduce | flops 8192 | bytes 65536
  193.2 4.7 %while.54 = (s32[]{:T(128)}, f32[128,512]{1,0:T(8,128)S(1)}, s32[2,2048]{1,0:T(2,128)S(1)}, s32[2,2048]{1,0:T(2,128)S(1)}, f32[2,2048]{1,0:T(2,128)S(1)}, /*index=5*/s32[]{:T(128)}, s32[]{:T(128)}) while((s32[]{:T(128)}, f32[128,512]{1,0:T(8,128)S(1)}, s32[2,2048]{1,0:T(2,128)S(1)}, s32[2,2048]{1,0:T(2,128)S(1)}, ...), condition=%wide.region_5.6_spmd.clone, body=%wide.region_4.5_spmd.clone.sunk | while | flops 1613103104 | bytes 598111 | solution.py:141
  193.2 2.3 %fusion.110 = f32[128,512]{1,0:T(8,128)S(1)} fusion(f32[2048]{0:T(1024)S(1)} %bitcast.152, s32[2048]{0:T(1024)S(1)} %bitcast.156, s32[2048]{0:T(1024)S(1)} %bitcast.157, f32[128,512]{1,0:T(8,128)S(1)} %get-tuple-element.539, pred[]{:T(512)S(6)} %compare.10), kind=kOutput, calls=%fused_computation.26.clone.1 | convolution fusion | flops 1613103104 | bytes 548865 | tf_op jit(solution)/shard_map/while/body/eval_jaxpr/dot_general | solution.py:131
  195.6 2.3 %fusion.110 = f32[128,512]{1,0:T(8,128)S(1)} fusion(f32[2048]{0:T(1024)S(1)} %bitcast.152, s32[2048]{0:T(1024)S(1)} %bitcast.156, s32[2048]{0:T(1024)S(1)} %bitcast.157, f32[128,512]{1,0:T(8,128)S(1)} %get-tuple-element.539, pred[]{:T(512)S(6)} %compare.10), kind=kOutput, calls=%fused_computation.26.clone.1 | convolution fusion | flops 1613103104 | bytes 548865 | tf_op jit(solution)/shard_map/while/body/eval_jaxpr/dot_general | solution.py:131
  198.2 1.4 collective-permute-start.4
  199.6 3.9 %collective-permute-start.5 = (f32[2,4,2,512]{3,2,1,0:T(2,128)S(1)}, f32[2,4,2,512]{3,2,1,0:T(2,128)S(1)}, u32[]{:S(2)}, u32[]{:S(2)}) collective-permute-start(f32[2,4,2,512]{3,2,1,0:T(2,128)S(1)} %get-tuple-element.339), channel_id=1, source_target_pairs={{1,0},{2,1},{3,2},{4,3},{5,4},{6,5},{7,6},{0,7},{9,8},{10,9},{11,1... | collective-permute-start | bytes 98312 | tf_op jit(solution)/shard_map/ppermute | solution.py:26
  203.9 0.9 collective-permute-done.4
  204.9 0.8 fusion.97
  205.7 3.7 %collective-permute-start.6 = (f32[2,2,36,512]{3,2,1,0:T(8,128)}, f32[2,2,36,512]{3,2,1,0:T(8,128)S(1)}, u32[]{:S(2)}, u32[]{:S(2)}) collective-permute-start(f32[2,2,36,512]{3,2,1,0:T(8,128)} %get-tuple-element.329), channel_id=1, source_target_pairs={{8,0},{16,8},{24,16},{32,24},{40,32},{48,40},{56,48},{64,56},{72,6... | collective-permute-start | bytes 884744 | tf_op jit(solution)/shard_map/ppermute | solution.py:26
  209.4 2.8 %collective-permute-start.7 = (f32[2,2,36,512]{3,2,1,0:T(8,128)S(1)}, f32[2,2,36,512]{3,2,1,0:T(8,128)S(1)}, u32[]{:S(2)}, u32[]{:S(2)}) collective-permute-start(f32[2,2,36,512]{3,2,1,0:T(8,128)S(1)} %get-tuple-element.330), channel_id=1, source_target_pairs={{0,8},{8,16},{16,24},{24,32},{32,40},{40,48},{48,56},{56,64},{64,7... | collective-permute-start | bytes 884744 | tf_op jit(solution)/shard_map/ppermute | solution.py:25
  212.2 7.0 %while.55 = (s32[]{:T(128)}, f32[128,512]{1,0:T(8,128)}, s32[2,2048]{1,0:T(2,128)S(1)}, s32[2,2048]{1,0:T(2,128)S(1)}, f32[2,2048]{1,0:T(2,128)S(1)}, /*index=5*/s32[]{:T(128)}, s32[]{:T(128)}) while((s32[]{:T(128)}, f32[128,512]{1,0:T(8,128)}, s32[2,2048]{1,0:T(2,128)S(1)}, s32[2,2048]{1,0:T(2,128)S(1)}, ...), condition=%wide.region_11.12_spmd.clone, body=%wide.region_10.11_spmd.clone.sunk | while | flops 1613103104 | bytes 598111 | solution.py:141
  212.3 3.0 %fusion.112 = f32[128,512]{1,0:T(8,128)} fusion(f32[2048]{0:T(1024)S(1)} %bitcast.153, s32[2048]{0:T(1024)S(1)} %bitcast.158, s32[2048]{0:T(1024)S(1)} %bitcast.159, f32[128,512]{1,0:T(8,128)} %get-tuple-element.560, pred[]{:T(512)S(6)} %compare.11), kind=kOutput, calls=%fused_computation.39.clone.1 | convolution fusion | flops 1613103104 | bytes 548865 | tf_op jit(solution)/shard_map/while/body/eval_jaxpr/dot_general | solution.py:131
  215.3 3.9 %fusion.112 = f32[128,512]{1,0:T(8,128)} fusion(f32[2048]{0:T(1024)S(1)} %bitcast.153, s32[2048]{0:T(1024)S(1)} %bitcast.158, s32[2048]{0:T(1024)S(1)} %bitcast.159, f32[128,512]{1,0:T(8,128)} %get-tuple-element.560, pred[]{:T(512)S(6)} %compare.11), kind=kOutput, calls=%fused_computation.39.clone.1 | convolution fusion | flops 1613103104 | bytes 548865 | tf_op jit(solution)/shard_map/while/body/eval_jaxpr/dot_general | solution.py:131
  220.7 1.2 multiply_add_fusion
  221.8 0.8 broadcast_select_fusion
  (76 shorter events, 7.5 us)
Async XLA Ops:
  1.6 18.4 %collective-permute-start = (f32[2,4,2,512]{3,2,1,0:T(2,128)S(1)}, f32[2,4,2,512]{3,2,1,0:T(2,128)S(1)}, u32[]{:S(2)}, u32[]{:S(2)}) collective-permute-start(f32[2,4,2,512]{3,2,1,0:T(2,128)S(1)} %get-tuple-element.344), channel_id=1, source_target_pairs={{0,1},{1,2},{2,3},{3,4},{4,5},{5,6},{6,7},{7,0},{8,9},{9,10},{10,1... | collective-permute-start | bytes 98312 | tf_op jit(solution)/shard_map/ppermute | solution.py:25
  5.4 14.6 %collective-permute-start.1 = (f32[2,4,2,512]{3,2,1,0:T(2,128)S(1)}, f32[2,4,2,512]{3,2,1,0:T(2,128)S(1)}, u32[]{:S(2)}, u32[]{:S(2)}) collective-permute-start(f32[2,4,2,512]{3,2,1,0:T(2,128)S(1)} %get-tuple-element.343), channel_id=1, source_target_pairs={{1,0},{2,1},{3,2},{4,3},{5,4},{6,5},{7,6},{0,7},{9,8},{10,9},{11,1... | collective-permute-start | bytes 98312 | tf_op jit(solution)/shard_map/ppermute | solution.py:26
  12.1 7.9 %copy-start = (f32[4,32,512]{2,1,0:T(8,128)S(1)}, f32[4,32,512]{2,1,0:T(8,128)}, u32[]{:S(2)}) copy-start(f32[4,32,512]{2,1,0:T(8,128)} %param.19) | copy-start | bytes 786436
  21.1 7.0 %copy-start.2 = (f32[128,512]{1,0:T(8,128)S(1)}, f32[128,512]{1,0:T(8,128)}, u32[]{:S(2)}) copy-start(f32[128,512]{1,0:T(8,128)} %get-tuple-element.573) | copy-start | bytes 786436
  21.1 9.4 %collective-permute-start.2 = (f32[2,2,36,512]{3,2,1,0:T(8,128)S(1)}, f32[2,2,36,512]{3,2,1,0:T(8,128)S(1)}, u32[]{:S(2)}, u32[]{:S(2)}) collective-permute-start(f32[2,2,36,512]{3,2,1,0:T(8,128)S(1)} %get-tuple-element.331), channel_id=1, source_target_pairs={{8,0},{16,8},{24,16},{32,24},{40,32},{48,40},{56,48},{64,56},{72,6... | collective-permute-start | bytes 884744 | tf_op jit(solution)/shard_map/ppermute | solution.py:26
  26.0 5.9 %collective-permute-start.3 = (f32[2,2,36,512]{3,2,1,0:T(8,128)S(1)}, f32[2,2,36,512]{3,2,1,0:T(8,128)S(1)}, u32[]{:S(2)}, u32[]{:S(2)}) collective-permute-start(f32[2,2,36,512]{3,2,1,0:T(8,128)S(1)} %get-tuple-element.332), channel_id=1, source_target_pairs={{0,8},{8,16},{16,24},{24,32},{32,40},{40,48},{48,56},{56,64},{64,7... | collective-permute-start | bytes 884744 | tf_op jit(solution)/shard_map/ppermute | solution.py:25
  32.3 1.0 copy-start.4
  32.3 1.0 copy-start.5
  33.5 85.5 %copy-start.8 = (f32[2,16]{1,0:T(2,128)S(1)}, f32[2,16]{1,0:T(2,128)}, u32[]{:S(2)}) copy-start(f32[2,16]{1,0:T(2,128)} %param.22) | copy-start | bytes 388
  39.1 181.4 %copy-start.3 = (f32[128,512]{1,0:T(8,128)}, f32[128,512]{1,0:T(8,128)S(1)}, u32[]{:S(2)}) copy-start(f32[128,512]{1,0:T(8,128)S(1)} %get-tuple-element.574) | copy-start | bytes 786436
  193.2 4.8 %copy-start.6 = (f32[4,32,512]{2,1,0:T(8,128)S(1)}, f32[4,32,512]{2,1,0:T(8,128)}, u32[]{:S(2)}) copy-start(f32[4,32,512]{2,1,0:T(8,128)} %param.20) | copy-start | bytes 786436
  198.1 22.4 %copy-start.1 = (f32[4,32,512]{2,1,0:T(8,128)}, f32[4,32,512]{2,1,0:T(8,128)S(1)}, u32[]{:S(2)}) copy-start(f32[4,32,512]{2,1,0:T(8,128)S(1)} %fusion.67) | copy-start | bytes 786436
  198.2 6.6 %collective-permute-start.4 = (f32[2,4,2,512]{3,2,1,0:T(2,128)S(1)}, f32[2,4,2,512]{3,2,1,0:T(2,128)S(1)}, u32[]{:S(2)}, u32[]{:S(2)}) collective-permute-start(f32[2,4,2,512]{3,2,1,0:T(2,128)S(1)} %get-tuple-element.340), channel_id=1, source_target_pairs={{0,1},{1,2},{2,3},{3,4},{4,5},{5,6},{6,7},{7,0},{8,9},{9,10},{10,1... | collective-permute-start | bytes 98312 | tf_op jit(solution)/shard_map/ppermute | solution.py:25
  199.6 5.2 %collective-permute-start.5 = (f32[2,4,2,512]{3,2,1,0:T(2,128)S(1)}, f32[2,4,2,512]{3,2,1,0:T(2,128)S(1)}, u32[]{:S(2)}, u32[]{:S(2)}) collective-permute-start(f32[2,4,2,512]{3,2,1,0:T(2,128)S(1)} %get-tuple-element.339), channel_id=1, source_target_pairs={{1,0},{2,1},{3,2},{4,3},{5,4},{6,5},{7,6},{0,7},{9,8},{10,9},{11,1... | collective-permute-start | bytes 98312 | tf_op jit(solution)/shard_map/ppermute | solution.py:26
  205.7 13.7 %collective-permute-start.6 = (f32[2,2,36,512]{3,2,1,0:T(8,128)}, f32[2,2,36,512]{3,2,1,0:T(8,128)S(1)}, u32[]{:S(2)}, u32[]{:S(2)}) collective-permute-start(f32[2,2,36,512]{3,2,1,0:T(8,128)} %get-tuple-element.329), channel_id=1, source_target_pairs={{8,0},{16,8},{24,16},{32,24},{40,32},{48,40},{56,48},{64,56},{72,6... | collective-permute-start | bytes 884744 | tf_op jit(solution)/shard_map/ppermute | solution.py:26
  209.4 10.0 %collective-permute-start.7 = (f32[2,2,36,512]{3,2,1,0:T(8,128)S(1)}, f32[2,2,36,512]{3,2,1,0:T(8,128)S(1)}, u32[]{:S(2)}, u32[]{:S(2)}) collective-permute-start(f32[2,2,36,512]{3,2,1,0:T(8,128)S(1)} %get-tuple-element.330), channel_id=1, source_target_pairs={{0,8},{8,16},{16,24},{24,32},{32,40},{40,48},{48,56},{56,64},{64,7... | collective-permute-start | bytes 884744 | tf_op jit(solution)/shard_map/ppermute | solution.py:25
  219.7 1.0 copy-start.7
where the time goes:
time: 223 us
  blocking collectives  154 us (69%)
  starting transfers between devices  24.8 us (11%)
  matrix products  24.7 us (11%)
  other arithmetic  10 us (4%)
  waiting for transfers between devices  4.62 us (2%)
  local copies, waits for them, and re-layouts  3.42 us (2%)
    unnamed x2, blocking collectives  154 us
    ppermute x4, starting transfers between devices, padded_2(): after = lax.ppermute(initial, axis, down)  14.8 us
    dot_general x4, matrix products, one_block(): jnp.dot(pick_rows, flat, precision=lax.Precision.HIGHEST, preferred_eleme...  12.5 us
    dot_general x6, matrix products, add_block(): lax.dot_general(pick_rows, spread, (((0,), (0,)), ((), ())), precision=la...  12.2 us
    ppermute x4, starting transfers between devices, padded_2(): before = lax.ppermute(last, axis, up)  9.96 us
  transfers between devices with their start and end apart: 8, of which 3 were waited for; matrix products, arithmetic and copies ran while one was open for 9% of the time, Pallas kernels for 0%

commit v1 on v0

v1 whole, which is shorter than its diff:
```python
import jax
import jax.numpy as jnp
import numpy as np
from jax import lax
from jax.experimental import pallas as pl
from jax.experimental.pallas import tpu as pltpu
from jax.sharding import Mesh
from jax.sharding import PartitionSpec as P

CENTRE = -7.5
NEAR = 4.0 / 3.0
FAR = -1.0 / 12.0
RATIO = 0.1
DAMP = 0.3

GZ = ("yl", "z", "c")
GY = ("x", "yh")
O = 16
NZ_DEV, NY_DEV = 32, 8
CZ, CY, NX = 4, 32, 512
NZ, NY = NZ_DEV * CZ, NY_DEV * CY
FR = CY + 2 * O
VMEM_LIMIT = 48 * 1024 * 1024
ZROWS = 5 * CY + 8


def coefficient_table():
    z = np.clip(np.arange(-2, NZ + 2), 0, NZ - 1).astype(np.float32)
    low = np.maximum(np.float32(CZ) - z, np.float32(0)) / np.float32(CZ)
    high = np.maximum(z - np.float32(NZ - 1 - CZ), np.float32(0)) / np.float32(CZ)
    a = np.float32(DAMP) * (low * low + high * high)
    one = np.float32(1)
    return np.stack([one + a, one - a, one / (one - a), one / (one + a)]).astype(np.float32)


def smem():
    return pl.BlockSpec(memory_space=pltpu.SMEM)


def vmem():
    return pl.BlockSpec(memory_space=pltpu.VMEM)


def x_terms(u):
    lane = lax.broadcasted_iota(jnp.int32, u.shape, 1)
    a = jnp.where(lane >= 1, pltpu.roll(u, 1, 1), 0.0)
    b = jnp.where(lane < NX - 1, pltpu.roll(u, NX - 1, 1), 0.0)
    c = jnp.where(lane >= 2, pltpu.roll(u, 2, 1), 0.0)
    d = jnp.where(lane < NX - 2, pltpu.roll(u, NX - 2, 1), 0.0)
    return a + b, c + d


def laplace(f, k, s):
    rows = lambda layer, shift: f[layer, s + shift : s + shift + 8, :]
    u = rows(k, 0)
    near, far = x_terms(u)
    near = near + ((rows(k, -1) + rows(k, 1)) + (rows(k - 1, 0) + rows(k + 1, 0)))
    far = far + ((rows(k, -2) + rows(k, 2)) + (rows(k - 2, 0) + rows(k + 2, 0)))
    return u, CENTRE * u + NEAR * near + FAR * far


def pack_y(meta, u, a, u1, a1, v, h, g):
    def pack(dst, high):
        four = slice(CY - 4, CY) if high else slice(0, 4)
        two = slice(CY - 2, CY) if high else slice(0, 2)
        dst[:, 0:4, :] = u[:, four, :]
        dst[:, 4:8, :] = a[:, four, :]
        dst[:, 8:10, :] = u1[:, two, :]
        dst[:, 10:12, :] = a1[:, two, :]
        dst[:, 12:14, :] = v[:, two, :]
        dst[:, 14:16, :] = v[:, two, :]

    @pl.when(meta[2] == 0)
    def _():
        pack(h, True)
        pack(g, False)

    @pl.when(meta[2] != 0)
    def _():
        pack(h, False)
        pack(g, True)


def fill_y(meta, rh, rg, low, high):
    @pl.when(meta[2] == 0)
    def _():
        high(rh)
        low(rg)

    @pl.when(meta[2] != 0)
    def _():
        low(rh)
        high(rg)


def local_step(meta, coef, u, a, u1, a1, v, rh, rg, u0p, a0p, zc, zb, uf, af, u1f, a1f, vf):
    for f, own in ((uf, u), (af, a)):
        f[2:6, O : O + CY, :] = own[...]
        for k in (0, 1, 6, 7):
            f[k, :, :] = jnp.zeros((FR, NX), jnp.float32)
    for f, own in ((u1f, u1), (a1f, a1), (vf, v)):
        f[:, O : O + CY, :] = own[...]

    def low(r):
        uf[2:6, O - 4 : O, :] = r[:, 0:4, :]
        af[2:6, O - 4 : O, :] = r[:, 4:8, :]
        u1f[:, O - 2 : O, :] = r[:, 8:10, :]
        a1f[:, O - 2 : O, :] = r[:, 10:12, :]
        vf[:, O - 2 : O, :] = r[:, 12:14, :]

    def high(r):
        e = O + CY
        uf[2:6, e : e + 4, :] = r[:, 0:4, :]
        af[2:6, e : e + 4, :] = r[:, 4:8, :]
        u1f[:, e : e + 2, :] = r[:, 8:10, :]
        a1f[:, e : e + 2, :] = r[:, 10:12, :]
        vf[:, e : e + 2, :] = r[:, 12:14, :]

    fill_y(meta, rh, rg, low, high)
    z0 = meta[0]

    def layer(l, carry):
        i = z0 + l + 2
        up, dn, iu, ia = coef[0, i], coef[1, i], coef[2, i], coef[3, i]
        for s in range(O - 8, O + CY + 8, 8):
            c = vf[l, s : s + 8, :] * RATIO
            c = c * c
            u, lu = laplace(uf, l + 2, s)
            u0p[l, s : s + 8, :] = (2.0 * u - up * u1f[l, s : s + 8, :] + c * lu) * iu
            w, lw = laplace(af, l + 2, s)
            a0p[l, s : s + 8, :] = (2.0 * w - dn * a1f[l, s : s + 8, :] + c * lw) * ia
        return carry

    lax.fori_loop(0, CZ, layer, 0)

    def pack(dst, l):
        e = O + CY
        own = (uf, l + 2, u0p, l), (af, l + 2, a0p, l)
        dst[:, 0:CY, :] = uf[l + 2 : l + 4, O:e, :]
        dst[:, CY : 2 * CY, :] = af[l + 2 : l + 4, O:e, :]
        dst[:, 2 * CY : 3 * CY, :] = u0p[l : l + 2, O:e, :]
        dst[:, 3 * CY : 4 * CY, :] = a0p[l : l + 2, O:e, :]
        dst[:, 4 * CY : 5 * CY, :] = vf[l : l + 2, O:e, :]
        b = 5 * CY
        dst[:, b : b + 2, :] = uf[l + 2 : l + 4, O - 2 : O, :]
        dst[:, b + 2 : b + 4, :] = uf[l + 2 : l + 4, e : e + 2, :]
        dst[:, b + 4 : b + 6, :] = af[l + 2 : l + 4, O - 2 : O, :]
        dst[:, b + 6 : b + 8, :] = af[l + 2 : l + 4, e : e + 2, :]

    @pl.when(meta[3] == 0)
    def _():
        pack(zc, 2)
        pack(zb, 0)

    @pl.when(meta[3] != 0)
    def _():
        pack(zc, 0)
        pack(zb, 2)


def list_receivers(meta, rec, out, bits, words_v, words, sem):
    z0, y0 = meta[0], meta[1]
    lz = rec[0:1, :] - z0
    ly = ((rec[1:2, :] - y0 + O) & (NY - 1)) - O
    own_z = (lz >= 0) & (lz < CZ)
    own_y = (ly >= 0) & (ly < CY)
    near = (lz >= -2) & (lz < CZ + 2) & (ly >= -2) & (ly < CY + 2) & (own_z | own_y)
    m = near.astype(jnp.int32)
    for i in range(32):
        bits[i : i + 1, :] = m[:, 128 * i : 128 * i + 128] << i
    words_v[...] = jnp.sum(bits[...], axis=0, keepdims=True)
    copy = pltpu.make_async_copy(words_v, words, sem)
    copy.start()
    copy.wait()

    def word_step(w, count):
        def bit_step(carry):
            word, count = carry
            low = word & (-word)
            out[0, count + 1] = (31 - lax.clz(low)) * 128 + w
            return word ^ low, count + 1

        return lax.while_loop(lambda carry: carry[0] != 0, bit_step, (words[0, w], count))[1]

    out[0, 0] = lax.fori_loop(0, 128, word_step, 0)


def last_step(
    meta, coef, u, a, u1, a1, v, rh, rg, u0p, a0p, rc, rb, found, rec, table, src, amp,
    u2, u0o, a2, a0o, grad,
    uf, af, vf, u0f, a0f,
):
    e = O + CY
    z0, y0 = meta[0], meta[1]
    uf[2:6, O:e, :] = u[...]
    vf[2:6, O:e, :] = v[...]

    def low(r):
        uf[2:6, O - 2 : O, :] = r[:, 2:4, :]
        vf[2:6, O - 2 : O, :] = r[:, 12:14, :]

    def high(r):
        uf[2:6, e : e + 2, :] = r[:, 0:2, :]
        vf[2:6, e : e + 2, :] = r[:, 12:14, :]

    fill_y(meta, rh, rg, low, high)

    def fill_z(r, k):
        b = 5 * CY
        uf[k : k + 2, O:e, :] = r[:, 0:CY, :]
        af[k : k + 2, O:e, :] = r[:, CY : 2 * CY, :]
        u0f[k : k + 2, O:e, :] = r[:, 2 * CY : 3 * CY, :]
        a0f[k : k + 2, O:e, :] = r[:, 3 * CY : 4 * CY, :]
        vf[k : k + 2, O:e, :] = r[:, 4 * CY : 5 * CY, :]
        uf[k : k + 2, O - 2 : O, :] = r[:, b : b + 2, :]
        uf[k : k + 2, e : e + 2, :] = r[:, b + 2 : b + 4, :]
        af[k : k + 2, O - 2 : O, :] = r[:, b + 4 : b + 6, :]
        af[k : k + 2, e : e + 2, :] = r[:, b + 6 : b + 8, :]

    @pl.when(meta[3] == 0)
    def _():
        fill_z(rb, 0)
        fill_z(rc, 6)

    @pl.when(meta[3] != 0)
    def _():
        fill_z(rc, 0)
        fill_z(rb, 6)

    lacks = ((0, None, 2), (1, 2, 3), (2, 1, 0), (3, None, 1), (4, None, 6), (5, 6, 7), (6, 5, 4), (7, None, 5))
    for k, near, far in lacks:
        own = 2 <= k < 6
        iu, ia = coef[2, z0 + k], coef[3, z0 + k]

        def term(f, layer, s):
            if 2 <= layer < 6 and f is af:
                return a[layer - 2, pl.ds(s - O, 8), :]
            return f[layer, pl.ds(s, 8), :]

        def rows(t, carry):
            s = pl.multiple_of(t * 8, 8)
            c = vf[k, pl.ds(s, 8), :] * RATIO
            c = c * c
            for f, f0, p, scale in ((uf, u0f, u0p, iu), (af, a0f, a0p, ia)):
                lap = FAR * term(f, far, s)
                if near is not None:
                    lap = lap + NEAR * term(f, near, s)
                base = p[k - 2, pl.ds(s, 8), :] if own else f0[k, pl.ds(s, 8), :]
                f0[k, pl.ds(s, 8), :] = base + (c * scale) * lap
            return carry

        first = O // 8
        lax.fori_loop(first - own, first + CY // 8 + own, rows, 0)

    place = lax.broadcasted_iota(jnp.int32, (8, 128), 0) * 128 + lax.broadcasted_iota(jnp.int32, (8, 128), 1)

    def cell(z, y, x):
        lz = z - z0
        ly = ((y - y0 + O) & (NY - 1)) - O
        rows = (ly >> 3) << 3
        cols = pl.ds(pl.multiple_of((x >> 7) << 7, 128), 128)
        return lz, ly, rows, cols, place == ((ly & 7) * 128 + (x & 127))

    def add_source_0(i, carry):
        lz, ly, rows, cols, hit = cell(src[0, i], src[1, i], src[2, i])
        own_z = (lz >= 0) & (lz < CZ)
        own_y = (ly >= 0) & (ly < CY)
        near = (lz >= -2) & (lz < CZ + 2) & (ly >= -2) & (ly < CY + 2) & (own_z | own_y)

        @pl.when(near)
        def _():
            at = (lz + 2, pl.ds(pl.multiple_of(rows + O, 8), 8), cols)
            c = vf[at] * RATIO
            u0f[at] = u0f[at] + jnp.where(hit, (c * c) * (amp[0, i] * coef[2, z0 + lz + 2]), 0.0)

        return carry

    lax.fori_loop(0, src.shape[1], add_source_0, 0)

    def observed(step, r):
        return table[(r >> 7) * 2 + ((r >> 4) & 1), ((r >> 5) & 3) * 32 + step * 16 + (r & 15)]

    def add_receiver_0(n, carry):
        r = found[0, n + 1]
        lz, ly, rows, cols, hit = cell(rec[0, r], rec[1, r], rec[2, r])
        at = (lz + 2, pl.ds(pl.multiple_of(rows + O, 8), 8), cols)
        residual = (uf[at] - observed(0, r)) * coef[3, z0 + lz + 2]
        a0f[at] = a0f[at] + jnp.where(hit, residual, 0.0)
        return carry

    count = found[0, 0]
    lax.fori_loop(0, count, add_receiver_0, 0)

    def layer(l, carry):
        i = z0 + l + 2
        up, dn, iu, ia = coef[0, i], coef[1, i], coef[2, i], coef[3, i]
        for s in range(O, O + CY, 8):
            y = slice(s - O, s - O + 8)
            vel = v[l, y, :]
            c = vel * RATIO
            c = c * c
            un, an = u[l, y, :], a[l, y, :]
            q, lu = laplace(u0f, l + 2, s)
            new = (2.0 * q - up * un + c * lu) * iu
            u2[l, y, :] = new
            u0o[l, y, :] = q
            w, lw = laplace(a0f, l + 2, s)
            a2[l, y, :] = (2.0 * w - dn * an + c * lw) * ia
            a0o[l, y, :] = w
            grad[l, y, :] = (2.0 / vel) * (an * (u1[l, y, :] - 2.0 * un + q) + w * (un - 2.0 * q + new))
        return carry

    lax.fori_loop(0, CZ, layer, 0)

    def add_source_1(i, carry):
        lz, ly, rows, cols, hit = cell(src[0, i], src[1, i], src[2, i])

        @pl.when((lz >= 0) & (lz < CZ) & (ly >= 0) & (ly < CY))
        def _():
            at = (lz, pl.ds(pl.multiple_of(rows, 8), 8), cols)
            vel = v[at]
            c = vel * RATIO
            added = jnp.where(hit, (c * c) * (amp[1, i] * coef[2, z0 + lz + 2]), 0.0)
            u2[at] = u2[at] + added
            grad[at] = grad[at] + (2.0 / vel) * a0o[at] * added

        return carry

    lax.fori_loop(0, src.shape[1], add_source_1, 0)

    def add_receiver_1(n, carry):
        r = found[0, n + 1]
        lz, ly, rows, cols, hit = cell(rec[0, r], rec[1, r], rec[2, r])

        @pl.when((lz >= 0) & (lz < CZ) & (ly >= 0) & (ly < CY))
        def _():
            at = (lz, pl.ds(pl.multiple_of(rows, 8), 8), cols)
            residual = (u0o[at] - observed(1, r)) * coef[3, z0 + lz + 2]
            a2[at] = a2[at] + jnp.where(hit, residual, 0.0)

        return carry

    lax.fori_loop(0, count, add_receiver_1, 0)


def f32(*shape):
    return jax.ShapeDtypeStruct(shape, jnp.float32)


def params():
    return pltpu.CompilerParams(vmem_limit_bytes=VMEM_LIMIT)


def swap(value, axis, size, first):
    pairs = [(i, (first + ((i - first) % size ^ 1)) % size) for i in range(size)]
    return lax.ppermute(value, axis, pairs)


def swap_open(value, axis, size):
    pairs = [(i, i + 1) for i in range(1, size - 1, 2)]
    return lax.ppermute(value, axis, pairs + [(j, i) for i, j in pairs])


def shards(u, u1, a, a1, v, obs, rec, src, amp):
    assert u.shape == (CZ, CY, NX)
    gz, gy = lax.axis_index(GZ), lax.axis_index(GY)
    x, yh, core = lax.axis_index("x"), lax.axis_index("yh"), lax.axis_index("c")
    meta = jnp.stack([gz * CZ, gy * CY, yh, core]).astype(jnp.int32)
    coef = jnp.asarray(coefficient_table())

    lanes = jnp.arange(128, dtype=jnp.int32) // 32
    mine = jnp.where(lanes == x, jnp.tile(obs.reshape(32), 4), 0.0)[None]
    mine = mine + swap(mine, "x", 4, 0)
    mine = mine + swap(mine, "x", 4, 1)

    pack = f32(CZ, 16, NX)
    h, g = pl.pallas_call(
        pack_y,
        out_shape=(pack, pack),
        in_specs=[smem()] + [vmem()] * 5,
        out_specs=(vmem(), vmem()),
        compiler_params=params(),
        name="pack_y",
    )(meta, u, a, u1, a1, v)
    rh = swap(h, GY, NY_DEV, 0)
    rg = swap(g, GY, NY_DEV, 1)

    frame, zpack = f32(CZ, FR, NX), f32(2, ZROWS, NX)
    full = pltpu.VMEM((8, FR, NX), jnp.float32)
    part = pltpu.VMEM((CZ, FR, NX), jnp.float32)
    u0p, a0p, zc, zb = pl.pallas_call(
        local_step,
        out_shape=(frame, frame, zpack, zpack),
        in_specs=[smem()] * 2 + [vmem()] * 7,
        out_specs=(vmem(),) * 4,
        scratch_shapes=[full, full, part, part, part],
        compiler_params=params(),
        name="local_step",
    )(meta, coef, u, a, u1, a1, v, rh, rg)

    rc = swap(zc, GZ, NZ_DEV, 0)
    rb = swap_open(zb, GZ, NZ_DEV)

    found = pl.pallas_call(
        list_receivers,
        out_shape=jax.ShapeDtypeStruct((1, rec.shape[1] + 128), jnp.int32),
        in_specs=[smem(), vmem()],
        out_specs=smem(),
        scratch_shapes=[
            pltpu.VMEM((32, 128), jnp.int32),
            pltpu.VMEM((1, 128), jnp.int32),
            pltpu.SMEM((1, 128), jnp.int32),
            pltpu.SemaphoreType.DMA,
        ],
        compiler_params=params(),
        name="list_receivers",
    )(meta, rec)

    table = lax.all_to_all(jnp.broadcast_to(mine, (64, 128)), ("yl", "z", "c", "yh"), 0, 0, tiled=True)

    block = f32(CZ, CY, NX)
    return pl.pallas_call(
        last_step,
        out_shape=(block,) * 5,
        in_specs=[smem()] * 2 + [vmem()] * 11 + [smem()] * 5,
        out_specs=(vmem(),) * 5,
        scratch_shapes=[full] * 5,
        compiler_params=params(),
        name="last_step",
    )(meta, coef, u, a, u1, a1, v, rh, rg, u0p, a0p, rc, rb, found, rec, table, src, amp)


def solution(mesh):
    fine = Mesh(mesh.devices.reshape(2, 8, 2, 4, 2), ("yl", "z", "c", "x", "yh"))
    field = P(GZ, GY, None)
    return jax.shard_map(
        shards,
        mesh=fine,
        in_specs=(field,) * 5 + (P(None, GZ + GY), P(), P(), P()),
        out_specs=(field,) * 5,
        check_vma=False,
    )
```

time: 223 us -> 64.8 us (0.29)
  blocking collectives: 154 us -> 0 us
  matrix products: 24.7 us -> 0 us
  Pallas kernels: 0 us -> 15.5 us
  other arithmetic: 10 us -> 0.1 us
  waiting for transfers between devices: 4.62 us -> 14.3 us
  local copies, waits for them, and re-layouts: 3.42 us -> 9.46 us
    unnamed x2 -> x0, blocking collectives: 154 us -> none
    dot_general x10 -> x0, matrix products: 24.7 us -> none  [the longest x4 12.5 us: one_block(): jnp.dot(pick_rows, flat, precision=lax.Precision.HIGHEST, preferred_eleme...]
    pallas_call x0 -> x4, Pallas kernels: none -> 15.5 us  [the longest x1 7.64 us: shards(): pl.pallas_call(last_step, out_shape=(block,) * 5, in_specs=[smem()] * 2 +...]
    ppermute x8 -> x6, starting transfers between devices: 24.8 us -> 13.2 us  [the longest x5 9.68 us: swap(): return lax.ppermute(value, axis, pairs)]
    all_to_all x0 -> x1, starting transfers between devices: none -> 11 us  [shards(): lax.all_to_all(jnp.broadcast_to(mine, (64, 128)), ('yl', 'z', 'c', 'yh'),...]
    unnamed x22 -> x38, local copies, waits for them, and re-layouts: 0.49 us -> 8.65 us
    ppermute x8 -> x6, waiting for transfers between devices: 4.62 us -> 9.68 us  [the longest x5 9.67 us: swap(): return lax.ppermute(value, axis, pairs)]
    all_to_all x0 -> x1, waiting for transfers between devices: none -> 4.63 us  [shards(): lax.all_to_all(jnp.broadcast_to(mine, (64, 128)), ('yl', 'z', 'c', 'yh'),...]
  transfers between devices with their start and end apart: 8 -> 7, of which waited for: 3 -> 5; matrix products, arithmetic and copies ran while one was open for 9% -> 1% of each run, Pallas kernels for 0% -> 6%
where the time goes in v1:
time: 64.8 us; the launch traced here: 64.3 us
  starting transfers between devices  24.2 us (37%)
  Pallas kernels  15.5 us (24%)
  waiting for transfers between devices  14.3 us (22%)
  local copies, waits for them, and re-layouts  9.46 us (15%)
  between operations  0.8 us (1%)
    all_to_all x1, starting transfers between devices, shards(): lax.all_to_all(jnp.broadcast_to(mine, (64, 128)), ('yl', 'z', 'c', 'yh'),...  11 us
    ppermute x5, starting transfers between devices, swap(): return lax.ppermute(value, axis, pairs)  9.68 us
    ppermute x5, waiting for transfers between devices, swap(): return lax.ppermute(value, axis, pairs)  9.67 us
    unnamed x38, local copies, waits for them, and re-layouts  8.65 us
    pallas_call x1, Pallas kernels, shards(): pl.pallas_call(last_step, out_shape=(block,) * 5, in_specs=[smem()] * 2 +...  7.64 us
    all_to_all x1, waiting for transfers between devices, shards(): lax.all_to_all(jnp.broadcast_to(mine, (64, 128)), ('yl', 'z', 'c', 'yh'),...  4.63 us
    pallas_call x1, Pallas kernels, shards(): pl.pallas_call(list_receivers, out_shape=jax.ShapeDtypeStruct((1, rec.sha...  3.91 us
    ppermute x1, starting transfers between devices, swap_open(): return lax.ppermute(value, axis, pairs + [(j, i) for i, j in pairs])  3.55 us
  transfers between devices with their start and end apart: 7, of which 5 were waited for; matrix products, arithmetic and copies ran while one was open for 1% of the time, Pallas kernels for 6%

profile of v1, /device:TPU:1, one launch (start us, length us, event | category | flops | bytes accessed | tf_op | source)
XLA Modules:
  0.0 64.3 jit_solution(2938128243636616316)
XLA Ops:
  0.6 0.1 pad_add_fusion.meta
  0.7 0.9 %copy-done = f32[4,32,512]{2,1,0:T(8,128)S(1)} copy-done((f32[4,32,512]{2,1,0:T(8,128)S(1)}, f32[4,32,512]{2,1,0:T(8,128)}, u32[]{:S(2)}) %copy-start) | copy-done | bytes 262168
  1.7 0.9 %copy-done.2 = f32[4,32,512]{2,1,0:T(8,128)S(1)} copy-done((f32[4,32,512]{2,1,0:T(8,128)S(1)}, f32[4,32,512]{2,1,0:T(8,128)}, u32[]{:S(2)}) %copy-start.2) | copy-done | bytes 262168
  2.6 0.9 %copy-done.4 = f32[4,32,512]{2,1,0:T(8,128)S(1)} copy-done((f32[4,32,512]{2,1,0:T(8,128)S(1)}, f32[4,32,512]{2,1,0:T(8,128)}, u32[]{:S(2)}) %copy-start.4) | copy-done | bytes 262168
  3.6 0.9 %copy-done.6 = f32[4,32,512]{2,1,0:T(8,128)S(1)} copy-done((f32[4,32,512]{2,1,0:T(8,128)S(1)}, f32[4,32,512]{2,1,0:T(8,128)}, u32[]{:S(2)}) %copy-start.6) | copy-done | bytes 262168
  4.5 0.9 %copy-done.8 = f32[4,32,512]{2,1,0:T(8,128)S(1)} copy-done((f32[4,32,512]{2,1,0:T(8,128)S(1)}, f32[4,32,512]{2,1,0:T(8,128)}, u32[]{:S(2)}) %copy-start.8) | copy-done | bytes 262168
  5.5 0.6 pack_y.1
  6.1 0.0 copy-start.15
  6.2 3.8 %collective-permute-start = (f32[4,16,512]{2,1,0:T(8,128)S(1)}, f32[4,16,512]{2,1,0:T(8,128)S(1)}, u32[]{:S(2)}, u32[]{:S(2)}) collective-permute-start(f32[4,16,512]{2,1,0:T(8,128)S(1)} %get-tuple-element.11), channel_id=1, source_target_pairs={{0,1},{1,0},{2,3},{3,2},{4,5},{5,4},{6,7},{7,6},{8,9},{9,8},{10,11... | collective-permute-start | bytes 393224 | tf_op jit(solution)/shard_map/ppermute | solution.py:356
  10.0 2.3 %collective-permute-start.1 = (f32[4,16,512]{2,1,0:T(8,128)S(1)}, f32[4,16,512]{2,1,0:T(8,128)S(1)}, u32[]{:S(2)}, u32[]{:S(2)}) collective-permute-start(f32[4,16,512]{2,1,0:T(8,128)S(1)} %get-tuple-element.12), channel_id=1, source_target_pairs={{0,7},{1,2},{2,1},{3,4},{4,3},{5,6},{6,5},{7,0},{8,15},{9,10},{10,... | collective-permute-start | bytes 393224 | tf_op jit(solution)/shard_map/ppermute | solution.py:356
  12.3 0.1 tile.10
  12.4 0.1 tile.12
  12.5 1.0 %collective-permute-done.rh = f32[4,16,512]{2,1,0:T(8,128)S(1)} collective-permute-done((f32[4,16,512]{2,1,0:T(8,128)S(1)}, f32[4,16,512]{2,1,0:T(8,128)S(1)}, u32[]{:S(2)}, u32[]{:S(2)}) %collective-permute-start) | collective-permute-done | bytes 131104 | tf_op jit(solution)/shard_map/ppermute | solution.py:356
  13.4 4.0 %collective-permute-done.1.rg = f32[4,16,512]{2,1,0:T(8,128)S(1)} collective-permute-done((f32[4,16,512]{2,1,0:T(8,128)S(1)}, f32[4,16,512]{2,1,0:T(8,128)S(1)}, u32[]{:S(2)}, u32[]{:S(2)}) %collective-permute-start.1) | collective-permute-done | bytes 131104 | tf_op jit(solution)/shard_map/ppermute | solution.py:356
  17.5 3.3 %local_step.1 = (f32[4,64,512]{2,1,0:T(8,128)S(1)}, f32[4,64,512]{2,1,0:T(8,128)S(1)}, f32[2,168,512]{2,1,0:T(8,128)}, f32[2,168,512]{2,1,0:T(8,128)}) custom-call(s32[4]{0:T(128)S(1)} %pad_add_fusion.meta, f32[4,132]{1,0:T(4,128)S(1)} %copy-done.15, f32[4,32,512]{2,1,0:T(8,128)S(1)} %copy-done.1, f32[4,32,512]{2,1,0:T(8,128)S(1)} %copy-done.3, ...), custom_call_target="tpu_custom_call" | custom-call | tf_op jit(solution)/shard_map/local_step/pallas_call | solution.py:391
  20.7 0.8 %copy-done.10 = f32[4,64,512]{2,1,0:T(8,128)} copy-done((f32[4,64,512]{2,1,0:T(8,128)}, f32[4,64,512]{2,1,0:T(8,128)S(1)}, u32[]{:S(2)}) %copy-start.10) | copy-done | bytes 524312
  21.6 2.1 %collective-permute-start.2 = (f32[2,168,512]{2,1,0:T(8,128)}, f32[2,168,512]{2,1,0:T(8,128)S(1)}, u32[]{:S(2)}, u32[]{:S(2)}) collective-permute-start(f32[2,168,512]{2,1,0:T(8,128)} %get-tuple-element.15), channel_id=1, source_target_pairs={{0,8},{8,0},{16,24},{24,16},{32,40},{40,32},{48,56},{56,48},{64,72... | collective-permute-start | bytes 2064392 | tf_op jit(solution)/shard_map/ppermute | solution.py:356
  23.7 3.6 %collective-permute-start.3 = (f32[2,168,512]{2,1,0:T(8,128)}, f32[2,168,512]{2,1,0:T(8,128)S(1)}, u32[]{:S(2)}, u32[]{:S(2)}) collective-permute-start(f32[2,168,512]{2,1,0:T(8,128)} %get-tuple-element.16), channel_id=1, source_target_pairs={{8,16},{24,32},{40,48},{56,64},{72,80},{88,96},{104,112},{120,128}... | collective-permute-start | bytes 2064392 | tf_op jit(solution)/shard_map/ppermute | solution.py:361
  27.3 0.1 collective-permute-start.4
  27.4 2.4 %collective-permute-done.4 = f32[1,128]{1,0:T(1,128)S(1)} collective-permute-done((f32[1,128]{1,0:T(1,128)S(1)}, f32[1,128]{1,0:T(1,128)S(1)}, u32[]{:S(2)}, u32[]{:S(2)}) %collective-permute-start.4) | collective-permute-done | bytes 544 | tf_op jit(solution)/shard_map/ppermute | solution.py:356
  29.7 1.4 %collective-permute-start.5 = (f32[1,128]{1,0:T(1,128)S(1)}, f32[1,128]{1,0:T(1,128)S(1)}, u32[]{:S(2)}, u32[]{:S(2)}) collective-permute-start(f32[1,128]{1,0:T(1,128)S(1)} %fusion), channel_id=1, source_target_pairs={{0,6},{2,4},{4,2},{6,0},{1,7},{3,5},{5,3},{7,1},{8,14},{10,12},{12... | collective-permute-start | bytes 1544 | tf_op jit(solution)/shard_map/ppermute | solution.py:356
  31.1 2.3 %collective-permute-done.5 = f32[1,128]{1,0:T(1,128)S(1)} collective-permute-done((f32[1,128]{1,0:T(1,128)S(1)}, f32[1,128]{1,0:T(1,128)S(1)}, u32[]{:S(2)}, u32[]{:S(2)}) %collective-permute-start.5) | collective-permute-done | bytes 544 | tf_op jit(solution)/shard_map/ppermute | solution.py:356
  33.4 0.6 broadcast_in_dim.11
  34.1 11.0 %all-to-all-start = ((f32[64,1,128]{2,1,0:T(1,128)}), f32[64,1,128]{2,1,0:T(1,128)}, u32[]{:S(2)}, u32[]{:S(2)}) async-start(f32[64,1,128]{2,1,0:T(1,128)} %broadcast_in_dim.11), calls=%async_computation | async-start | bytes 65536 | tf_op jit(solution)/shard_map/all_to_all | solution.py:419
  45.0 3.9 %list_receivers.1.found = s32[1,4224]{1,0:T(1,128)S(1)} custom-call(s32[4]{0:T(128)S(1)} %pad_add_fusion.meta, s32[3,4096]{1,0:T(4,128)S(1)} %copy-done.12), custom_call_target="tpu_custom_call" | custom-call | tf_op jit(solution)/shard_map/list_receivers/pallas_call | solution.py:404
  49.0 0.6 copy-done.13
  49.6 4.6 %all-to-all-done = f32[64,1,128]{2,1,0:T(1,128)} async-done(((f32[64,1,128]{2,1,0:T(1,128)}), f32[64,1,128]{2,1,0:T(1,128)}, u32[]{:S(2)}, u32[]{:S(2)}) %all-to-all-start) | async-done | bytes 32800 | tf_op jit(solution)/shard_map/all_to_all | solution.py:419
  54.2 0.7 %copy-done.16 = s32[3,4]{1,0:T(4,128)S(1)} copy-done((s32[3,4]{1,0:T(4,128)S(1)}, s32[3,4]{1,0:T(4,128)}, u32[]{:S(2)}) %copy-start.16) | copy-done | bytes 72
  54.9 0.0 copy-done.17
  54.9 1.0 %copy-done.11 = f32[4,64,512]{2,1,0:T(8,128)S(1)} copy-done((f32[4,64,512]{2,1,0:T(8,128)S(1)}, f32[4,64,512]{2,1,0:T(8,128)}, u32[]{:S(2)}) %copy-start.11) | copy-done | bytes 524312
  55.9 0.7 %copy-done.14 = s32[1,4224]{1,0:T(1,128)S(1)} copy-done((s32[1,4224]{1,0:T(1,128)S(1)}, s32[1,4224]{1,0:T(1,128)}, u32[]{:S(2)}) %copy-start.14) | copy-done | bytes 16920
  56.7 7.6 %last_step.1 = (f32[4,32,512]{2,1,0:T(8,128)}, f32[4,32,512]{2,1,0:T(8,128)}, f32[4,32,512]{2,1,0:T(8,128)}, f32[4,32,512]{2,1,0:T(8,128)}, f32[4,32,512]{2,1,0:T(8,128)}) custom-call(s32[4]{0:T(128)S(1)} %pad_add_fusion.meta, f32[4,132]{1,0:T(4,128)S(1)} %copy-done.15, f32[4,32,512]{2,1,0:T(8,128)S(1)} %copy-done.1, f32[4,32,512]{2,1,0:T(8,128)S(1)} %copy-done.3, ...), custom_call_target="tpu_custom_call" | custom-call | tf_op jit(solution)/shard_map/last_step/pallas_call | solution.py:422
  (32 shorter events, 0.1 us)
Async XLA Ops:
  0.7 1.0 %copy-start = (f32[4,32,512]{2,1,0:T(8,128)S(1)}, f32[4,32,512]{2,1,0:T(8,128)}, u32[]{:S(2)}) copy-start(f32[4,32,512]{2,1,0:T(8,128)} %u.5) | copy-start | bytes 786436
  1.7 0.9 %copy-start.2 = (f32[4,32,512]{2,1,0:T(8,128)S(1)}, f32[4,32,512]{2,1,0:T(8,128)}, u32[]{:S(2)}) copy-start(f32[4,32,512]{2,1,0:T(8,128)} %a.5) | copy-start | bytes 786436
  2.6 0.9 %copy-start.4 = (f32[4,32,512]{2,1,0:T(8,128)S(1)}, f32[4,32,512]{2,1,0:T(8,128)}, u32[]{:S(2)}) copy-start(f32[4,32,512]{2,1,0:T(8,128)} %u1_.5) | copy-start | bytes 786436
  3.6 0.9 %copy-start.6 = (f32[4,32,512]{2,1,0:T(8,128)S(1)}, f32[4,32,512]{2,1,0:T(8,128)}, u32[]{:S(2)}) copy-start(f32[4,32,512]{2,1,0:T(8,128)} %a1.5) | copy-start | bytes 786436
  4.5 0.9 %copy-start.8 = (f32[4,32,512]{2,1,0:T(8,128)S(1)}, f32[4,32,512]{2,1,0:T(8,128)}, u32[]{:S(2)}) copy-start(f32[4,32,512]{2,1,0:T(8,128)} %v.5) | copy-start | bytes 786436
  5.5 11.9 %copy-start.1 = (f32[4,32,512]{2,1,0:T(8,128)S(1)}, f32[4,32,512]{2,1,0:T(8,128)}, u32[]{:S(2)}) copy-start(f32[4,32,512]{2,1,0:T(8,128)} %u.5) | copy-start | bytes 786436
  5.5 11.9 %copy-start.3 = (f32[4,32,512]{2,1,0:T(8,128)S(1)}, f32[4,32,512]{2,1,0:T(8,128)}, u32[]{:S(2)}) copy-start(f32[4,32,512]{2,1,0:T(8,128)} %a.5) | copy-start | bytes 786436
  5.5 11.9 %copy-start.5 = (f32[4,32,512]{2,1,0:T(8,128)S(1)}, f32[4,32,512]{2,1,0:T(8,128)}, u32[]{:S(2)}) copy-start(f32[4,32,512]{2,1,0:T(8,128)} %u1_.5) | copy-start | bytes 786436
  5.5 12.0 %copy-start.7 = (f32[4,32,512]{2,1,0:T(8,128)S(1)}, f32[4,32,512]{2,1,0:T(8,128)}, u32[]{:S(2)}) copy-start(f32[4,32,512]{2,1,0:T(8,128)} %a1.5) | copy-start | bytes 786436
  5.5 12.0 %copy-start.9 = (f32[4,32,512]{2,1,0:T(8,128)S(1)}, f32[4,32,512]{2,1,0:T(8,128)}, u32[]{:S(2)}) copy-start(f32[4,32,512]{2,1,0:T(8,128)} %v.5) | copy-start | bytes 786436
  6.1 6.2 %copy-start.18 = (f32[2,16]{1,0:T(2,128)S(1)}, f32[2,16]{1,0:T(2,128)}, u32[]{:S(2)}) copy-start(f32[2,16]{1,0:T(2,128)} %param.15) | copy-start | bytes 388
  6.1 11.3 %copy-start.15 = (f32[4,132]{1,0:T(4,128)S(1)}, f32[4,132]{1,0:T(4,128)}, u32[]{:S(2)}) copy-start(f32[4,132]{1,0:T(4,128)} %constant.48.clone.coef) | copy-start | bytes 6340
  6.2 7.3 %collective-permute-start = (f32[4,16,512]{2,1,0:T(8,128)S(1)}, f32[4,16,512]{2,1,0:T(8,128)S(1)}, u32[]{:S(2)}, u32[]{:S(2)}) collective-permute-start(f32[4,16,512]{2,1,0:T(8,128)S(1)} %get-tuple-element.11), channel_id=1, source_target_pairs={{0,1},{1,0},{2,3},{3,2},{4,5},{5,4},{6,7},{7,6},{8,9},{9,8},{10,11... | collective-permute-start | bytes 393224 | tf_op jit(solution)/shard_map/ppermute | solution.py:356
  10.0 7.4 %collective-permute-start.1 = (f32[4,16,512]{2,1,0:T(8,128)S(1)}, f32[4,16,512]{2,1,0:T(8,128)S(1)}, u32[]{:S(2)}, u32[]{:S(2)}) collective-permute-start(f32[4,16,512]{2,1,0:T(8,128)S(1)} %get-tuple-element.12), channel_id=1, source_target_pairs={{0,7},{1,2},{2,1},{3,4},{4,3},{5,6},{6,5},{7,0},{8,15},{9,10},{10,... | collective-permute-start | bytes 393224 | tf_op jit(solution)/shard_map/ppermute | solution.py:356
  20.7 0.8 %copy-start.10 = (f32[4,64,512]{2,1,0:T(8,128)}, f32[4,64,512]{2,1,0:T(8,128)S(1)}, u32[]{:S(2)}) copy-start(f32[4,64,512]{2,1,0:T(8,128)S(1)} %get-tuple-element.14.a0p) | copy-start | bytes 1572868
  21.6 23.5 %copy-start.12 = (s32[3,4096]{1,0:T(4,128)S(1)}, s32[3,4096]{1,0:T(4,128)}, u32[]{:S(2)}) copy-start(s32[3,4096]{1,0:T(4,128)} %rec.3) | copy-start | bytes 147460
  21.6 32.6 %collective-permute-start.2 = (f32[2,168,512]{2,1,0:T(8,128)}, f32[2,168,512]{2,1,0:T(8,128)S(1)}, u32[]{:S(2)}, u32[]{:S(2)}) collective-permute-start(f32[2,168,512]{2,1,0:T(8,128)} %get-tuple-element.15), channel_id=1, source_target_pairs={{0,8},{8,0},{16,24},{24,16},{32,40},{40,32},{48,56},{56,48},{64,72... | collective-permute-start | bytes 2064392 | tf_op jit(solution)/shard_map/ppermute | solution.py:356
  23.7 30.5 %collective-permute-start.3 = (f32[2,168,512]{2,1,0:T(8,128)}, f32[2,168,512]{2,1,0:T(8,128)S(1)}, u32[]{:S(2)}, u32[]{:S(2)}) collective-permute-start(f32[2,168,512]{2,1,0:T(8,128)} %get-tuple-element.16), channel_id=1, source_target_pairs={{8,16},{24,32},{40,48},{56,64},{72,80},{88,96},{104,112},{120,128}... | collective-permute-start | bytes 2064392 | tf_op jit(solution)/shard_map/ppermute | solution.py:361
  27.3 2.5 %collective-permute-start.4 = (f32[1,128]{1,0:T(1,128)S(1)}, f32[1,128]{1,0:T(1,128)S(1)}, u32[]{:S(2)}, u32[]{:S(2)}) collective-permute-start(f32[1,128]{1,0:T(1,128)S(1)} %compare_select_fusion), channel_id=1, source_target_pairs={{0,2},{2,0},{4,6},{6,4},{1,3},{3,1},{5,7},{7,5},{8,10},{10,8},{12,... | collective-permute-start | bytes 1544 | tf_op jit(solution)/shard_map/ppermute | solution.py:356
  29.7 3.7 %collective-permute-start.5 = (f32[1,128]{1,0:T(1,128)S(1)}, f32[1,128]{1,0:T(1,128)S(1)}, u32[]{:S(2)}, u32[]{:S(2)}) collective-permute-start(f32[1,128]{1,0:T(1,128)S(1)} %fusion), channel_id=1, source_target_pairs={{0,6},{2,4},{4,2},{6,0},{1,7},{3,5},{5,3},{7,1},{8,14},{10,12},{12... | collective-permute-start | bytes 1544 | tf_op jit(solution)/shard_map/ppermute | solution.py:356
  34.1 20.1 %all-to-all-start = ((f32[64,1,128]{2,1,0:T(1,128)}), f32[64,1,128]{2,1,0:T(1,128)}, u32[]{:S(2)}, u32[]{:S(2)}) async-start(f32[64,1,128]{2,1,0:T(1,128)} %broadcast_in_dim.11), calls=%async_computation | async-start | bytes 65536 | tf_op jit(solution)/shard_map/all_to_all | solution.py:419
  49.0 0.6 copy-start.13
  54.2 0.7 %copy-start.16 = (s32[3,4]{1,0:T(4,128)S(1)}, s32[3,4]{1,0:T(4,128)}, u32[]{:S(2)}) copy-start(s32[3,4]{1,0:T(4,128)} %src.1) | copy-start | bytes 148
  54.2 0.7 %copy-start.17 = (f32[2,4]{1,0:T(2,128)S(1)}, f32[2,4]{1,0:T(2,128)}, u32[]{:S(2)}) copy-start(f32[2,4]{1,0:T(2,128)} %amp.1) | copy-start | bytes 100
  54.9 1.0 %copy-start.11 = (f32[4,64,512]{2,1,0:T(8,128)S(1)}, f32[4,64,512]{2,1,0:T(8,128)}, u32[]{:S(2)}) copy-start(f32[4,64,512]{2,1,0:T(8,128)} %copy-done.10) | copy-start | bytes 1572868
  55.9 0.7 %copy-start.14 = (s32[1,4224]{1,0:T(1,128)S(1)}, s32[1,4224]{1,0:T(1,128)}, u32[]{:S(2)}) copy-start(s32[1,4224]{1,0:T(1,128)} %copy-done.13) | copy-start | bytes 50692

commit v2 on v1

v2 whole, which is shorter than its diff:
```python
import jax
import jax.numpy as jnp
import numpy as np
from jax import lax
from jax.experimental import pallas as pl
from jax.experimental.pallas import tpu as pltpu
from jax.sharding import Mesh
from jax.sharding import PartitionSpec as P

CENTRE = -7.5
NEAR = 4.0 / 3.0
FAR = -1.0 / 12.0
RATIO = 0.1
DAMP = 0.3

GZ = ("yl", "z", "c")
GY = ("xh", "xl", "yh")
O = 8
NZ_DEV, NY_DEV = 32, 8
CZ, CY, NX = 4, 32, 512
NZ, NY = NZ_DEV * CZ, NY_DEV * CY
FR = CY + 2 * O
VMEM_LIMIT = 16 * 1024 * 1024
ZROWS = 5 * CY + 8


def coefficient_table():
    z = np.clip(np.arange(-2, NZ + 2), 0, NZ - 1).astype(np.float32)
    low = np.maximum(np.float32(CZ) - z, np.float32(0)) / np.float32(CZ)
    high = np.maximum(z - np.float32(NZ - 1 - CZ), np.float32(0)) / np.float32(CZ)
    a = np.float32(DAMP) * (low * low + high * high)
    one = np.float32(1)
    return np.stack([one + a, one - a, one / (one - a), one / (one + a)]).astype(np.float32)


def smem():
    return pl.BlockSpec(memory_space=pltpu.SMEM)


def vmem():
    return pl.BlockSpec(memory_space=pltpu.VMEM)


def x_terms(u):
    lane = lax.broadcasted_iota(jnp.int32, u.shape, 1)
    a = jnp.where(lane >= 1, pltpu.roll(u, 1, 1), 0.0)
    b = jnp.where(lane < NX - 1, pltpu.roll(u, NX - 1, 1), 0.0)
    c = jnp.where(lane >= 2, pltpu.roll(u, 2, 1), 0.0)
    d = jnp.where(lane < NX - 2, pltpu.roll(u, NX - 2, 1), 0.0)
    return a + b, c + d


def laplace(f, k, s):
    rows = lambda layer, shift: f[layer, s + shift : s + shift + 8, :]
    u = rows(k, 0)
    near, far = x_terms(u)
    near = near + ((rows(k, -1) + rows(k, 1)) + (rows(k - 1, 0) + rows(k + 1, 0)))
    far = far + ((rows(k, -2) + rows(k, 2)) + (rows(k - 2, 0) + rows(k + 2, 0)))
    return u, CENTRE * u + NEAR * near + FAR * far


def depth_factors(l):
    near_up = jnp.where(l >= 1, jnp.float32(NEAR), jnp.float32(0.0))
    near_dn = jnp.where(l < CZ - 1, jnp.float32(NEAR), jnp.float32(0.0))
    far_up = jnp.where(l >= 2, jnp.float32(FAR), jnp.float32(0.0))
    far_dn = jnp.where(l < CZ - 2, jnp.float32(FAR), jnp.float32(0.0))
    layers = jnp.maximum(l - 1, 0), jnp.minimum(l + 1, CZ - 1), jnp.maximum(l - 2, 0), jnp.minimum(l + 2, CZ - 1)
    return tuple(zip(layers, (near_up, near_dn, far_up, far_dn)))


def partial_laplace(f, l, s, size, factors):
    u = f[l, s : s + 8, :]

    def shifted(shift):
        if 0 <= s + shift and s + shift + 8 <= size:
            return f[l, s + shift : s + shift + 8, :]
        return pltpu.roll(u, (-shift) % 8, 0)

    near, far = x_terms(u)
    lap = CENTRE * u + NEAR * (near + (shifted(-1) + shifted(1))) + FAR * (far + (shifted(-2) + shifted(2)))
    for layer, factor in factors:
        lap = lap + factor * f[layer, s : s + 8, :]
    return u, lap


def pack_y(meta, u, a, u1, a1, v, obs, h, g, own, first, last, obs_v, row, sem):
    copies = []
    for i, ref in enumerate((u, a, u1, a1, v)):
        copies.append(pltpu.make_async_copy(ref.at[:, 0:8, :], first.at[i], sem.at[2 * i]))
        copies.append(pltpu.make_async_copy(ref.at[:, CY - 8 : CY, :], last.at[i], sem.at[2 * i + 1]))
    copies.append(pltpu.make_async_copy(obs, obs_v, sem.at[10]))
    for copy in copies:
        copy.start()
    for copy in copies:
        copy.wait()
    for k in range(4):
        for t in range(2):
            row[0:1, 32 * k + 16 * t : 32 * k + 16 * t + 16] = obs_v[t : t + 1, :]
    lane = lax.broadcasted_iota(jnp.int32, (1, 128), 1)
    mine = jnp.where((lane >> 5) == meta[4] * 2 + meta[2], row[0:1, :], 0.0)
    own[...] = mine

    def pack(dst, high):
        rows = last if high else first
        four = slice(4, 8) if high else slice(0, 4)
        two = slice(6, 8) if high else slice(0, 2)
        dst[:, 0:4, :] = rows[0, :, four, :]
        dst[:, 4:8, :] = rows[1, :, four, :]
        dst[:, 8:10, :] = rows[2, :, two, :]
        dst[:, 10:12, :] = rows[3, :, two, :]
        dst[:, 12:14, :] = rows[4, :, two, :]
        dst[:, 14:16, :] = jnp.zeros((CZ, 2, NX), jnp.float32)
        dst[0, 14:15, 0:128] = mine

    @pl.when(meta[2] == 0)
    def _():
        pack(h, True)
        pack(g, False)

    @pl.when(meta[2] != 0)
    def _():
        pack(h, False)
        pack(g, True)


def pick_y(meta, rh, rg, low, high):
    @pl.when(meta[2] == 0)
    def _():
        high(rh)
        low(rg)

    @pl.when(meta[2] != 0)
    def _():
        low(rh)
        high(rg)


def own_step(meta, coef, u, a, u1, a1, v, u0p, a0p):
    z0 = meta[0]

    def layer(l, carry):
        i = z0 + l + 2
        up, dn, iu, ia = coef[0, i], coef[1, i], coef[2, i], coef[3, i]
        factors = depth_factors(l)
        for s in range(0, CY, 8):
            y = slice(s, s + 8)
            c = v[l, y, :] * RATIO
            c = c * c
            p, lap = partial_laplace(u, l, s, CY, factors)
            u0p[l, y, :] = (2.0 * p - up * u1[l, y, :] + c * lap) * iu
            q, lap = partial_laplace(a, l, s, CY, factors)
            a0p[l, y, :] = (2.0 * q - dn * a1[l, y, :] + c * lap) * ia
        return carry

    lax.fori_loop(0, CZ, layer, 0)


def edge_step(
    meta, coef, u, a, u1, a1, v, rh, rg, own, u0p, a0p, ulo, uhi, alo, ahi, zc, zb, traces,
    pu, pa, pu1, pa1, pv,
):
    z0 = meta[0]
    pu[0, :, 4:8, :] = u[:, 0:4, :]
    pu[1, :, 0:4, :] = u[:, CY - 4 : CY, :]
    pa[0, :, 4:8, :] = a[:, 0:4, :]
    pa[1, :, 0:4, :] = a[:, CY - 4 : CY, :]
    for part, block in ((pu1, u1), (pa1, a1), (pv, v)):
        part[0, :, 4:6, :] = block[:, 0:2, :]
        part[1, :, 2:4, :] = block[:, CY - 2 : CY, :]

    def low(r):
        pu[0, :, 0:4, :] = r[:, 0:4, :]
        pa[0, :, 0:4, :] = r[:, 4:8, :]
        pu1[0, :, 2:4, :] = r[:, 8:10, :]
        pa1[0, :, 2:4, :] = r[:, 10:12, :]
        pv[0, :, 2:4, :] = r[:, 12:14, :]

    def high(r):
        pu[1, :, 4:8, :] = r[:, 0:4, :]
        pa[1, :, 4:8, :] = r[:, 4:8, :]
        pu1[1, :, 4:6, :] = r[:, 8:10, :]
        pa1[1, :, 4:6, :] = r[:, 10:12, :]
        pv[1, :, 4:6, :] = r[:, 12:14, :]

    pick_y(meta, rh, rg, low, high)

    def layer(l, carry):
        i = z0 + l + 2
        up, dn, iu, ia = coef[0, i], coef[1, i], coef[2, i], coef[3, i]
        factors = depth_factors(l)
        for side, uo, ao in ((0, ulo, alo), (1, uhi, ahi)):
            c = pv[side, l] * RATIO
            c = c * c
            p, lap = partial_laplace(pu.at[side], l, 0, 8, factors)
            uo[l] = (2.0 * p - up * pu1[side, l] + c * lap) * iu
            q, lap = partial_laplace(pa.at[side], l, 0, 8, factors)
            ao[l] = (2.0 * q - dn * pa1[side, l] + c * lap) * ia
        return carry

    lax.fori_loop(0, CZ, layer, 0)

    def pack(dst, l):
        m = slice(l, l + 2)
        dst[:, 0:CY, :] = u[m]
        dst[:, CY : 2 * CY, :] = a[m]
        dst[:, 4 * CY : 5 * CY, :] = v[m]
        for b, p, lo, hi in ((2 * CY, u0p, ulo, uhi), (3 * CY, a0p, alo, ahi)):
            dst[:, b : b + CY, :] = p[m]
            dst[:, b : b + 2, :] = lo[m, 4:6, :]
            dst[:, b + CY - 2 : b + CY, :] = hi[m, 2:4, :]
        b = 5 * CY
        dst[:, b : b + 2, :] = pu[0, m, 2:4, :]
        dst[:, b + 2 : b + 4, :] = pu[1, m, 4:6, :]
        dst[:, b + 4 : b + 6, :] = pa[0, m, 2:4, :]
        dst[:, b + 6 : b + 8, :] = pa[1, m, 4:6, :]

    @pl.when(meta[3] == 0)
    def _():
        pack(zc, 2)
        pack(zb, 0)

    @pl.when(meta[3] != 0)
    def _():
        pack(zc, 0)
        pack(zb, 2)

    mine = rg[0, 14:15, 0:128] + rg[0, 15:16, 0:128] + rh[0, 14:15, 0:128] + own[...]
    traces[...] = jnp.broadcast_to(mine, traces.shape)


def list_receivers(meta, rec, rec_s, out, bits, words_v, words, sem):
    z0, y0 = meta[0], meta[1]
    lz = rec[0:1, :] - z0
    ly = ((rec[1:2, :] - y0 + 16) & (NY - 1)) - 16
    own_z = (lz >= 0) & (lz < CZ)
    own_y = (ly >= 0) & (ly < CY)
    near = (lz >= -2) & (lz < CZ + 2) & (ly >= -2) & (ly < CY + 2) & (own_z | own_y)
    m = near.astype(jnp.int32)
    for i in range(32):
        bits[i : i + 1, :] = m[:, 128 * i : 128 * i + 128] << i
    words_v[...] = jnp.sum(bits[...], axis=0, keepdims=True)
    copy = pltpu.make_async_copy(words_v, words, sem)
    copy.start()
    copy.wait()

    def word_step(w, count):
        def bit_step(carry):
            word, count = carry
            low = word & (-word)
            r = (31 - lax.clz(low)) * 128 + w
            z = rec_s[0, r] - z0 + 2
            y = (rec_s[1, r] - y0 + 2) & (NY - 1)
            out[0, count + 1] = r | (rec_s[2, r] << 12) | (y << 21) | (z << 27)
            return word ^ low, count + 1

        return lax.while_loop(lambda carry: carry[0] != 0, bit_step, (words[0, w], count))[1]

    out[0, 0] = lax.fori_loop(0, 128, word_step, 0)


def cell_place():
    return lax.broadcasted_iota(jnp.int32, (8, 128), 0) * 128 + lax.broadcasted_iota(jnp.int32, (8, 128), 1)


def cell_at(place, layer, row, x):
    rows = pl.ds(pl.multiple_of((row >> 3) << 3, 8), 8)
    cols = pl.ds(pl.multiple_of((x >> 7) << 7, 128), 128)
    return (layer, rows, cols), place == ((row & 7) * 128 + (x & 127))


def wave_step(
    meta, coef, u, a, u1, v, rh, rg, u0p, a0p, ulo, uhi, alo, ahi, rc, rb, src, amp,
    u2, u0o, w, gp, uf, u0f, a0f,
    af, vf,
):
    e = O + CY
    z0, y0 = meta[0], meta[1]
    uf[2:6, O:e, :] = u[...]
    vf[2:6, O:e, :] = v[...]
    u0f[2:6, O:e, :] = u0p[...]
    a0f[2:6, O:e, :] = a0p[...]
    for f0, lo, hi in ((u0f, ulo, uhi), (a0f, alo, ahi)):
        f0[2:6, O - 2 : O + 2, :] = lo[:, 2:6, :]
        f0[2:6, e - 2 : e + 2, :] = hi[:, 2:6, :]

    def low(r):
        uf[2:6, O - 2 : O, :] = r[:, 2:4, :]
        vf[2:6, O - 2 : O, :] = r[:, 12:14, :]

    def high(r):
        uf[2:6, e : e + 2, :] = r[:, 0:2, :]
        vf[2:6, e : e + 2, :] = r[:, 12:14, :]

    pick_y(meta, rh, rg, low, high)

    def fill_z(r, k):
        b = 5 * CY
        m = slice(k, k + 2)
        uf[m, O:e, :] = r[:, 0:CY, :]
        af[m, O:e, :] = r[:, CY : 2 * CY, :]
        u0f[m, O:e, :] = r[:, 2 * CY : 3 * CY, :]
        a0f[m, O:e, :] = r[:, 3 * CY : 4 * CY, :]
        vf[m, O:e, :] = r[:, 4 * CY : 5 * CY, :]
        uf[m, O - 2 : O, :] = r[:, b : b + 2, :]
        uf[m, e : e + 2, :] = r[:, b + 2 : b + 4, :]
        af[m, O - 2 : O, :] = r[:, b + 4 : b + 6, :]
        af[m, e : e + 2, :] = r[:, b + 6 : b + 8, :]

    @pl.when(meta[3] == 0)
    def _():
        fill_z(rb, 0)
        fill_z(rc, 6)

    @pl.when(meta[3] != 0)
    def _():
        fill_z(rc, 0)
        fill_z(rb, 6)

    lacks = ((0, None, 2), (1, 2, 3), (2, 1, 0), (3, None, 1), (4, None, 6), (5, 6, 7), (6, 5, 4), (7, None, 5))
    for k, near, far in lacks:
        edge = 2 <= k < 6
        iu, ia = coef[2, z0 + k], coef[3, z0 + k]

        def rows(t, carry):
            s = pl.multiple_of(t * 8, 8)
            c = vf[k, pl.ds(s, 8), :] * RATIO
            c = c * c
            for f, own, f0, scale in ((uf, u, u0f, iu), (af, a, a0f, ia)):
                term = lambda j: own[j - 2, pl.ds(s - O, 8), :] if 2 <= j < 6 else f[j, pl.ds(s, 8), :]
                lap = FAR * term(far)
                if near is not None:
                    lap = lap + NEAR * term(near)
                f0[k, pl.ds(s, 8), :] = f0[k, pl.ds(s, 8), :] + (c * scale) * lap
            return carry

        first = O // 8
        lax.fori_loop(first - edge, first + CY // 8 + edge, rows, 0)

    place = cell_place()

    def source_cell(i):
        return src[0, i] - z0, ((src[1, i] - y0 + 16) & (NY - 1)) - 16, src[2, i]

    def add_source_0(i, carry):
        lz, ly, x = source_cell(i)
        own_z = (lz >= 0) & (lz < CZ)
        own_y = (ly >= 0) & (ly < CY)
        near = (lz >= -2) & (lz < CZ + 2) & (ly >= -2) & (ly < CY + 2) & (own_z | own_y)

        @pl.when(near)
        def _():
            at, hit = cell_at(place, lz + 2, ly + O, x)
            c = vf[at] * RATIO
            u0f[at] = u0f[at] + jnp.where(hit, (c * c) * (amp[0, i] * coef[2, z0 + lz + 2]), 0.0)

        return carry

    lax.fori_loop(0, src.shape[1], add_source_0, 0)

    def layer(l, carry):
        i = z0 + l + 2
        up, iu = coef[0, i], coef[2, i]
        for s in range(O, O + CY, 8):
            y = slice(s - O, s - O + 8)
            vel = v[l, y, :]
            c = vel * RATIO
            c = c * c
            un = u[l, y, :]
            q, lap = laplace(u0f, l + 2, s)
            new = (2.0 * q - up * un + c * lap) * iu
            u2[l, y, :] = new
            u0o[l, y, :] = q
            slow = 2.0 / vel
            w[l, y, :] = slow * (un - 2.0 * q + new)
            gp[l, y, :] = slow * a[l, y, :] * (u1[l, y, :] - 2.0 * un + q)
        return carry

    lax.fori_loop(0, CZ, layer, 0)

    def add_source_1(i, carry):
        lz, ly, x = source_cell(i)

        @pl.when((lz >= 0) & (lz < CZ) & (ly >= 0) & (ly < CY))
        def _():
            at, hit = cell_at(place, lz, ly, x)
            vel = v[at]
            c = vel * RATIO
            added = jnp.where(hit, (c * c) * (amp[1, i] * coef[2, z0 + lz + 2]), 0.0)
            u2[at] = u2[at] + added
            w[at] = w[at] + (2.0 / vel) * added

        return carry

    lax.fori_loop(0, src.shape[1], add_source_1, 0)


def adjoint_step(meta, coef, a, v, uf, u0f, a0p, w, gp, found, table, a2, a0o, grad, a0f):
    z0, yh, xl = meta[0], meta[2], meta[4]
    for k in range(8):
        a0f[k] = a0p[k]
    place = cell_place()
    turn = 1 - 2 * yh

    def observed(step, r):
        x = (r >> 5) & 3
        sender = (x + turn * ((x ^ xl) & 1)) & 3
        return table[(r >> 7) * 2 + (sender >> 1), ((x & 1) * 2 + ((r >> 4) & 1)) * 32 + step * 16 + (r & 15)]

    def add_receiver_0(n, carry):
        code = found[0, n + 1]
        r, x, y, z = code & 4095, (code >> 12) & 511, (code >> 21) & 63, code >> 27
        at, hit = cell_at(place, z, y + (O - 2), x)
        residual = (uf[at] - observed(0, r)) * coef[3, z0 + z]
        a0f[at] = a0f[at] + jnp.where(hit, residual, 0.0)
        return carry

    count = found[0, 0]
    lax.fori_loop(0, count, add_receiver_0, 0)

    def layer(l, carry):
        i = z0 + l + 2
        dn, ia = coef[1, i], coef[3, i]
        for s in range(O, O + CY, 8):
            y = slice(s - O, s - O + 8)
            c = v[l, y, :] * RATIO
            c = c * c
            q, lap = laplace(a0f, l + 2, s)
            a2[l, y, :] = (2.0 * q - dn * a[l, y, :] + c * lap) * ia
            a0o[l, y, :] = q
            grad[l, y, :] = gp[l, y, :] + w[l, y, :] * q
        return carry

    lax.fori_loop(0, CZ, layer, 0)

    def add_receiver_1(n, carry):
        code = found[0, n + 1]
        r, x, y, z = code & 4095, (code >> 12) & 511, ((code >> 21) & 63) - 2, (code >> 27) - 2

        @pl.when((z >= 0) & (z < CZ) & (y >= 0) & (y < CY))
        def _():
            at, hit = cell_at(place, z, y, x)
            before, _ = cell_at(place, z + 2, y + O, x)
            residual = (u0f[before] - observed(1, r)) * coef[3, z0 + z + 2]
            a2[at] = a2[at] + jnp.where(hit, residual, 0.0)

        return carry

    lax.fori_loop(0, count, add_receiver_1, 0)


def f32(*shape):
    return jax.ShapeDtypeStruct(shape, jnp.float32)


def call(kernel, out_shape, in_specs, scratch_shapes=()):
    many = isinstance(out_shape, tuple)
    return pl.pallas_call(
        kernel,
        out_shape=out_shape,
        in_specs=in_specs,
        out_specs=(vmem(),) * len(out_shape) if many else smem(),
        scratch_shapes=scratch_shapes,
        compiler_params=pltpu.CompilerParams(vmem_limit_bytes=VMEM_LIMIT),
        name=kernel.__name__,
    )


def swap(value, axis, size, first):
    pairs = [(i, (first + ((i - first) % size ^ 1)) % size) for i in range(size)]
    return lax.ppermute(value, axis, pairs)


def swap_open(value, axis, size):
    pairs = [(i, i + 1) for i in range(1, size - 1, 2)]
    return lax.ppermute(value, axis, pairs + [(j, i) for i, j in pairs])


def shards(u, u1, a, a1, v, obs, rec, src, amp):
    assert u.shape == (CZ, CY, NX)
    gz, gy = lax.axis_index(GZ), lax.axis_index(GY)
    meta = [gz * CZ, gy * CY, lax.axis_index("yh"), lax.axis_index("c"), lax.axis_index("xl")]
    meta = jnp.stack(meta).astype(jnp.int32)
    coef = jnp.asarray(coefficient_table())
    block, edge = f32(CZ, CY, NX), f32(CZ, 8, NX)
    frame, zpack = f32(8, FR, NX), f32(2, ZROWS, NX)
    part = pltpu.VMEM((2, CZ, 8, NX), jnp.float32)
    full = pltpu.VMEM((8, FR, NX), jnp.float32)

    h, g, own = call(
        pack_y,
        (f32(CZ, 16, NX), f32(CZ, 16, NX), f32(1, 128)),
        [smem()] + [pl.BlockSpec(memory_space=pltpu.HBM)] * 6,
        [pltpu.VMEM((5, CZ, 8, NX), jnp.float32)] * 2
        + [pltpu.VMEM((2, 16), jnp.float32), pltpu.VMEM((1, 128), jnp.float32), pltpu.SemaphoreType.DMA((11,))],
    )(meta, u, a, u1, a1, v, obs)
    rh = swap(h, GY, NY_DEV, 0)
    g = lax.dynamic_update_slice(g, rh[0:1, 14:15, :], (0, 15, 0))
    rg = swap(g, GY, NY_DEV, 1)

    u0p, a0p = call(own_step, (block, block), [smem()] * 2 + [vmem()] * 5)(meta, coef, u, a, u1, a1, v)

    found = call(
        list_receivers,
        jax.ShapeDtypeStruct((1, rec.shape[1] + 128), jnp.int32),
        [smem(), vmem(), smem()],
        [
            pltpu.VMEM((32, 128), jnp.int32),
            pltpu.VMEM((1, 128), jnp.int32),
            pltpu.SMEM((1, 128), jnp.int32),
            pltpu.SemaphoreType.DMA,
        ],
    )(meta, rec, rec)

    ulo, uhi, alo, ahi, zc, zb, traces = call(
        edge_step,
        (edge,) * 4 + (zpack, zpack, f32(64, 128)),
        [smem()] * 2 + [vmem()] * 10,
        [part] * 5,
    )(meta, coef, u, a, u1, a1, v, rh, rg, own, u0p, a0p)

    rc = swap(zc, GZ, NZ_DEV, 0)
    rb = swap_open(zb, GZ, NZ_DEV)
    table = lax.all_to_all(traces, ("yl", "z", "c", "xh"), 0, 0, tiled=True)

    u2, u0, w, gp, uf, u0f, a0f = call(
        wave_step,
        (block,) * 4 + (frame,) * 3,
        [smem()] * 2 + [vmem()] * 14 + [smem()] * 2,
        [full] * 2,
    )(meta, coef, u, a, u1, v, rh, rg, u0p, a0p, ulo, uhi, alo, ahi, rc, rb, src, amp)

    a2, a0, grad = call(
        adjoint_step,
        (block,) * 3,
        [smem()] * 2 + [vmem()] * 7 + [smem()] * 2,
        [full],
    )(meta, coef, a, v, uf, u0f, a0f, w, gp, found, table)
    return u2, u0, a2, a0, grad


def solution(mesh):
    fine = Mesh(mesh.devices.reshape(2, 8, 2, 2, 2, 2), ("yl", "z", "c", "xh", "xl", "yh"))
    field = P(GZ, GY, None)
    return jax.shard_map(
        shards,
        mesh=fine,
        in_specs=(field,) * 5 + (P(None, GZ + GY), P(), P(), P()),
        out_specs=(field,) * 5,
        check_vma=False,
    )
```

time: 64.8 us -> 74.2 us (1.15)
  the two profiles are of different devices: /device:TPU:1 before, /device:TPU:23 now
where the time goes in v2:
time: 74.2 us; the launch traced here: 73.3 us
  local copies, waits for them, and re-layouts  24.5 us (33%)
  Pallas kernels  18.8 us (25%)
  starting transfers between devices  18 us (24%)
  waiting for transfers between devices  11.2 us (15%)
  between operations  0.82 us (1%)
    unnamed x78, local copies, waits for them, and re-layouts  24.3 us
    all_to_all x1, starting transfers between devices, shards(): table = lax.all_to_all(traces, ('yl', 'z', 'c', 'xh'), 0, 0, tiled=True)  11.6 us
    ppermute x3, waiting for transfers between devices, swap(): return lax.ppermute(value, axis, pairs)  11.2 us
    pallas_call x1, Pallas kernels, shards(): call(adjoint_step, (block,) * 3, [smem()] * 2 + [vmem()] * 7 + [smem()] *...  5.29 us
    pallas_call x1, Pallas kernels, shards(): call(list_receivers, jax.ShapeDtypeStruct((1, rec.shape[1] + 128), jnp.in...  5.28 us
    ppermute x1, starting transfers between devices, swap_open(): return lax.ppermute(value, axis, pairs + [(j, i) for i, j in pairs])  3.55 us
    pallas_call x1, Pallas kernels, shards(): call(wave_step, (block,) * 4 + (frame,) * 3, [smem()] * 2 + [vmem()] * 14...  3 us
    ppermute x3, starting transfers between devices, swap(): return lax.ppermute(value, axis, pairs)  2.88 us
  transfers between devices with their start and end apart: 5, of which 2 were waited for; matrix products, arithmetic and copies ran while one was open for 0% of the time, Pallas kernels for 13%

profile of v2, /device:TPU:23, one launch (start us, length us, event | category | flops | bytes accessed | tf_op | source)
XLA Modules:
  0.0 73.3 jit_solution(6009728124587303406)
XLA Ops:
  1.3 0.9 %copy-done = f32[4,32,512]{2,1,0:T(8,128)S(1)} copy-done((f32[4,32,512]{2,1,0:T(8,128)S(1)}, f32[4,32,512]{2,1,0:T(8,128)}, u32[]{:S(2)}) %copy-start) | copy-done | bytes 262168
  2.3 0.9 %copy-done.2 = f32[4,32,512]{2,1,0:T(8,128)S(1)} copy-done((f32[4,32,512]{2,1,0:T(8,128)S(1)}, f32[4,32,512]{2,1,0:T(8,128)}, u32[]{:S(2)}) %copy-start.2) | copy-done | bytes 262168
  3.2 0.9 %copy-done.4 = f32[4,32,512]{2,1,0:T(8,128)S(1)} copy-done((f32[4,32,512]{2,1,0:T(8,128)S(1)}, f32[4,32,512]{2,1,0:T(8,128)}, u32[]{:S(2)}) %copy-start.4) | copy-done | bytes 262168
  4.2 0.9 %copy-done.6 = f32[4,32,512]{2,1,0:T(8,128)S(1)} copy-done((f32[4,32,512]{2,1,0:T(8,128)S(1)}, f32[4,32,512]{2,1,0:T(8,128)}, u32[]{:S(2)}) %copy-start.6) | copy-done | bytes 262168
  5.1 0.9 %copy-done.8 = f32[4,32,512]{2,1,0:T(8,128)S(1)} copy-done((f32[4,32,512]{2,1,0:T(8,128)S(1)}, f32[4,32,512]{2,1,0:T(8,128)}, u32[]{:S(2)}) %copy-start.8) | copy-done | bytes 262168
  6.1 1.0 %pack_y.1 = (f32[4,16,512]{2,1,0:T(8,128)S(1)}, f32[4,16,512]{2,1,0:T(8,128)S(1)}, f32[1,128]{1,0:T(1,128)S(1)}) custom-call(s32[5]{0:T(128)S(1)} %stack.23.meta, f32[4,32,512]{2,1,0:T(8,128)S(1)} %copy-done.4, f32[4,32,512]{2,1,0:T(8,128)S(1)} %copy-done, f32[4,32,512]{2,1,0:T(8,128)S(1)} %copy-done.6, f32[4,32,512]{2,1,0:T(8,128)S(1)} %copy-done.8, ...), custom_call_target="tpu_custom_call" | custom-call | tf_op jit(solution)/shard_map/pack_y/pallas_call | solution.py:489
  7.2 5.9 %collective-permute-done.rh = f32[4,16,512]{2,1,0:T(8,128)S(1)} collective-permute-done((f32[4,16,512]{2,1,0:T(8,128)S(1)}, f32[4,16,512]{2,1,0:T(8,128)S(1)}, u32[]{:S(2)}, u32[]{:S(2)}) %collective-permute-start) | collective-permute-done | bytes 131104 | tf_op jit(solution)/shard_map/ppermute | solution.py:470
  13.8 1.5 %own_step.1 = (f32[4,32,512]{2,1,0:T(8,128)S(1)}, f32[4,32,512]{2,1,0:T(8,128)S(1)}) custom-call(s32[5]{0:T(128)S(1)} %stack.23.meta, f32[4,132]{1,0:T(4,128)S(1)} %copy-done.27, f32[4,32,512]{2,1,0:T(8,128)S(1)} %copy-done.5, f32[4,32,512]{2,1,0:T(8,128)S(1)} %copy-done.1, f32[4,32,512]{2,1,0:T(8,128)S(1)} %copy-done.7, f32[4,32,512]{2,1,0:T(8,128)S(1)} %copy-done.9, ...), custom_call_target="tpu_custom_call" | custom-call | tf_op jit(solution)/shard_map/own_step/pallas_call | solution.py:500
  15.3 5.4 %collective-permute-done.1.rg = f32[4,16,512]{2,1,0:T(8,128)S(1)} collective-permute-done((f32[4,16,512]{2,1,0:T(8,128)S(1)}, f32[4,16,512]{2,1,0:T(8,128)S(1)}, u32[]{:S(2)}, u32[]{:S(2)}) %collective-permute-start.1) | collective-permute-done | bytes 131104 | tf_op jit(solution)/shard_map/ppermute | solution.py:470
  20.7 2.7 %edge_step.1 = (f32[4,8,512]{2,1,0:T(8,128)S(1)}, f32[4,8,512]{2,1,0:T(8,128)S(1)}, f32[4,8,512]{2,1,0:T(8,128)S(1)}, f32[4,8,512]{2,1,0:T(8,128)S(1)}, f32[2,16...) custom-call(s32[5]{0:T(128)S(1)} %stack.23.meta, f32[4,132]{1,0:T(4,128)S(1)} %copy-done.27, ...), custom_call_target="tpu_custom_call" | custom-call | tf_op jit(solution)/shard_map/edge_step/pallas_call | solution.py:514
  25.9 2.7 %collective-permute-start.2 = (f32[2,168,512]{2,1,0:T(8,128)}, f32[2,168,512]{2,1,0:T(8,128)S(1)}, u32[]{:S(2)}, u32[]{:S(2)}) collective-permute-start(f32[2,168,512]{2,1,0:T(8,128)} %get-tuple-element.36), channel_id=1, source_target_pairs={{0,8},{8,0},{16,24},{24,16},{32,40},{40,32},{48,56},{56,48},{64,72... | collective-permute-start | bytes 2064392 | tf_op jit(solution)/shard_map/ppermute | solution.py:470
  28.6 3.6 %collective-permute-start.3 = (f32[2,168,512]{2,1,0:T(8,128)}, f32[2,168,512]{2,1,0:T(8,128)S(1)}, u32[]{:S(2)}, u32[]{:S(2)}) collective-permute-start(f32[2,168,512]{2,1,0:T(8,128)} %get-tuple-element.37), channel_id=1, source_target_pairs={{8,16},{24,32},{40,48},{56,64},{72,80},{88,96},{104,112},{120,128}... | collective-permute-start | bytes 2064392 | tf_op jit(solution)/shard_map/ppermute | solution.py:475
  32.1 11.6 %all-to-all-start = ((f32[64,1,128]{2,1,0:T(1,128)}), f32[64,1,128]{2,1,0:T(1,128)S(1)}, u32[]{:S(2)}, u32[]{:S(2)}) async-start(f32[64,1,128]{2,1,0:T(1,128)} %bitcast.6), calls=%async_computation | async-start | bytes 65536 | tf_op jit(solution)/shard_map/all_to_all | solution.py:523
  43.7 5.3 %list_receivers.1.found = s32[1,4224]{1,0:T(1,128)S(1)} custom-call(s32[5]{0:T(128)S(1)} %stack.23.meta, s32[3,4096]{1,0:T(4,128)S(1)} %copy-done.22, s32[3,4096]{1,0:T(4,128)S(1)} %copy-done.22), custom_call_target="tpu_custom_call" | custom-call | tf_op jit(solution)/shard_map/list_receivers/pallas_call | solution.py:502
  49.6 0.9 %copy-done.12 = f32[2,168,512]{2,1,0:T(8,128)} copy-done((f32[2,168,512]{2,1,0:T(8,128)}, f32[2,168,512]{2,1,0:T(8,128)S(1)}, u32[]{:S(2)}) %copy-start.12) | copy-done | bytes 688152
  50.5 0.9 %copy-done.14 = f32[2,168,512]{2,1,0:T(8,128)} copy-done((f32[2,168,512]{2,1,0:T(8,128)}, f32[2,168,512]{2,1,0:T(8,128)S(1)}, u32[]{:S(2)}) %copy-start.14) | copy-done | bytes 688152
  52.0 1.1 %copy-done.13 = f32[2,168,512]{2,1,0:T(8,128)S(1)} copy-done((f32[2,168,512]{2,1,0:T(8,128)S(1)}, f32[2,168,512]{2,1,0:T(8,128)}, u32[]{:S(2)}) %copy-start.13) | copy-done | bytes 688152
  53.1 1.1 %copy-done.15 = f32[2,168,512]{2,1,0:T(8,128)S(1)} copy-done((f32[2,168,512]{2,1,0:T(8,128)S(1)}, f32[2,168,512]{2,1,0:T(8,128)}, u32[]{:S(2)}) %copy-start.15) | copy-done | bytes 688152
  54.2 0.8 %copy-done.29 = f32[4,8,512]{2,1,0:T(8,128)S(1)} copy-done((f32[4,8,512]{2,1,0:T(8,128)S(1)}, f32[4,8,512]{2,1,0:T(8,128)}, u32[]{:S(2)}) %copy-start.29) | copy-done | bytes 65560
  55.1 0.8 %copy-done.31 = f32[4,8,512]{2,1,0:T(8,128)S(1)} copy-done((f32[4,8,512]{2,1,0:T(8,128)S(1)}, f32[4,8,512]{2,1,0:T(8,128)}, u32[]{:S(2)}) %copy-start.31) | copy-done | bytes 65560
  55.9 0.8 %copy-done.33 = f32[4,8,512]{2,1,0:T(8,128)S(1)} copy-done((f32[4,8,512]{2,1,0:T(8,128)S(1)}, f32[4,8,512]{2,1,0:T(8,128)}, u32[]{:S(2)}) %copy-start.33) | copy-done | bytes 65560
  56.7 0.8 %copy-done.35 = f32[4,8,512]{2,1,0:T(8,128)S(1)} copy-done((f32[4,8,512]{2,1,0:T(8,128)S(1)}, f32[4,8,512]{2,1,0:T(8,128)}, u32[]{:S(2)}) %copy-start.35) | copy-done | bytes 65560
  57.6 3.0 %wave_step.1 = (f32[4,32,512]{2,1,0:T(8,128)}, f32[4,32,512]{2,1,0:T(8,128)}, f32[4,32,512]{2,1,0:T(8,128)S(1)}, f32[4,32,512]{2,1,0:T(8,128)S(1)}, f32[8,48,512...) custom-call(s32[5]{0:T(128)S(1)} %stack.23.meta, f32[4,132]{1,0:T(4,128)S(1)} %copy-done.27, ...), custom_call_target="tpu_custom_call" | custom-call | tf_op jit(solution)/shard_map/wave_step/pallas_call | solution.py:525
  60.6 0.9 %copy-done.10 = f32[8,48,512]{2,1,0:T(8,128)} copy-done((f32[8,48,512]{2,1,0:T(8,128)}, f32[8,48,512]{2,1,0:T(8,128)S(1)}, u32[]{:S(2)}) %copy-start.10) | copy-done | bytes 786456
  61.5 0.7 copy-done.18
  62.2 0.7 copy-done.20
  63.5 1.1 %copy-done.11 = f32[8,48,512]{2,1,0:T(8,128)S(1)} copy-done((f32[8,48,512]{2,1,0:T(8,128)S(1)}, f32[8,48,512]{2,1,0:T(8,128)}, u32[]{:S(2)}) %copy-start.11) | copy-done | bytes 786456
  64.6 0.9 %copy-done.19 = f32[4,32,512]{2,1,0:T(8,128)S(1)} copy-done((f32[4,32,512]{2,1,0:T(8,128)S(1)}, f32[4,32,512]{2,1,0:T(8,128)}, u32[]{:S(2)}) %copy-start.19) | copy-done | bytes 262168
  65.6 0.9 %copy-done.21 = f32[4,32,512]{2,1,0:T(8,128)S(1)} copy-done((f32[4,32,512]{2,1,0:T(8,128)S(1)}, f32[4,32,512]{2,1,0:T(8,128)}, u32[]{:S(2)}) %copy-start.21) | copy-done | bytes 262168
  66.5 0.8 %copy-done.24 = f32[64,1,128]{2,1,0:T(1,128)S(1)} copy-done((f32[64,1,128]{2,1,0:T(1,128)S(1)}, f32[64,1,128]{2,1,0:T(1,128)}, u32[]{:S(2)}) %copy-start.24) | copy-done | bytes 32792
  67.3 0.7 copy-done.26
  68.0 5.3 %adjoint_step.1 = (f32[4,32,512]{2,1,0:T(8,128)}, f32[4,32,512]{2,1,0:T(8,128)}, f32[4,32,512]{2,1,0:T(8,128)}) custom-call(s32[5]{0:T(128)S(1)} %stack.23.meta, f32[4,132]{1,0:T(4,128)S(1)} %copy-done.27, f32[4,32,512]{2,1,0:T(8,128)S(1)} %copy-done.1, f32[4,32,512]{2,1,0:T(8,128)S(1)} %copy-done.3, f32[8,48,512]{2,1,0:T(8,128)S(1)} %get-tuple-element.40.uf, ...), custom_call_target="tpu_custom_call" | custom-call | tf_op jit(solution)/shard_map/adjoint_step/pallas_call | solution.py:532
  (65 shorter events, 5.9 us)
Async XLA Ops:
  1.3 0.9 %copy-start = (f32[4,32,512]{2,1,0:T(8,128)S(1)}, f32[4,32,512]{2,1,0:T(8,128)}, u32[]{:S(2)}) copy-start(f32[4,32,512]{2,1,0:T(8,128)} %a.9) | copy-start | bytes 786436
  2.3 0.9 %copy-start.2 = (f32[4,32,512]{2,1,0:T(8,128)S(1)}, f32[4,32,512]{2,1,0:T(8,128)}, u32[]{:S(2)}) copy-start(f32[4,32,512]{2,1,0:T(8,128)} %v.9) | copy-start | bytes 786436
  3.2 0.9 %copy-start.4 = (f32[4,32,512]{2,1,0:T(8,128)S(1)}, f32[4,32,512]{2,1,0:T(8,128)}, u32[]{:S(2)}) copy-start(f32[4,32,512]{2,1,0:T(8,128)} %u.7) | copy-start | bytes 786436
  4.2 0.9 %copy-start.6 = (f32[4,32,512]{2,1,0:T(8,128)S(1)}, f32[4,32,512]{2,1,0:T(8,128)}, u32[]{:S(2)}) copy-start(f32[4,32,512]{2,1,0:T(8,128)} %u1_.7) | copy-start | bytes 786436
  5.1 0.9 %copy-start.8 = (f32[4,32,512]{2,1,0:T(8,128)S(1)}, f32[4,32,512]{2,1,0:T(8,128)}, u32[]{:S(2)}) copy-start(f32[4,32,512]{2,1,0:T(8,128)} %a1.5) | copy-start | bytes 786436
  6.1 7.2 %copy-start.1 = (f32[4,32,512]{2,1,0:T(8,128)S(1)}, f32[4,32,512]{2,1,0:T(8,128)}, u32[]{:S(2)}) copy-start(f32[4,32,512]{2,1,0:T(8,128)} %a.9) | copy-start | bytes 786436
  6.1 7.2 %copy-start.3 = (f32[4,32,512]{2,1,0:T(8,128)S(1)}, f32[4,32,512]{2,1,0:T(8,128)}, u32[]{:S(2)}) copy-start(f32[4,32,512]{2,1,0:T(8,128)} %v.9) | copy-start | bytes 786436
  6.1 7.2 %copy-start.5 = (f32[4,32,512]{2,1,0:T(8,128)S(1)}, f32[4,32,512]{2,1,0:T(8,128)}, u32[]{:S(2)}) copy-start(f32[4,32,512]{2,1,0:T(8,128)} %u.7) | copy-start | bytes 786436
  6.1 7.2 %copy-start.7 = (f32[4,32,512]{2,1,0:T(8,128)S(1)}, f32[4,32,512]{2,1,0:T(8,128)}, u32[]{:S(2)}) copy-start(f32[4,32,512]{2,1,0:T(8,128)} %u1_.7) | copy-start | bytes 786436
  6.1 7.2 %copy-start.9 = (f32[4,32,512]{2,1,0:T(8,128)S(1)}, f32[4,32,512]{2,1,0:T(8,128)}, u32[]{:S(2)}) copy-start(f32[4,32,512]{2,1,0:T(8,128)} %a1.5) | copy-start | bytes 786436
  7.1 6.0 %collective-permute-start = (f32[4,16,512]{2,1,0:T(8,128)S(1)}, f32[4,16,512]{2,1,0:T(8,128)S(1)}, u32[]{:S(2)}, u32[]{:S(2)}) collective-permute-start(f32[4,16,512]{2,1,0:T(8,128)S(1)} %get-tuple-element.27), channel_id=1, source_target_pairs={{0,1},{1,0},{2,3},{3,2},{4,5},{5,4},{6,7},{7,6},{8,9},{9,8},{10,11... | collective-permute-start | bytes 393224 | tf_op jit(solution)/shard_map/ppermute | solution.py:470
  13.1 7.5 %collective-permute-start.1 = (f32[4,16,512]{2,1,0:T(8,128)S(1)}, f32[4,16,512]{2,1,0:T(8,128)S(1)}, u32[]{:S(2)}, u32[]{:S(2)}) collective-permute-start(f32[4,16,512]{2,1,0:T(8,128)S(1)} %dynamic_update_slice.3), channel_id=1, source_target_pairs={{0,7},{1,2},{2,1},{3,4},{4,3},{5,6},{6,5},{7,0},{8,15},{9,10},{10,... | collective-permute-start | bytes 393224 | tf_op jit(solution)/shard_map/ppermute | solution.py:470
  20.7 2.7 %copy-start.16 = (f32[4,16,512]{2,1,0:T(8,128)}, f32[4,16,512]{2,1,0:T(8,128)S(1)}, u32[]{:S(2)}) copy-start(f32[4,16,512]{2,1,0:T(8,128)S(1)} %collective-permute-done.1.rg) | copy-start | bytes 393220
  25.9 17.8 %copy-start.22 = (s32[3,4096]{1,0:T(4,128)S(1)}, s32[3,4096]{1,0:T(4,128)}, u32[]{:S(2)}) copy-start(s32[3,4096]{1,0:T(4,128)} %rec_s.1) | copy-start | bytes 147460
  25.9 25.5 %copy-start.17 = (f32[4,16,512]{2,1,0:T(8,128)S(1)}, f32[4,16,512]{2,1,0:T(8,128)}, u32[]{:S(2)}) copy-start(f32[4,16,512]{2,1,0:T(8,128)} %copy-done.16) | copy-start | bytes 393220
  25.9 23.7 %collective-permute-start.2 = (f32[2,168,512]{2,1,0:T(8,128)}, f32[2,168,512]{2,1,0:T(8,128)S(1)}, u32[]{:S(2)}, u32[]{:S(2)}) collective-permute-start(f32[2,168,512]{2,1,0:T(8,128)} %get-tuple-element.36), channel_id=1, source_target_pairs={{0,8},{8,0},{16,24},{24,16},{32,40},{40,32},{48,56},{56,48},{64,72... | collective-permute-start | bytes 2064392 | tf_op jit(solution)/shard_map/ppermute | solution.py:470
  28.6 21.9 %collective-permute-start.3 = (f32[2,168,512]{2,1,0:T(8,128)}, f32[2,168,512]{2,1,0:T(8,128)S(1)}, u32[]{:S(2)}, u32[]{:S(2)}) collective-permute-start(f32[2,168,512]{2,1,0:T(8,128)} %get-tuple-element.37), channel_id=1, source_target_pairs={{8,16},{24,32},{40,48},{56,64},{72,80},{88,96},{104,112},{120,128}... | collective-permute-start | bytes 2064392 | tf_op jit(solution)/shard_map/ppermute | solution.py:475
  32.1 30.8 %all-to-all-start = ((f32[64,1,128]{2,1,0:T(1,128)}), f32[64,1,128]{2,1,0:T(1,128)S(1)}, u32[]{:S(2)}, u32[]{:S(2)}) async-start(f32[64,1,128]{2,1,0:T(1,128)} %bitcast.6), calls=%async_computation | async-start | bytes 65536 | tf_op jit(solution)/shard_map/all_to_all | solution.py:523
  49.6 0.9 %copy-start.12 = (f32[2,168,512]{2,1,0:T(8,128)}, f32[2,168,512]{2,1,0:T(8,128)S(1)}, u32[]{:S(2)}) copy-start(f32[2,168,512]{2,1,0:T(8,128)S(1)} %collective-permute-done.2.rc) | copy-start | bytes 2064388
  50.5 0.9 %copy-start.14 = (f32[2,168,512]{2,1,0:T(8,128)}, f32[2,168,512]{2,1,0:T(8,128)S(1)}, u32[]{:S(2)}) copy-start(f32[2,168,512]{2,1,0:T(8,128)S(1)} %collective-permute-done.3.rb) | copy-start | bytes 2064388
  52.0 1.1 %copy-start.13 = (f32[2,168,512]{2,1,0:T(8,128)S(1)}, f32[2,168,512]{2,1,0:T(8,128)}, u32[]{:S(2)}) copy-start(f32[2,168,512]{2,1,0:T(8,128)} %copy-done.12) | copy-start | bytes 2064388
  53.1 1.1 %copy-start.15 = (f32[2,168,512]{2,1,0:T(8,128)S(1)}, f32[2,168,512]{2,1,0:T(8,128)}, u32[]{:S(2)}) copy-start(f32[2,168,512]{2,1,0:T(8,128)} %copy-done.14) | copy-start | bytes 2064388
  54.2 0.8 %copy-start.29 = (f32[4,8,512]{2,1,0:T(8,128)S(1)}, f32[4,8,512]{2,1,0:T(8,128)}, u32[]{:S(2)}) copy-start(f32[4,8,512]{2,1,0:T(8,128)} %copy-done.28) | copy-start | bytes 196612
  55.1 0.8 %copy-start.31 = (f32[4,8,512]{2,1,0:T(8,128)S(1)}, f32[4,8,512]{2,1,0:T(8,128)}, u32[]{:S(2)}) copy-start(f32[4,8,512]{2,1,0:T(8,128)} %copy-done.30) | copy-start | bytes 196612
  55.9 0.8 %copy-start.33 = (f32[4,8,512]{2,1,0:T(8,128)S(1)}, f32[4,8,512]{2,1,0:T(8,128)}, u32[]{:S(2)}) copy-start(f32[4,8,512]{2,1,0:T(8,128)} %copy-done.32) | copy-start | bytes 196612
  56.7 0.8 %copy-start.35 = (f32[4,8,512]{2,1,0:T(8,128)S(1)}, f32[4,8,512]{2,1,0:T(8,128)}, u32[]{:S(2)}) copy-start(f32[4,8,512]{2,1,0:T(8,128)} %copy-done.34) | copy-start | bytes 196612
  60.6 0.9 %copy-start.10 = (f32[8,48,512]{2,1,0:T(8,128)}, f32[8,48,512]{2,1,0:T(8,128)S(1)}, u32[]{:S(2)}) copy-start(f32[8,48,512]{2,1,0:T(8,128)S(1)} %get-tuple-element.42.a0p) | copy-start | bytes 2359300
  63.5 1.1 %copy-start.11 = (f32[8,48,512]{2,1,0:T(8,128)S(1)}, f32[8,48,512]{2,1,0:T(8,128)}, u32[]{:S(2)}) copy-start(f32[8,48,512]{2,1,0:T(8,128)} %copy-done.10) | copy-start | bytes 2359300
  64.6 0.9 %copy-start.19 = (f32[4,32,512]{2,1,0:T(8,128)S(1)}, f32[4,32,512]{2,1,0:T(8,128)}, u32[]{:S(2)}) copy-start(f32[4,32,512]{2,1,0:T(8,128)} %copy-done.18) | copy-start | bytes 786436
  65.6 0.9 %copy-start.21 = (f32[4,32,512]{2,1,0:T(8,128)S(1)}, f32[4,32,512]{2,1,0:T(8,128)}, u32[]{:S(2)}) copy-start(f32[4,32,512]{2,1,0:T(8,128)} %copy-done.20) | copy-start | bytes 786436
  66.5 0.8 %copy-start.24 = (f32[64,1,128]{2,1,0:T(1,128)S(1)}, f32[64,1,128]{2,1,0:T(1,128)}, u32[]{:S(2)}) copy-start(f32[64,1,128]{2,1,0:T(1,128)} %copy-done.23) | copy-start | bytes 98308
  67.3 0.7 copy-start.26
  (12 other events, 7.9 us)

commit v3 on v2

--- a/solution.py
+++ b/solution.py
@@ -14,14 +14,15 @@
 DAMP = 0.3
 
 GZ = ("yl", "z", "c")
-GY = ("xh", "xl", "yh")
+GY = ("x", "yh")
 O = 8
 NZ_DEV, NY_DEV = 32, 8
 CZ, CY, NX = 4, 32, 512
 NZ, NY = NZ_DEV * CZ, NY_DEV * CY
 FR = CY + 2 * O
-VMEM_LIMIT = 16 * 1024 * 1024
+VMEM_LIMIT = 8 * 1024 * 1024
 ZROWS = 5 * CY + 8
+GROUP = 4
 
 
 def coefficient_table():
@@ -38,7 +39,7 @@
 
 
 def vmem():
-    return pl.BlockSpec(memory_space=pltpu.VMEM)
+    return pl.BlockSpec()
 
 
 def x_terms(u):
@@ -97,7 +98,7 @@
         for t in range(2):
             row[0:1, 32 * k + 16 * t : 32 * k + 16 * t + 16] = obs_v[t : t + 1, :]
     lane = lax.broadcasted_iota(jnp.int32, (1, 128), 1)
-    mine = jnp.where((lane >> 5) == meta[4] * 2 + meta[2], row[0:1, :], 0.0)
+    mine = jnp.where((lane >> 5) == meta[2], row[0:1, :], 0.0)
     own[...] = mine
 
     def pack(dst, high):
@@ -156,7 +157,7 @@
 
 
 def edge_step(
-    meta, coef, u, a, u1, a1, v, rh, rg, own, u0p, a0p, ulo, uhi, alo, ahi, zc, zb, traces,
+    meta, coef, u, a, u1, a1, v, rh, rg, own, u0p, a0p, ut, at, zc, zb, traces,
     pu, pa, pu1, pa1, pv,
 ):
     z0 = meta[0]
@@ -188,26 +189,30 @@
         i = z0 + l + 2
         up, dn, iu, ia = coef[0, i], coef[1, i], coef[2, i], coef[3, i]
         factors = depth_factors(l)
-        for side, uo, ao in ((0, ulo, alo), (1, uhi, ahi)):
+        for side in range(2):
             c = pv[side, l] * RATIO
             c = c * c
             p, lap = partial_laplace(pu.at[side], l, 0, 8, factors)
-            uo[l] = (2.0 * p - up * pu1[side, l] + c * lap) * iu
+            ut[side, l] = (2.0 * p - up * pu1[side, l] + c * lap) * iu
             q, lap = partial_laplace(pa.at[side], l, 0, 8, factors)
-            ao[l] = (2.0 * q - dn * pa1[side, l] + c * lap) * ia
+            at[side, l] = (2.0 * q - dn * pa1[side, l] + c * lap) * ia
         return carry
 
     lax.fori_loop(0, CZ, layer, 0)
+    ut[0, :, 0:2, :] = pu[0, :, 2:4, :]
+    ut[0, :, 6:8, :] = pv[0, :, 2:4, :]
+    ut[1, :, 6:8, :] = pu[1, :, 4:6, :]
+    ut[1, :, 0:2, :] = pv[1, :, 4:6, :]
 
     def pack(dst, l):
         m = slice(l, l + 2)
         dst[:, 0:CY, :] = u[m]
         dst[:, CY : 2 * CY, :] = a[m]
         dst[:, 4 * CY : 5 * CY, :] = v[m]
-        for b, p, lo, hi in ((2 * CY, u0p, ulo, uhi), (3 * CY, a0p, alo, ahi)):
+        for b, p, t in ((2 * CY, u0p, ut), (3 * CY, a0p, at)):
             dst[:, b : b + CY, :] = p[m]
-            dst[:, b : b + 2, :] = lo[m, 4:6, :]
-            dst[:, b + CY - 2 : b + CY, :] = hi[m, 2:4, :]
+            dst[:, b : b + 2, :] = t[0, m, 4:6, :]
+            dst[:, b + CY - 2 : b + CY, :] = t[1, m, 2:4, :]
         b = 5 * CY
         dst[:, b : b + 2, :] = pu[0, m, 2:4, :]
         dst[:, b + 2 : b + 4, :] = pu[1, m, 4:6, :]
@@ -224,38 +229,43 @@
         pack(zc, 0)
         pack(zb, 2)
 
-    mine = rg[0, 14:15, 0:128] + rg[0, 15:16, 0:128] + rh[0, 14:15, 0:128] + own[...]
+    mine = rh[0, 14:15, 0:128] + own[...]
     traces[...] = jnp.broadcast_to(mine, traces.shape)
 
 
-def list_receivers(meta, rec, rec_s, out, bits, words_v, words, sem):
+def list_receivers(meta, rec, out, bits, words_v, codes_v, words, codes, sem):
     z0, y0 = meta[0], meta[1]
     lz = rec[0:1, :] - z0
     ly = ((rec[1:2, :] - y0 + 16) & (NY - 1)) - 16
     own_z = (lz >= 0) & (lz < CZ)
     own_y = (ly >= 0) & (ly < CY)
     near = (lz >= -2) & (lz < CZ + 2) & (ly >= -2) & (ly < CY + 2) & (own_z | own_y)
+    own = jnp.where(own_z & own_y, 1 << 30, 0)
+    number = lax.broadcasted_iota(jnp.int32, lz.shape, 1)
+    codes_v[...] = number | (rec[2:3, :] << 12) | ((ly + 2) << 21) | ((lz + 2) << 27) | own
     m = near.astype(jnp.int32)
     for i in range(32):
         bits[i : i + 1, :] = m[:, 128 * i : 128 * i + 128] << i
     words_v[...] = jnp.sum(bits[...], axis=0, keepdims=True)
-    copy = pltpu.make_async_copy(words_v, words, sem)
-    copy.start()
-    copy.wait()
+    copies = [pltpu.make_async_copy(codes_v, codes, sem.at[0]), pltpu.make_async_copy(words_v, words, sem.at[1])]
+    for copy in copies:
+        copy.start()
+    for copy in copies:
+        copy.wait()
 
     def word_step(w, count):
         def bit_step(carry):
             word, count = carry
             low = word & (-word)
-            r = (31 - lax.clz(low)) * 128 + w
-            z = rec_s[0, r] - z0 + 2
-            y = (rec_s[1, r] - y0 + 2) & (NY - 1)
-            out[0, count + 1] = r | (rec_s[2, r] << 12) | (y << 21) | (z << 27)
+            out[0, count + 1] = codes[0, (31 - lax.clz(low)) * 128 + w]
             return word ^ low, count + 1
 
         return lax.while_loop(lambda carry: carry[0] != 0, bit_step, (words[0, w], count))[1]
 
-    out[0, 0] = lax.fori_loop(0, 128, word_step, 0)
+    count = lax.fori_loop(0, 128, word_step, 0)
+    out[0, 0] = count
+    for k in range(GROUP - 1):
+        out[0, count + 1 + k] = (2 << 21) | (2 << 27)
 
 
 def cell_place():
@@ -269,9 +279,9 @@
 
 
 def wave_step(
-    meta, coef, u, a, u1, v, rh, rg, u0p, a0p, ulo, uhi, alo, ahi, rc, rb, src, amp,
-    u2, u0o, w, gp, uf, u0f, a0f,
-    af, vf,
+    meta, coef, u, a, u1, v, u0p, a0p, ut, at, rc, rb, src, amp, found,
+    u2, u0o, w, gp, ep, a0f,
+    uf, u0f, af, vf,
 ):
     e = O + CY
     z0, y0 = meta[0], meta[1]
@@ -279,19 +289,13 @@
     vf[2:6, O:e, :] = v[...]
     u0f[2:6, O:e, :] = u0p[...]
     a0f[2:6, O:e, :] = a0p[...]
-    for f0, lo, hi in ((u0f, ulo, uhi), (a0f, alo, ahi)):
-        f0[2:6, O - 2 : O + 2, :] = lo[:, 2:6, :]
-        f0[2:6, e - 2 : e + 2, :] = hi[:, 2:6, :]
-
-    def low(r):
-        uf[2:6, O - 2 : O, :] = r[:, 2:4, :]
-        vf[2:6, O - 2 : O, :] = r[:, 12:14, :]
-
-    def high(r):
-        uf[2:6, e : e + 2, :] = r[:, 0:2, :]
-        vf[2:6, e : e + 2, :] = r[:, 12:14, :]
-
-    pick_y(meta, rh, rg, low, high)
+    for f0, t in ((u0f, ut), (a0f, at)):
+        f0[2:6, O - 2 : O + 2, :] = t[0, :, 2:6, :]
+        f0[2:6, e - 2 : e + 2, :] = t[1, :, 2:6, :]
+    uf[2:6, O - 2 : O, :] = ut[0, :, 0:2, :]
+    uf[2:6, e : e + 2, :] = ut[1, :, 6:8, :]
+    vf[2:6, O - 2 : O, :] = ut[0, :, 6:8, :]
+    vf[2:6, e : e + 2, :] = ut[1, :, 0:2, :]
 
     def fill_z(r, k):
         b = 5 * CY
@@ -359,7 +363,7 @@
 
     def layer(l, carry):
         i = z0 + l + 2
-        up, iu = coef[0, i], coef[2, i]
+        up, dn, iu = coef[0, i], coef[1, i], coef[2, i]
         for s in range(O, O + CY, 8):
             y = slice(s - O, s - O + 8)
             vel = v[l, y, :]
@@ -372,7 +376,9 @@
             u0o[l, y, :] = q
             slow = 2.0 / vel
             w[l, y, :] = slow * (un - 2.0 * q + new)
-            gp[l, y, :] = slow * a[l, y, :] * (u1[l, y, :] - 2.0 * un + q)
+            an = a[l, y, :]
+            gp[l, y, :] = slow * an * (u1[l, y, :] - 2.0 * un + q)
+            ep[l, y, :] = -dn * an
         return carry
 
     lax.fori_loop(0, CZ, layer, 0)
@@ -393,60 +399,68 @@
 
     lax.fori_loop(0, src.shape[1], add_source_1, 0)
 
-
-def adjoint_step(meta, coef, a, v, uf, u0f, a0p, w, gp, found, table, a2, a0o, grad, a0f):
-    z0, yh, xl = meta[0], meta[2], meta[4]
+    def sample(code, valid, own):
+        _, framed, inner, hit, z = receiver(code, place)
+        a0f[framed] = a0f[framed] + jnp.where(hit, uf[framed] * (coef[3, z0 + z] * valid), 0.0)
+        ep[inner] = ep[inner] + jnp.where(hit, u0f[framed] * own, 0.0)
+
+    each_receiver(found, place, sample)
+
+
+def receiver(code, place):
+    r, x, y, z = code & 4095, (code >> 12) & 511, (code >> 21) & 63, (code >> 27) & 7
+    framed, hit = cell_at(place, z, y + (O - 2), x)
+    own, _ = cell_at(place, jnp.clip(z - 2, 0, CZ - 1), jnp.clip(y - 2, 0, CY - 1), x)
+    return r, framed, own, hit, z
+
+
+def each_receiver(found, place, one):
+    count = found[0, 0]
+
+    def group(b, carry):
+        for k in range(GROUP):
+            n = b * GROUP + k
+            code = found[0, n + 1]
+            valid = jnp.where(n < count, jnp.float32(1.0), jnp.float32(0.0))
+            one(code, valid, jnp.where(code >= 1 << 30, valid, jnp.float32(0.0)))
+        return carry
+
+    lax.fori_loop(0, (count + GROUP - 1) // GROUP, group, 0)
+
+
+def adjoint_step(meta, coef, v, a0p, w, gp, ep, found, table, a2, a0o, grad, a0f, ef):
+    z0 = meta[0]
     for k in range(8):
         a0f[k] = a0p[k]
+    for l in range(CZ):
+        ef[l] = ep[l]
     place = cell_place()
-    turn = 1 - 2 * yh
-
-    def observed(step, r):
-        x = (r >> 5) & 3
-        sender = (x + turn * ((x ^ xl) & 1)) & 3
-        return table[(r >> 7) * 2 + (sender >> 1), ((x & 1) * 2 + ((r >> 4) & 1)) * 32 + step * 16 + (r & 15)]
-
-    def add_receiver_0(n, carry):
-        code = found[0, n + 1]
-        r, x, y, z = code & 4095, (code >> 12) & 511, (code >> 21) & 63, code >> 27
-        at, hit = cell_at(place, z, y + (O - 2), x)
-        residual = (uf[at] - observed(0, r)) * coef[3, z0 + z]
-        a0f[at] = a0f[at] + jnp.where(hit, residual, 0.0)
-        return carry
-
-    count = found[0, 0]
-    lax.fori_loop(0, count, add_receiver_0, 0)
+
+    def subtract(code, valid, own):
+        r, framed, inner, hit, z = receiver(code, place)
+        col = ((r >> 4) & 1) * 32 + (r & 15)
+        first = table[r >> 5, col] * (coef[3, z0 + z] * valid)
+        second = table[r >> 5, col + 16] * own
+        a0f[framed] = a0f[framed] - jnp.where(hit, first, 0.0)
+        ef[inner] = ef[inner] - jnp.where(hit, second, 0.0)
+
+    each_receiver(found, place, subtract)
 
     def layer(l, carry):
         i = z0 + l + 2
-        dn, ia = coef[1, i], coef[3, i]
+        ia = coef[3, i]
         for s in range(O, O + CY, 8):
             y = slice(s - O, s - O + 8)
             c = v[l, y, :] * RATIO
             c = c * c
             q, lap = laplace(a0f, l + 2, s)
-            a2[l, y, :] = (2.0 * q - dn * a[l, y, :] + c * lap) * ia
+            a2[l, y, :] = (2.0 * q + ef[l, y, :] + c * lap) * ia
             a0o[l, y, :] = q
             grad[l, y, :] = gp[l, y, :] + w[l, y, :] * q
         return carry
 
     lax.fori_loop(0, CZ, layer, 0)
 
-    def add_receiver_1(n, carry):
-        code = found[0, n + 1]
-        r, x, y, z = code & 4095, (code >> 12) & 511, ((code >> 21) & 63) - 2, (code >> 27) - 2
-
-        @pl.when((z >= 0) & (z < CZ) & (y >= 0) & (y < CY))
-        def _():
-            at, hit = cell_at(place, z, y, x)
-            before, _ = cell_at(place, z + 2, y + O, x)
-            residual = (u0f[before] - observed(1, r)) * coef[3, z0 + z + 2]
-            a2[at] = a2[at] + jnp.where(hit, residual, 0.0)
-
-        return carry
-
-    lax.fori_loop(0, count, add_receiver_1, 0)
-
 
 def f32(*shape):
     return jax.ShapeDtypeStruct(shape, jnp.float32)
@@ -454,7 +468,7 @@
 
 def call(kernel, out_shape, in_specs, scratch_shapes=()):
     many = isinstance(out_shape, tuple)
-    return pl.pallas_call(
+    made = pl.pallas_call(
         kernel,
         out_shape=out_shape,
         in_specs=in_specs,
@@ -464,6 +478,13 @@
         name=kernel.__name__,
     )
 
+    def run(*args):
+        if kernel is pack_y:
+            args = args[:1] + tuple(pltpu.with_memory_space_constraint(x, pltpu.HBM) for x in args[1:])
+        return made(*args)
+
+    return run
+
 
 def swap(value, axis, size, first):
     pairs = [(i, (first + ((i - first) % size ^ 1)) % size) for i in range(size)]
@@ -478,10 +499,10 @@
 def shards(u, u1, a, a1, v, obs, rec, src, amp):
     assert u.shape == (CZ, CY, NX)
     gz, gy = lax.axis_index(GZ), lax.axis_index(GY)
-    meta = [gz * CZ, gy * CY, lax.axis_index("yh"), lax.axis_index("c"), lax.axis_index("xl")]
+    meta = [gz * CZ, gy * CY, lax.axis_index("yh"), lax.axis_index("c")]
     meta = jnp.stack(meta).astype(jnp.int32)
     coef = jnp.asarray(coefficient_table())
-    block, edge = f32(CZ, CY, NX), f32(CZ, 8, NX)
+    block, edge = f32(CZ, CY, NX), f32(2, CZ, 8, NX)
     frame, zpack = f32(8, FR, NX), f32(2, ZROWS, NX)
     part = pltpu.VMEM((2, CZ, 8, NX), jnp.float32)
     full = pltpu.VMEM((8, FR, NX), jnp.float32)
@@ -494,7 +515,6 @@
         + [pltpu.VMEM((2, 16), jnp.float32), pltpu.VMEM((1, 128), jnp.float32), pltpu.SemaphoreType.DMA((11,))],
     )(meta, u, a, u1, a1, v, obs)
     rh = swap(h, GY, NY_DEV, 0)
-    g = lax.dynamic_update_slice(g, rh[0:1, 14:15, :], (0, 15, 0))
     rg = swap(g, GY, NY_DEV, 1)
 
     u0p, a0p = call(own_step, (block, block), [smem()] * 2 + [vmem()] * 5)(meta, coef, u, a, u1, a1, v)
@@ -502,44 +522,46 @@
     found = call(
         list_receivers,
         jax.ShapeDtypeStruct((1, rec.shape[1] + 128), jnp.int32),
-        [smem(), vmem(), smem()],
+        [smem(), vmem()],
         [
             pltpu.VMEM((32, 128), jnp.int32),
             pltpu.VMEM((1, 128), jnp.int32),
+            pltpu.VMEM(rec[:1].shape, jnp.int32),
             pltpu.SMEM((1, 128), jnp.int32),
-            pltpu.SemaphoreType.DMA,
+            pltpu.SMEM(rec[:1].shape, jnp.int32),
+            pltpu.SemaphoreType.DMA((2,)),
         ],
-    )(meta, rec, rec)
-
-    ulo, uhi, alo, ahi, zc, zb, traces = call(
+    )(meta, rec)
+
+    ut, at, zc, zb, traces = call(
         edge_step,
-        (edge,) * 4 + (zpack, zpack, f32(64, 128)),
+        (edge,) * 2 + (zpack, zpack, f32(128, 128)),
         [smem()] * 2 + [vmem()] * 10,
         [part] * 5,
     )(meta, coef, u, a, u1, a1, v, rh, rg, own, u0p, a0p)
 
     rc = swap(zc, GZ, NZ_DEV, 0)
     rb = swap_open(zb, GZ, NZ_DEV)
-    table = lax.all_to_all(traces, ("yl", "z", "c", "xh"), 0, 0, tiled=True)
-
-    u2, u0, w, gp, uf, u0f, a0f = call(
+    table = lax.all_to_all(traces, GZ + ("x",), 0, 0, tiled=True)
+
+    u2, u0, w, gp, ep, a0f = call(
         wave_step,
-        (block,) * 4 + (frame,) * 3,
-        [smem()] * 2 + [vmem()] * 14 + [smem()] * 2,
-        [full] * 2,
-    )(meta, coef, u, a, u1, v, rh, rg, u0p, a0p, ulo, uhi, alo, ahi, rc, rb, src, amp)
+        (block,) * 5 + (frame,),
+        [smem()] * 2 + [vmem()] * 10 + [smem()] * 3,
+        [full] * 4,
+    )(meta, coef, u, a, u1, v, u0p, a0p, ut, at, rc, rb, src, amp, found)
 
     a2, a0, grad = call(
         adjoint_step,
         (block,) * 3,
-        [smem()] * 2 + [vmem()] * 7 + [smem()] * 2,
-        [full],
-    )(meta, coef, a, v, uf, u0f, a0f, w, gp, found, table)
+        [smem()] * 2 + [vmem()] * 5 + [smem()] * 2,
+        [full, pltpu.VMEM((CZ, CY, NX), jnp.float32)],
+    )(meta, coef, v, a0f, w, gp, ep, found, table)
     return u2, u0, a2, a0, grad
 
 
 def solution(mesh):
-    fine = Mesh(mesh.devices.reshape(2, 8, 2, 2, 2, 2), ("yl", "z", "c", "xh", "xl", "yh"))
+    fine = Mesh(mesh.devices.reshape(2, 8, 2, 4, 2), ("yl", "z", "c", "x", "yh"))
     field = P(GZ, GY, None)
     return jax.shard_map(
         shards,

time: 74.2 us -> 53.2 us (0.72)
  the two profiles are of different devices: /device:TPU:23 before, /device:TPU:1 now
where the time goes in v3:
time: 53.2 us; the launch traced here: 52.6 us
  starting transfers between devices  22.2 us (42%)
  Pallas kernels  18.4 us (35%)
  local copies, waits for them, and re-layouts  7.52 us (14%)
  waiting for transfers between devices  3.57 us (7%)
  between operations  0.79 us (1%)
    pallas_call x6, Pallas kernels, run(): return made(*args)  18.4 us
    all_to_all x1, starting transfers between devices, shards(): table = lax.all_to_all(traces, GZ + ('x',), 0, 0, tiled=True)  10.5 us
    ppermute x3, starting transfers between devices, swap(): return lax.ppermute(value, axis, pairs)  8.3 us
    unnamed x34, local copies, waits for them, and re-layouts  7.52 us
    ppermute x3, waiting for transfers between devices, swap(): return lax.ppermute(value, axis, pairs)  3.56 us
    ppermute x1, starting transfers between devices, swap_open(): return lax.ppermute(value, axis, pairs + [(j, i) for i, j in pairs])  3.42 us
  transfers between devices with their start and end apart: 5, of which 1 were waited for; matrix products, arithmetic and copies ran while one was open for 0% of the time, Pallas kernels for 18%

profile of v3, /device:TPU:1, one launch (start us, length us, event | category | flops | bytes accessed | tf_op | source)
XLA Modules:
  0.0 52.6 jit_solution(13934677459392715105)
XLA Ops:
  0.6 0.1 pad_add_fusion.meta
  0.7 0.0 copy-start.4
  0.7 0.0 copy-start.13
  0.8 1.8 %pack_y.1 = (f32[4,16,512]{2,1,0:T(8,128)S(1)}, f32[4,16,512]{2,1,0:T(8,128)S(1)}, f32[1,128]{1,0:T(1,128)S(1)}) custom-call(s32[4]{0:T(128)S(1)} %pad_add_fusion.meta, f32[4,32,512]{2,1,0:T(8,128)} %u.7, f32[4,32,512]{2,1,0:T(8,128)} %a.7, f32[4,32,512]{2,1,0:T(8,128)} %u1_.7, f32[4,32,512]{2,1,0:T(8,128)} %a1.5, f32[4,32,512]{2,1,0:T(8,128)} %v.9, f32[2,16]{1,0:T(2,128)} %obs.1), custom_call_target="tpu_custom_call" | custom-call | tf_op jit(solution)/shard_map/pack_y/pallas_call | solution.py:484
  2.6 3.9 %collective-permute-start = (f32[4,16,512]{2,1,0:T(8,128)S(1)}, f32[4,16,512]{2,1,0:T(8,128)S(1)}, u32[]{:S(2)}, u32[]{:S(2)}) collective-permute-start(f32[4,16,512]{2,1,0:T(8,128)S(1)} %get-tuple-element.26), channel_id=1, source_target_pairs={{0,1},{1,0},{2,3},{3,2},{4,5},{5,4},{6,7},{7,6},{8,9},{9,8},{10,11... | collective-permute-start | bytes 393224 | tf_op jit(solution)/shard_map/ppermute | solution.py:491
  6.5 2.3 %collective-permute-start.1 = (f32[4,16,512]{2,1,0:T(8,128)S(1)}, f32[4,16,512]{2,1,0:T(8,128)S(1)}, u32[]{:S(2)}, u32[]{:S(2)}) collective-permute-start(f32[4,16,512]{2,1,0:T(8,128)S(1)} %get-tuple-element.27), channel_id=1, source_target_pairs={{0,7},{1,2},{2,1},{3,4},{4,3},{5,6},{6,5},{7,0},{8,15},{9,10},{10,... | collective-permute-start | bytes 393224 | tf_op jit(solution)/shard_map/ppermute | solution.py:491
  8.8 0.0 copy-done.1
  8.8 0.0 copy-done.3
  8.8 1.5 %own_step.1 = (f32[4,32,512]{2,1,0:T(8,128)S(1)}, f32[4,32,512]{2,1,0:T(8,128)S(1)}) custom-call(s32[4]{0:T(128)S(1)} %pad_add_fusion.meta, f32[4,132]{1,0:T(4,128)S(1)} %copy-done.13, f32[4,32,512]{2,1,0:T(8,128)S(1)} %copy-done.1, f32[4,32,512]{2,1,0:T(8,128)S(1)} %copy-done.2, f32[4,32,512]{2,1,0:T(8,128)S(1)} %copy-done.3, f32[4,32,512]{2,1,0:T(8,128)S(1)} %copy-done.4, ...), custom_call_target="tpu_custom_call" | custom-call | tf_op jit(solution)/shard_map/own_step/pallas_call | solution.py:484
  10.4 0.0 collective-permute-done.rh
  10.4 3.6 %collective-permute-done.1.rg = f32[4,16,512]{2,1,0:T(8,128)S(1)} collective-permute-done((f32[4,16,512]{2,1,0:T(8,128)S(1)}, f32[4,16,512]{2,1,0:T(8,128)S(1)}, u32[]{:S(2)}, u32[]{:S(2)}) %collective-permute-start.1) | collective-permute-done | bytes 131104 | tf_op jit(solution)/shard_map/ppermute | solution.py:491
  13.9 2.6 %edge_step.1 = (f32[2,4,8,512]{3,2,1,0:T(8,128)S(1)}, f32[2,4,8,512]{3,2,1,0:T(8,128)S(1)}, f32[2,168,512]{2,1,0:T(8,128)}, f32[2,168,512]{2,1,0:T(8,128)}, f32[128,128]{1,0:T(8,128)}) custom-call(s32[4]{0:T(128)S(1)} %pad_add_fusion.meta, f32[4,132]{1,0:T(4,128)S(1)} %copy-done.13, f32[4,32,512]{2,1,0:T(8,128)S(1)} %copy-done.1, ...), custom_call_target="tpu_custom_call" | custom-call | tf_op jit(solution)/shard_map/edge_step/pallas_call | solution.py:484
  16.6 0.7 %copy-done.11 = f32[2,4,8,512]{3,2,1,0:T(8,128)} copy-done((f32[2,4,8,512]{3,2,1,0:T(8,128)}, f32[2,4,8,512]{3,2,1,0:T(8,128)S(1)}, u32[]{:S(2)}) %copy-start.11) | copy-done | bytes 131096
  17.2 2.1 %collective-permute-start.2 = (f32[2,168,512]{2,1,0:T(8,128)}, f32[2,168,512]{2,1,0:T(8,128)S(1)}, u32[]{:S(2)}, u32[]{:S(2)}) collective-permute-start(f32[2,168,512]{2,1,0:T(8,128)} %get-tuple-element.31), channel_id=1, source_target_pairs={{0,8},{8,0},{16,24},{24,16},{32,40},{40,32},{48,56},{56,48},{64,72... | collective-permute-start | bytes 2064392 | tf_op jit(solution)/shard_map/ppermute | solution.py:491
  19.4 3.4 %collective-permute-start.3 = (f32[2,168,512]{2,1,0:T(8,128)}, f32[2,168,512]{2,1,0:T(8,128)S(1)}, u32[]{:S(2)}, u32[]{:S(2)}) collective-permute-start(f32[2,168,512]{2,1,0:T(8,128)} %get-tuple-element.32), channel_id=1, source_target_pairs={{8,16},{24,32},{40,48},{56,64},{72,80},{88,96},{104,112},{120,128}... | collective-permute-start | bytes 2064392 | tf_op jit(solution)/shard_map/ppermute | solution.py:496
  22.8 0.0 copy-start.14
  22.8 10.5 %all-to-all-start = ((f32[128,1,128]{2,1,0:T(1,128)}), f32[128,1,128]{2,1,0:T(1,128)S(1)}, u32[]{:S(2)}, u32[]{:S(2)}) async-start(f32[128,1,128]{2,1,0:T(1,128)} %bitcast.5), calls=%async_computation | async-start | bytes 131072 | tf_op jit(solution)/shard_map/all_to_all | solution.py:545
  33.3 4.3 %list_receivers.1.found = s32[1,4224]{1,0:T(1,128)S(1)} custom-call(s32[4]{0:T(128)S(1)} %pad_add_fusion.meta, s32[3,4096]{1,0:T(4,128)S(1)} %copy-done.14), custom_call_target="tpu_custom_call" | custom-call | tf_op jit(solution)/shard_map/list_receivers/pallas_call | solution.py:484
  37.6 0.0 copy-start.15
  37.6 0.0 collective-permute-done.2.rc
  37.6 0.0 collective-permute-done.3.rb
  37.6 0.8 %copy-done.5 = f32[2,168,512]{2,1,0:T(8,128)} copy-done((f32[2,168,512]{2,1,0:T(8,128)}, f32[2,168,512]{2,1,0:T(8,128)S(1)}, u32[]{:S(2)}) %copy-start.5) | copy-done | bytes 688152
  38.5 0.7 %copy-done.16 = f32[2,4]{1,0:T(2,128)S(1)} copy-done((f32[2,4]{1,0:T(2,128)S(1)}, f32[2,4]{1,0:T(2,128)}, u32[]{:S(2)}) %copy-start.16) | copy-done | bytes 56
  39.2 1.1 %copy-done.6 = f32[2,168,512]{2,1,0:T(8,128)S(1)} copy-done((f32[2,168,512]{2,1,0:T(8,128)S(1)}, f32[2,168,512]{2,1,0:T(8,128)}, u32[]{:S(2)}) %copy-start.6) | copy-done | bytes 688152
  40.3 0.9 %copy-done.12 = f32[2,4,8,512]{3,2,1,0:T(8,128)S(1)} copy-done((f32[2,4,8,512]{3,2,1,0:T(8,128)S(1)}, f32[2,4,8,512]{3,2,1,0:T(8,128)}, u32[]{:S(2)}) %copy-start.12) | copy-done | bytes 131096
  41.2 3.9 %wave_step.1 = (f32[4,32,512]{2,1,0:T(8,128)}, f32[4,32,512]{2,1,0:T(8,128)}, f32[4,32,512]{2,1,0:T(8,128)S(1)}, f32[4,32,512]{2,1,0:T(8,128)S(1)}, f32[4,32,512...) custom-call(s32[4]{0:T(128)S(1)} %pad_add_fusion.meta, f32[4,132]{1,0:T(4,128)S(1)} %copy-done.13, f32[4,32,512]{2,1,0:T(8,128)S(1)} %copy-done.1, ...), custom_call_target="tpu_custom_call" | custom-call | tf_op jit(solution)/shard_map/wave_step/pallas_call | solution.py:484
  45.0 0.7 %copy-done.7 = f32[4,32,512]{2,1,0:T(8,128)} copy-done((f32[4,32,512]{2,1,0:T(8,128)}, f32[4,32,512]{2,1,0:T(8,128)S(1)}, u32[]{:S(2)}) %copy-start.7) | copy-done | bytes 262168
  45.7 0.7 %copy-done.9 = f32[4,32,512]{2,1,0:T(8,128)} copy-done((f32[4,32,512]{2,1,0:T(8,128)}, f32[4,32,512]{2,1,0:T(8,128)S(1)}, u32[]{:S(2)}) %copy-start.9) | copy-done | bytes 262168
  46.4 0.0 all-to-all-done
  46.4 0.9 %copy-done.8 = f32[4,32,512]{2,1,0:T(8,128)S(1)} copy-done((f32[4,32,512]{2,1,0:T(8,128)S(1)}, f32[4,32,512]{2,1,0:T(8,128)}, u32[]{:S(2)}) %copy-start.8) | copy-done | bytes 262168
  47.4 0.9 %copy-done.10 = f32[4,32,512]{2,1,0:T(8,128)S(1)} copy-done((f32[4,32,512]{2,1,0:T(8,128)S(1)}, f32[4,32,512]{2,1,0:T(8,128)}, u32[]{:S(2)}) %copy-start.10) | copy-done | bytes 262168
  48.3 4.3 %adjoint_step.1 = (f32[4,32,512]{2,1,0:T(8,128)}, f32[4,32,512]{2,1,0:T(8,128)}, f32[4,32,512]{2,1,0:T(8,128)}) custom-call(s32[4]{0:T(128)S(1)} %pad_add_fusion.meta, f32[4,132]{1,0:T(4,128)S(1)} %copy-done.13, f32[4,32,512]{2,1,0:T(8,128)S(1)} %copy-done, f32[8,48,512]{2,1,0:T(8,128)S(1)} %get-tuple-element.35.a0p, f32[4,32,512]{2,1,0:T(8,128)S(1)} %get-tuple-element.36.w, ...), custom_call_target="tpu_custom_call" | custom-call | tf_op jit(solution)/shard_map/adjoint_step/pallas_call | solution.py:484
  (19 shorter events, 0.0 us)
Async XLA Ops:
  0.7 8.1 %copy-start = (f32[4,32,512]{2,1,0:T(8,128)S(1)}, f32[4,32,512]{2,1,0:T(8,128)}, u32[]{:S(2)}) copy-start(f32[4,32,512]{2,1,0:T(8,128)} %v.9) | copy-start | bytes 786436
  0.7 8.1 %copy-start.1 = (f32[4,32,512]{2,1,0:T(8,128)S(1)}, f32[4,32,512]{2,1,0:T(8,128)}, u32[]{:S(2)}) copy-start(f32[4,32,512]{2,1,0:T(8,128)} %u.7) | copy-start | bytes 786436
  0.7 8.1 %copy-start.2 = (f32[4,32,512]{2,1,0:T(8,128)S(1)}, f32[4,32,512]{2,1,0:T(8,128)}, u32[]{:S(2)}) copy-start(f32[4,32,512]{2,1,0:T(8,128)} %a.7) | copy-start | bytes 786436
  0.7 8.1 %copy-start.3 = (f32[4,32,512]{2,1,0:T(8,128)S(1)}, f32[4,32,512]{2,1,0:T(8,128)}, u32[]{:S(2)}) copy-start(f32[4,32,512]{2,1,0:T(8,128)} %u1_.7) | copy-start | bytes 786436
  0.7 8.1 %copy-start.4 = (f32[4,32,512]{2,1,0:T(8,128)S(1)}, f32[4,32,512]{2,1,0:T(8,128)}, u32[]{:S(2)}) copy-start(f32[4,32,512]{2,1,0:T(8,128)} %a1.5) | copy-start | bytes 786436
  0.7 8.1 %copy-start.13 = (f32[4,132]{1,0:T(4,128)S(1)}, f32[4,132]{1,0:T(4,128)}, u32[]{:S(2)}) copy-start(f32[4,132]{1,0:T(4,128)} %constant.29.clone.coef) | copy-start | bytes 6340
  2.6 7.8 %collective-permute-start = (f32[4,16,512]{2,1,0:T(8,128)S(1)}, f32[4,16,512]{2,1,0:T(8,128)S(1)}, u32[]{:S(2)}, u32[]{:S(2)}) collective-permute-start(f32[4,16,512]{2,1,0:T(8,128)S(1)} %get-tuple-element.26), channel_id=1, source_target_pairs={{0,1},{1,0},{2,3},{3,2},{4,5},{5,4},{6,7},{7,6},{8,9},{9,8},{10,11... | collective-permute-start | bytes 393224 | tf_op jit(solution)/shard_map/ppermute | solution.py:491
  6.5 7.4 %collective-permute-start.1 = (f32[4,16,512]{2,1,0:T(8,128)S(1)}, f32[4,16,512]{2,1,0:T(8,128)S(1)}, u32[]{:S(2)}, u32[]{:S(2)}) collective-permute-start(f32[4,16,512]{2,1,0:T(8,128)S(1)} %get-tuple-element.27), channel_id=1, source_target_pairs={{0,7},{1,2},{2,1},{3,4},{4,3},{5,6},{6,5},{7,0},{8,15},{9,10},{10,... | collective-permute-start | bytes 393224 | tf_op jit(solution)/shard_map/ppermute | solution.py:491
  16.6 0.7 %copy-start.11 = (f32[2,4,8,512]{3,2,1,0:T(8,128)}, f32[2,4,8,512]{3,2,1,0:T(8,128)S(1)}, u32[]{:S(2)}) copy-start(f32[2,4,8,512]{3,2,1,0:T(8,128)S(1)} %get-tuple-element.30.at) | copy-start | bytes 393220
  17.2 20.4 %collective-permute-start.2 = (f32[2,168,512]{2,1,0:T(8,128)}, f32[2,168,512]{2,1,0:T(8,128)S(1)}, u32[]{:S(2)}, u32[]{:S(2)}) collective-permute-start(f32[2,168,512]{2,1,0:T(8,128)} %get-tuple-element.31), channel_id=1, source_target_pairs={{0,8},{8,0},{16,24},{24,16},{32,40},{40,32},{48,56},{56,48},{64,72... | collective-permute-start | bytes 2064392 | tf_op jit(solution)/shard_map/ppermute | solution.py:491
  19.4 18.3 %collective-permute-start.3 = (f32[2,168,512]{2,1,0:T(8,128)}, f32[2,168,512]{2,1,0:T(8,128)S(1)}, u32[]{:S(2)}, u32[]{:S(2)}) collective-permute-start(f32[2,168,512]{2,1,0:T(8,128)} %get-tuple-element.32), channel_id=1, source_target_pairs={{8,16},{24,32},{40,48},{56,64},{72,80},{88,96},{104,112},{120,128}... | collective-permute-start | bytes 2064392 | tf_op jit(solution)/shard_map/ppermute | solution.py:496
  22.8 10.5 %copy-start.14 = (s32[3,4096]{1,0:T(4,128)S(1)}, s32[3,4096]{1,0:T(4,128)}, u32[]{:S(2)}) copy-start(s32[3,4096]{1,0:T(4,128)} %rec.1) | copy-start | bytes 147460
  22.8 23.6 %all-to-all-start = ((f32[128,1,128]{2,1,0:T(1,128)}), f32[128,1,128]{2,1,0:T(1,128)S(1)}, u32[]{:S(2)}, u32[]{:S(2)}) async-start(f32[128,1,128]{2,1,0:T(1,128)} %bitcast.5), calls=%async_computation | async-start | bytes 131072 | tf_op jit(solution)/shard_map/all_to_all | solution.py:545
  37.6 0.9 %copy-start.15 = (s32[3,4]{1,0:T(4,128)S(1)}, s32[3,4]{1,0:T(4,128)}, u32[]{:S(2)}) copy-start(s32[3,4]{1,0:T(4,128)} %src.1) | copy-start | bytes 148
  37.6 0.8 %copy-start.5 = (f32[2,168,512]{2,1,0:T(8,128)}, f32[2,168,512]{2,1,0:T(8,128)S(1)}, u32[]{:S(2)}) copy-start(f32[2,168,512]{2,1,0:T(8,128)S(1)} %collective-permute-done.3.rb) | copy-start | bytes 2064388
  38.5 0.7 %copy-start.16 = (f32[2,4]{1,0:T(2,128)S(1)}, f32[2,4]{1,0:T(2,128)}, u32[]{:S(2)}) copy-start(f32[2,4]{1,0:T(2,128)} %amp.1) | copy-start | bytes 100
  39.2 1.1 %copy-start.6 = (f32[2,168,512]{2,1,0:T(8,128)S(1)}, f32[2,168,512]{2,1,0:T(8,128)}, u32[]{:S(2)}) copy-start(f32[2,168,512]{2,1,0:T(8,128)} %copy-done.5) | copy-start | bytes 2064388
  40.3 0.9 %copy-start.12 = (f32[2,4,8,512]{3,2,1,0:T(8,128)S(1)}, f32[2,4,8,512]{3,2,1,0:T(8,128)}, u32[]{:S(2)}) copy-start(f32[2,4,8,512]{3,2,1,0:T(8,128)} %copy-done.11) | copy-start | bytes 393220
  45.0 0.7 %copy-start.7 = (f32[4,32,512]{2,1,0:T(8,128)}, f32[4,32,512]{2,1,0:T(8,128)S(1)}, u32[]{:S(2)}) copy-start(f32[4,32,512]{2,1,0:T(8,128)S(1)} %get-tuple-element.37.gp) | copy-start | bytes 786436
  45.7 0.7 %copy-start.9 = (f32[4,32,512]{2,1,0:T(8,128)}, f32[4,32,512]{2,1,0:T(8,128)S(1)}, u32[]{:S(2)}) copy-start(f32[4,32,512]{2,1,0:T(8,128)S(1)} %get-tuple-element.38.ep) | copy-start | bytes 786436
  46.4 1.0 %copy-start.8 = (f32[4,32,512]{2,1,0:T(8,128)S(1)}, f32[4,32,512]{2,1,0:T(8,128)}, u32[]{:S(2)}) copy-start(f32[4,32,512]{2,1,0:T(8,128)} %copy-done.7) | copy-start | bytes 786436
  47.4 0.9 %copy-start.10 = (f32[4,32,512]{2,1,0:T(8,128)S(1)}, f32[4,32,512]{2,1,0:T(8,128)}, u32[]{:S(2)}) copy-start(f32[4,32,512]{2,1,0:T(8,128)} %copy-done.9) | copy-start | bytes 786436

commit v4 on v3

--- a/solution.py
+++ b/solution.py
@@ -466,9 +466,13 @@
     return jax.ShapeDtypeStruct(shape, jnp.float32)
 
 
+def hbm(*args):
+    return tuple(pltpu.with_memory_space_constraint(x, pltpu.HBM) for x in args)
+
+
 def call(kernel, out_shape, in_specs, scratch_shapes=()):
     many = isinstance(out_shape, tuple)
-    made = pl.pallas_call(
+    return pl.pallas_call(
         kernel,
         out_shape=out_shape,
         in_specs=in_specs,
@@ -477,13 +481,6 @@
         compiler_params=pltpu.CompilerParams(vmem_limit_bytes=VMEM_LIMIT),
         name=kernel.__name__,
     )
-
-    def run(*args):
-        if kernel is pack_y:
-            args = args[:1] + tuple(pltpu.with_memory_space_constraint(x, pltpu.HBM) for x in args[1:])
-        return made(*args)
-
-    return run
 
 
 def swap(value, axis, size, first):
@@ -513,7 +510,7 @@
         [smem()] + [pl.BlockSpec(memory_space=pltpu.HBM)] * 6,
         [pltpu.VMEM((5, CZ, 8, NX), jnp.float32)] * 2
         + [pltpu.VMEM((2, 16), jnp.float32), pltpu.VMEM((1, 128), jnp.float32), pltpu.SemaphoreType.DMA((11,))],
-    )(meta, u, a, u1, a1, v, obs)
+    )(meta, *hbm(u, a, u1, a1, v, obs))
     rh = swap(h, GY, NY_DEV, 0)
     rg = swap(g, GY, NY_DEV, 1)
 
@@ -533,6 +530,7 @@
         ],
     )(meta, rec)
 
+    rg, found = lax.optimization_barrier((rg, found))
     ut, at, zc, zb, traces = call(
         edge_step,
         (edge,) * 2 + (zpack, zpack, f32(128, 128)),
@@ -546,17 +544,17 @@
 
     u2, u0, w, gp, ep, a0f = call(
         wave_step,
-        (block,) * 5 + (frame,),
+        (block,) * 2 + (pltpu.HBM(block.shape, block.dtype),) * 3 + (frame,),
         [smem()] * 2 + [vmem()] * 10 + [smem()] * 3,
         [full] * 4,
-    )(meta, coef, u, a, u1, v, u0p, a0p, ut, at, rc, rb, src, amp, found)
+    )(meta, coef, *hbm(u, a, u1, v), u0p, a0p, ut, at, rc, rb, src, amp, found)
 
     a2, a0, grad = call(
         adjoint_step,
         (block,) * 3,
         [smem()] * 2 + [vmem()] * 5 + [smem()] * 2,
         [full, pltpu.VMEM((CZ, CY, NX), jnp.float32)],
-    )(meta, coef, v, a0f, w, gp, ep, found, table)
+    )(meta, coef, *hbm(v), a0f, *hbm(w, gp, ep), found, table)
     return u2, u0, a2, a0, grad
 
 

time: 53.2 us -> 48.1 us (0.904)
  local copies, waits for them, and re-layouts: 7.52 us -> 0.71 us
  waiting for transfers between devices: 3.57 us -> 7.27 us
  starting transfers between devices: 22.2 us -> 20 us
  Pallas kernels: 18.4 us -> 19 us
    unnamed x34 -> x18, local copies, waits for them, and re-layouts: 7.52 us -> 0.71 us
    all_to_all x1, waiting for transfers between devices: 0.01 us -> 5.13 us  [shards(): table = lax.all_to_all(traces, GZ + ('x',), 0, 0, tiled=True)]
    ppermute x3, starting transfers between devices: 8.3 us -> 6.7 us  [swap(): return lax.ppermute(value, axis, pairs)]
    ppermute x3, waiting for transfers between devices: 3.56 us -> 2.13 us  [swap(): return lax.ppermute(value, axis, pairs)]
    ppermute x1, starting transfers between devices: 3.42 us -> 2.23 us  [swap_open(): return lax.ppermute(value, axis, pairs + [(j, i) for i, j in pairs])]
    pallas_call x6, Pallas kernels: 18.4 us -> 19 us  [the longest x1 4.46 us: shards(): call(wave_step, (block,) * 2 + (pltpu.HBM(block.shape, block.dtype),) * 3...]
  transfers between devices with their start and end apart: 5 -> 5, of which waited for: 1 -> 2; matrix products, arithmetic and copies ran while one was open for 0% -> 0% of each run, Pallas kernels for 18% -> 21%
where the time goes in v4:
time: 48.1 us; the launch traced here: 47.8 us
  starting transfers between devices  20 us (42%)
  Pallas kernels  19 us (40%)
  waiting for transfers between devices  7.27 us (15%)
  between operations  0.8 us (2%)
  local copies, waits for them, and re-layouts  0.71 us (1%)
    all_to_all x1, starting transfers between devices, shards(): table = lax.all_to_all(traces, GZ + ('x',), 0, 0, tiled=True)  11 us
    ppermute x3, starting transfers between devices, swap(): return lax.ppermute(value, axis, pairs)  6.7 us
    all_to_all x1, waiting for transfers between devices, shards(): table = lax.all_to_all(traces, GZ + ('x',), 0, 0, tiled=True)  5.13 us
    pallas_call x1, Pallas kernels, shards(): call(wave_step, (block,) * 2 + (pltpu.HBM(block.shape, block.dtype),) * 3...  4.46 us
    pallas_call x1, Pallas kernels, shards(): call(list_receivers, jax.ShapeDtypeStruct((1, rec.shape[1] + 128), jnp.in...  4.27 us
    pallas_call x1, Pallas kernels, shards(): call(adjoint_step, (block,) * 3, [smem()] * 2 + [vmem()] * 5 + [smem()] *...  4.25 us
    pallas_call x1, Pallas kernels, shards(): call(edge_step, (edge,) * 2 + (zpack, zpack, f32(128, 128)), [smem()] * 2...  2.63 us
    ppermute x1, starting transfers between devices, swap_open(): return lax.ppermute(value, axis, pairs + [(j, i) for i, j in pairs])  2.23 us
  transfers between devices with their start and end apart: 5, of which 2 were waited for; matrix products, arithmetic and copies ran while one was open for 0% of the time, Pallas kernels for 21%

profile of v4, /device:TPU:1, one launch (start us, length us, event | category | flops | bytes accessed | tf_op | source)
XLA Modules:
  0.0 47.8 jit_solution(5513263894799748787)
XLA Ops:
  0.6 0.0 copy-start.6
  0.7 0.1 pad_add_fusion.meta
  0.7 0.0 copy-start
  0.7 0.0 copy-start.1
  0.7 0.0 copy-start.4
  0.8 1.8 %pack_y.1 = (f32[4,16,512]{2,1,0:T(8,128)S(1)}, f32[4,16,512]{2,1,0:T(8,128)S(1)}, f32[1,128]{1,0:T(1,128)S(1)}) custom-call(s32[4]{0:T(128)S(1)} %pad_add_fusion.meta, f32[4,32,512]{2,1,0:T(8,128)} %u.7, f32[4,32,512]{2,1,0:T(8,128)} %a.7, f32[4,32,512]{2,1,0:T(8,128)} %u1_.7, f32[4,32,512]{2,1,0:T(8,128)} %a1.5, f32[4,32,512]{2,1,0:T(8,128)} %v.9, f32[2,16]{1,0:T(2,128)} %obs.1), custom_call_target="tpu_custom_call" | custom-call | tf_op jit(solution)/shard_map/pack_y/pallas_call | solution.py:507
  2.6 6.1 %collective-permute-start.1 = (f32[4,16,512]{2,1,0:T(8,128)S(1)}, f32[4,16,512]{2,1,0:T(8,128)S(1)}, u32[]{:S(2)}, u32[]{:S(2)}) collective-permute-start(f32[4,16,512]{2,1,0:T(8,128)S(1)} %get-tuple-element.29), channel_id=1, source_target_pairs={{0,7},{1,2},{2,1},{3,4},{4,3},{5,6},{6,5},{7,0},{8,15},{9,10},{10,... | collective-permute-start | bytes 393224 | tf_op jit(solution)/shard_map/ppermute | solution.py:488
  8.7 0.0 collective-permute-start
  8.7 0.0 copy-done.6
  8.7 4.3 %list_receivers.1.found = s32[1,4224]{1,0:T(1,128)S(1)} custom-call(s32[4]{0:T(128)S(1)} %pad_add_fusion.meta, s32[3,4096]{1,0:T(4,128)S(1)} %copy-done.6), custom_call_target="tpu_custom_call" | custom-call | tf_op jit(solution)/shard_map/list_receivers/pallas_call | solution.py:519
  13.0 0.0 copy-done
  13.0 0.0 copy-done.1
  13.0 0.0 copy-done.2
  13.0 0.0 copy-done.3
  13.0 0.0 copy-done.4
  13.0 0.0 copy-done.5
  13.1 1.5 %own_step.1 = (f32[4,32,512]{2,1,0:T(8,128)S(1)}, f32[4,32,512]{2,1,0:T(8,128)S(1)}) custom-call(s32[4]{0:T(128)S(1)} %pad_add_fusion.meta, f32[4,132]{1,0:T(4,128)S(1)} %copy-done.5, f32[4,32,512]{2,1,0:T(8,128)S(1)} %copy-done.1, f32[4,32,512]{2,1,0:T(8,128)S(1)} %copy-done.2, f32[4,32,512]{2,1,0:T(8,128)S(1)} %copy-done.3, f32[4,32,512]{2,1,0:T(8,128)S(1)} %copy-done.4, ...), custom_call_target="tpu_custom_call" | custom-call | tf_op jit(solution)/shard_map/own_step/pallas_call | solution.py:517
  14.6 0.0 collective-permute-done.1.rg
  14.6 2.1 %collective-permute-done.rh = f32[4,16,512]{2,1,0:T(8,128)S(1)} collective-permute-done((f32[4,16,512]{2,1,0:T(8,128)S(1)}, f32[4,16,512]{2,1,0:T(8,128)S(1)}, u32[]{:S(2)}, u32[]{:S(2)}) %collective-permute-start) | collective-permute-done | bytes 131104 | tf_op jit(solution)/shard_map/ppermute | solution.py:488
  16.7 2.6 %edge_step.1 = (f32[2,4,8,512]{3,2,1,0:T(8,128)S(1)}, f32[2,4,8,512]{3,2,1,0:T(8,128)S(1)}, f32[2,168,512]{2,1,0:T(8,128)}, f32[2,168,512]{2,1,0:T(8,128)}, f32[128,128]{1,0:T(8,128)}) custom-call(s32[4]{0:T(128)S(1)} %pad_add_fusion.meta, f32[4,132]{1,0:T(4,128)S(1)} %copy-done.5, f32[4,32,512]{2,1,0:T(8,128)S(1)} %copy-done.1, ...), custom_call_target="tpu_custom_call" | custom-call | tf_op jit(solution)/shard_map/edge_step/pallas_call | solution.py:534
  19.4 0.6 %collective-permute-start.2 = (f32[2,168,512]{2,1,0:T(8,128)}, f32[2,168,512]{2,1,0:T(8,128)S(1)}, u32[]{:S(2)}, u32[]{:S(2)}) collective-permute-start(f32[2,168,512]{2,1,0:T(8,128)} %get-tuple-element.34), channel_id=1, source_target_pairs={{0,8},{8,0},{16,24},{24,16},{32,40},{40,32},{48,56},{56,48},{64,72... | collective-permute-start | bytes 2064392 | tf_op jit(solution)/shard_map/ppermute | solution.py:488
  20.0 2.2 %collective-permute-start.3 = (f32[2,168,512]{2,1,0:T(8,128)}, f32[2,168,512]{2,1,0:T(8,128)S(1)}, u32[]{:S(2)}, u32[]{:S(2)}) collective-permute-start(f32[2,168,512]{2,1,0:T(8,128)} %get-tuple-element.35), channel_id=1, source_target_pairs={{8,16},{24,32},{40,48},{56,64},{72,80},{88,96},{104,112},{120,128}... | collective-permute-start | bytes 2064392 | tf_op jit(solution)/shard_map/ppermute | solution.py:493
  22.2 11.0 %all-to-all-start = ((f32[128,1,128]{2,1,0:T(1,128)}), f32[128,1,128]{2,1,0:T(1,128)S(1)}, u32[]{:S(2)}, u32[]{:S(2)}) async-start(f32[128,1,128]{2,1,0:T(1,128)} %bitcast.5), calls=%async_computation | async-start | bytes 131072 | tf_op jit(solution)/shard_map/all_to_all | solution.py:543
  33.2 0.0 copy-start.7
  33.2 0.0 collective-permute-done.2.rc
  33.3 0.0 collective-permute-done.3.rb
  33.3 0.0 copy-start.8
  33.3 0.6 %copy-done.7 = s32[3,4]{1,0:T(4,128)S(1)} copy-done((s32[3,4]{1,0:T(4,128)S(1)}, s32[3,4]{1,0:T(4,128)}, u32[]{:S(2)}) %copy-start.7) | copy-done | bytes 72
  33.9 0.0 copy-done.8
  34.0 4.5 %wave_step.1 = (f32[4,32,512]{2,1,0:T(8,128)}, f32[4,32,512]{2,1,0:T(8,128)}, f32[4,32,512]{2,1,0:T(8,128)}, f32[4,32,512]{2,1,0:T(8,128)}, f32[4,32,512]{2,1,0:T(8,128)}, /*index=5*/f32[8,48,512]{2,1,0:T(8,128)S(1)}) custom-call(s32[4]{0:T(128)S(1)} %pad_add_fusion.meta, f32[4,132]{1,0:T(4,128)S(1)} %copy-done.5, f32[4,32,512]{2,1,0:T(8,128)} %u.7, ...), custom_call_target="tpu_custom_call" | custom-call | tf_op jit(solution)/shard_map/wave_step/pallas_call | solution.py:545
  38.4 5.1 %all-to-all-done = f32[128,1,128]{2,1,0:T(1,128)S(1)} async-done(((f32[128,1,128]{2,1,0:T(1,128)}), f32[128,1,128]{2,1,0:T(1,128)S(1)}, u32[]{:S(2)}, u32[]{:S(2)}) %all-to-all-start) | async-done | bytes 65568 | tf_op jit(solution)/shard_map/all_to_all | solution.py:543
  43.5 4.2 %adjoint_step.1 = (f32[4,32,512]{2,1,0:T(8,128)}, f32[4,32,512]{2,1,0:T(8,128)}, f32[4,32,512]{2,1,0:T(8,128)}) custom-call(s32[4]{0:T(128)S(1)} %pad_add_fusion.meta, f32[4,132]{1,0:T(4,128)S(1)} %copy-done.5, f32[4,32,512]{2,1,0:T(8,128)} %v.9, f32[8,48,512]{2,1,0:T(8,128)S(1)} %get-tuple-element.39.a0p, f32[4,32,512]{2,1,0:T(8,128)} %get-tuple-element.40.w, ...), custom_call_target="tpu_custom_call" | custom-call | tf_op jit(solution)/shard_map/adjoint_step/pallas_call | solution.py:552
  (3 shorter events, 0.0 us)
Async XLA Ops:
  0.6 8.1 %copy-start.6 = (s32[3,4096]{1,0:T(4,128)S(1)}, s32[3,4096]{1,0:T(4,128)}, u32[]{:S(2)}) copy-start(s32[3,4096]{1,0:T(4,128)} %rec.1) | copy-start | bytes 147460
  0.7 12.3 %copy-start = (f32[4,32,512]{2,1,0:T(8,128)S(1)}, f32[4,32,512]{2,1,0:T(8,128)}, u32[]{:S(2)}) copy-start(f32[4,32,512]{2,1,0:T(8,128)} %v.9) | copy-start | bytes 786436
  0.7 12.3 %copy-start.1 = (f32[4,32,512]{2,1,0:T(8,128)S(1)}, f32[4,32,512]{2,1,0:T(8,128)}, u32[]{:S(2)}) copy-start(f32[4,32,512]{2,1,0:T(8,128)} %u.7) | copy-start | bytes 786436
  0.7 12.3 %copy-start.2 = (f32[4,32,512]{2,1,0:T(8,128)S(1)}, f32[4,32,512]{2,1,0:T(8,128)}, u32[]{:S(2)}) copy-start(f32[4,32,512]{2,1,0:T(8,128)} %a.7) | copy-start | bytes 786436
  0.7 12.3 %copy-start.3 = (f32[4,32,512]{2,1,0:T(8,128)S(1)}, f32[4,32,512]{2,1,0:T(8,128)}, u32[]{:S(2)}) copy-start(f32[4,32,512]{2,1,0:T(8,128)} %u1_.7) | copy-start | bytes 786436
  0.7 12.3 %copy-start.4 = (f32[4,32,512]{2,1,0:T(8,128)S(1)}, f32[4,32,512]{2,1,0:T(8,128)}, u32[]{:S(2)}) copy-start(f32[4,32,512]{2,1,0:T(8,128)} %a1.5) | copy-start | bytes 786436
  2.6 12.0 %collective-permute-start.1 = (f32[4,16,512]{2,1,0:T(8,128)S(1)}, f32[4,16,512]{2,1,0:T(8,128)S(1)}, u32[]{:S(2)}, u32[]{:S(2)}) collective-permute-start(f32[4,16,512]{2,1,0:T(8,128)S(1)} %get-tuple-element.29), channel_id=1, source_target_pairs={{0,7},{1,2},{2,1},{3,4},{4,3},{5,6},{6,5},{7,0},{8,15},{9,10},{10,... | collective-permute-start | bytes 393224 | tf_op jit(solution)/shard_map/ppermute | solution.py:488
  8.7 4.3 %copy-start.5 = (f32[4,132]{1,0:T(4,128)S(1)}, f32[4,132]{1,0:T(4,128)}, u32[]{:S(2)}) copy-start(f32[4,132]{1,0:T(4,128)} %constant.29.clone.coef) | copy-start | bytes 6340
  8.7 8.0 %collective-permute-start = (f32[4,16,512]{2,1,0:T(8,128)S(1)}, f32[4,16,512]{2,1,0:T(8,128)S(1)}, u32[]{:S(2)}, u32[]{:S(2)}) collective-permute-start(f32[4,16,512]{2,1,0:T(8,128)S(1)} %get-tuple-element.28), channel_id=1, source_target_pairs={{0,1},{1,0},{2,3},{3,2},{4,5},{5,4},{6,7},{7,6},{8,9},{9,8},{10,11... | collective-permute-start | bytes 393224 | tf_op jit(solution)/shard_map/ppermute | solution.py:488
  19.4 13.9 %collective-permute-start.2 = (f32[2,168,512]{2,1,0:T(8,128)}, f32[2,168,512]{2,1,0:T(8,128)S(1)}, u32[]{:S(2)}, u32[]{:S(2)}) collective-permute-start(f32[2,168,512]{2,1,0:T(8,128)} %get-tuple-element.34), channel_id=1, source_target_pairs={{0,8},{8,0},{16,24},{24,16},{32,40},{40,32},{48,56},{56,48},{64,72... | collective-permute-start | bytes 2064392 | tf_op jit(solution)/shard_map/ppermute | solution.py:488
  20.0 13.3 %collective-permute-start.3 = (f32[2,168,512]{2,1,0:T(8,128)}, f32[2,168,512]{2,1,0:T(8,128)S(1)}, u32[]{:S(2)}, u32[]{:S(2)}) collective-permute-start(f32[2,168,512]{2,1,0:T(8,128)} %get-tuple-element.35), channel_id=1, source_target_pairs={{8,16},{24,32},{40,48},{56,64},{72,80},{88,96},{104,112},{120,128}... | collective-permute-start | bytes 2064392 | tf_op jit(solution)/shard_map/ppermute | solution.py:493
  22.2 21.3 %all-to-all-start = ((f32[128,1,128]{2,1,0:T(1,128)}), f32[128,1,128]{2,1,0:T(1,128)S(1)}, u32[]{:S(2)}, u32[]{:S(2)}) async-start(f32[128,1,128]{2,1,0:T(1,128)} %bitcast.5), calls=%async_computation | async-start | bytes 131072 | tf_op jit(solution)/shard_map/all_to_all | solution.py:543
  33.2 0.7 %copy-start.7 = (s32[3,4]{1,0:T(4,128)S(1)}, s32[3,4]{1,0:T(4,128)}, u32[]{:S(2)}) copy-start(s32[3,4]{1,0:T(4,128)} %src.1) | copy-start | bytes 148
  33.3 0.7 %copy-start.8 = (f32[2,4]{1,0:T(2,128)S(1)}, f32[2,4]{1,0:T(2,128)}, u32[]{:S(2)}) copy-start(f32[2,4]{1,0:T(2,128)} %amp.1) | copy-start | bytes 100

commit v5 on v4

v5 whole, which is shorter than its diff:
```python
import jax
import jax.numpy as jnp
import numpy as np
from jax import lax
from jax.experimental import pallas as pl
from jax.experimental.pallas import tpu as pltpu
from jax.sharding import Mesh
from jax.sharding import PartitionSpec as P

CENTRE = -7.5
NEAR = 4.0 / 3.0
FAR = -1.0 / 12.0
RATIO = 0.1
DAMP = 0.3

GZ = ("yl", "z", "c")
GY = ("xh", "xl", "yh")
O = 8
NZ_DEV, NY_DEV = 32, 8
CZ, CY, NX = 4, 32, 512
NZ, NY = NZ_DEV * CZ, NY_DEV * CY
FR = CY + 2 * O
VMEM_LIMIT = 8 * 1024 * 1024
ZROWS = 5 * CY + 8
GROUP = 4


def sponge_table():
    depth = np.arange(CZ + 1, dtype=np.float32) / np.float32(CZ)
    a = np.float32(DAMP) * (depth * depth)
    one = np.float32(1)
    return np.stack([one + a, one - a, one / (one - a), one / (one + a)]).astype(np.float32)


def sponge(z, which):
    into = jnp.minimum(jnp.maximum(jnp.maximum(CZ - z, z - (NZ - 1 - CZ)), 0), CZ)
    values = []
    for row in which:
        table = sponge_table()[row]
        value = jnp.float32(table[0])
        for k in range(1, CZ + 1):
            value = jnp.where(into == k, jnp.float32(table[k]), value)
        values.append(value)
    return values


def place_in_mesh():
    gz, gy = lax.axis_index(GZ), lax.axis_index(GY)
    return gz * CZ, gy * CY, lax.axis_index("yh"), lax.axis_index("c")


def smem():
    return pl.BlockSpec(memory_space=pltpu.SMEM)


def anywhere():
    return pl.BlockSpec(memory_space=pl.ANY)


def vmem():
    return pl.BlockSpec()


def x_terms(u):
    lane = lax.broadcasted_iota(jnp.int32, u.shape, 1)
    a = jnp.where(lane >= 1, pltpu.roll(u, 1, 1), 0.0)
    b = jnp.where(lane < NX - 1, pltpu.roll(u, NX - 1, 1), 0.0)
    c = jnp.where(lane >= 2, pltpu.roll(u, 2, 1), 0.0)
    d = jnp.where(lane < NX - 2, pltpu.roll(u, NX - 2, 1), 0.0)
    return a + b, c + d


def laplace(f, k, s):
    rows = lambda layer, shift: f[layer, s + shift : s + shift + 8, :]
    u = rows(k, 0)
    near, far = x_terms(u)
    near = near + ((rows(k, -1) + rows(k, 1)) + (rows(k - 1, 0) + rows(k + 1, 0)))
    far = far + ((rows(k, -2) + rows(k, 2)) + (rows(k - 2, 0) + rows(k + 2, 0)))
    return u, CENTRE * u + NEAR * near + FAR * far


def depth_factors(l):
    near_up = jnp.where(l >= 1, jnp.float32(NEAR), jnp.float32(0.0))
    near_dn = jnp.where(l < CZ - 1, jnp.float32(NEAR), jnp.float32(0.0))
    far_up = jnp.where(l >= 2, jnp.float32(FAR), jnp.float32(0.0))
    far_dn = jnp.where(l < CZ - 2, jnp.float32(FAR), jnp.float32(0.0))
    layers = jnp.maximum(l - 1, 0), jnp.minimum(l + 1, CZ - 1), jnp.maximum(l - 2, 0), jnp.minimum(l + 2, CZ - 1)
    return tuple(zip(layers, (near_up, near_dn, far_up, far_dn)))


def partial_laplace(f, l, s, size, factors):
    u = f[l, s : s + 8, :]

    def shifted(shift):
        if 0 <= s + shift and s + shift + 8 <= size:
            return f[l, s + shift : s + shift + 8, :]
        return pltpu.roll(u, (-shift) % 8, 0)

    near, far = x_terms(u)
    lap = CENTRE * u + NEAR * (near + (shifted(-1) + shifted(1))) + FAR * (far + (shifted(-2) + shifted(2)))
    for layer, factor in factors:
        lap = lap + factor * f[layer, s : s + 8, :]
    return u, lap


def pack_y(u, a, u1, a1, v, obs, h, g, own, first, last, obs_v, row, sem):
    _, y0, yh, _ = place_in_mesh()
    copies = []
    for i, ref in enumerate((u, a, u1, a1, v)):
        copies.append(pltpu.make_async_copy(ref.at[:, 0:8, :], first.at[i], sem.at[2 * i]))
        copies.append(pltpu.make_async_copy(ref.at[:, CY - 8 : CY, :], last.at[i], sem.at[2 * i + 1]))
    copies.append(pltpu.make_async_copy(obs, obs_v, sem.at[10]))
    for copy in copies:
        copy.start()
    for copy in copies:
        copy.wait()
    for k in range(4):
        for t in range(2):
            row[0:1, 32 * k + 16 * t : 32 * k + 16 * t + 16] = obs_v[t : t + 1, :]
    slot = lax.broadcasted_iota(jnp.int32, (1, 128), 1) >> 5
    mine = jnp.where(slot == ((y0 // CY) & 3), row[0:1, :], 0.0)
    own[...] = mine

    def pack(dst, high):
        rows = last if high else first
        four = slice(4, 8) if high else slice(0, 4)
        two = slice(6, 8) if high else slice(0, 2)
        dst[:, 0:4, :] = rows[0, :, four, :]
        dst[:, 4:8, :] = rows[1, :, four, :]
        dst[:, 8:10, :] = rows[2, :, two, :]
        dst[:, 10:12, :] = rows[3, :, two, :]
        dst[:, 12:14, :] = rows[4, :, two, :]
        dst[:, 14:16, :] = jnp.zeros((CZ, 2, NX), jnp.float32)
        dst[0, 14:15, 0:128] = mine

    @pl.when(yh == 0)
    def _():
        pack(h, True)
        pack(g, False)

    @pl.when(yh != 0)
    def _():
        pack(h, False)
        pack(g, True)


def pick_y(yh, rh, rg, low, high):
    @pl.when(yh == 0)
    def _():
        high(rh)
        low(rg)

    @pl.when(yh != 0)
    def _():
        low(rh)
        high(rg)


def own_step(u, a, u1, a1, v, u0p, a0p):
    z0, _, yh, core = place_in_mesh()

    def layer(l, carry):
        up, dn, iu, ia = sponge(z0 + l, range(4))
        factors = depth_factors(l)
        for s in range(0, CY, 8):
            y = slice(s, s + 8)
            c = v[l, y, :] * RATIO
            c = c * c
            p, lap = partial_laplace(u, l, s, CY, factors)
            u0p[l, y, :] = (2.0 * p - up * u1[l, y, :] + c * lap) * iu
            q, lap = partial_laplace(a, l, s, CY, factors)
            a0p[l, y, :] = (2.0 * q - dn * a1[l, y, :] + c * lap) * ia
        return carry

    lax.fori_loop(0, CZ, layer, 0)


def edge_step(
    u, a, u1, a1, v, rh, rg, u0p, a0p, ut, at, zc, zb,
    pu, pa, pu1, pa1, pv,
):
    z0, _, yh, core = place_in_mesh()
    pu[0, :, 4:8, :] = u[:, 0:4, :]
    pu[1, :, 0:4, :] = u[:, CY - 4 : CY, :]
    pa[0, :, 4:8, :] = a[:, 0:4, :]
    pa[1, :, 0:4, :] = a[:, CY - 4 : CY, :]
    for part, block in ((pu1, u1), (pa1, a1), (pv, v)):
        part[0, :, 4:6, :] = block[:, 0:2, :]
        part[1, :, 2:4, :] = block[:, CY - 2 : CY, :]

    def low(r):
        pu[0, :, 0:4, :] = r[:, 0:4, :]
        pa[0, :, 0:4, :] = r[:, 4:8, :]
        pu1[0, :, 2:4, :] = r[:, 8:10, :]
        pa1[0, :, 2:4, :] = r[:, 10:12, :]
        pv[0, :, 2:4, :] = r[:, 12:14, :]

    def high(r):
        pu[1, :, 4:8, :] = r[:, 0:4, :]
        pa[1, :, 4:8, :] = r[:, 4:8, :]
        pu1[1, :, 4:6, :] = r[:, 8:10, :]
        pa1[1, :, 4:6, :] = r[:, 10:12, :]
        pv[1, :, 4:6, :] = r[:, 12:14, :]

    pick_y(yh, rh, rg, low, high)

    def layer(l, carry):
        up, dn, iu, ia = sponge(z0 + l, range(4))
        factors = depth_factors(l)
        for side in range(2):
            c = pv[side, l] * RATIO
            c = c * c
            p, lap = partial_laplace(pu.at[side], l, 0, 8, factors)
            ut[side, l] = (2.0 * p - up * pu1[side, l] + c * lap) * iu
            q, lap = partial_laplace(pa.at[side], l, 0, 8, factors)
            at[side, l] = (2.0 * q - dn * pa1[side, l] + c * lap) * ia
        return carry

    lax.fori_loop(0, CZ, layer, 0)
    ut[0, :, 0:2, :] = pu[0, :, 2:4, :]
    ut[0, :, 6:8, :] = pv[0, :, 2:4, :]
    ut[1, :, 6:8, :] = pu[1, :, 4:6, :]
    ut[1, :, 0:2, :] = pv[1, :, 4:6, :]

    def pack(dst, l):
        m = slice(l, l + 2)
        dst[:, 0:CY, :] = u[m]
        dst[:, CY : 2 * CY, :] = a[m]
        dst[:, 4 * CY : 5 * CY, :] = v[m]
        for b, p, t in ((2 * CY, u0p, ut), (3 * CY, a0p, at)):
            dst[:, b : b + CY, :] = p[m]
            dst[:, b : b + 2, :] = t[0, m, 4:6, :]
            dst[:, b + CY - 2 : b + CY, :] = t[1, m, 2:4, :]
        b = 5 * CY
        dst[:, b : b + 2, :] = pu[0, m, 2:4, :]
        dst[:, b + 2 : b + 4, :] = pu[1, m, 4:6, :]
        dst[:, b + 4 : b + 6, :] = pa[0, m, 2:4, :]
        dst[:, b + 6 : b + 8, :] = pa[1, m, 4:6, :]

    @pl.when(core == 0)
    def _():
        pack(zc, 2)
        pack(zb, 0)

    @pl.when(core != 0)
    def _():
        pack(zc, 0)
        pack(zb, 2)


def list_receivers(rec, short, long, bits, words_v, codes_v, words, codes, found, sem):
    z0, y0, _, _ = place_in_mesh()
    lz = rec[0:1, :] - z0
    ly = ((rec[1:2, :] - y0 + 16) & (NY - 1)) - 16
    x = rec[2:3, :]
    own_z = (lz >= 0) & (lz < CZ)
    own_y = (ly >= 0) & (ly < CY)
    near = (lz >= -2) & (lz < CZ + 2) & (ly >= -2) & (ly < CY + 2) & (own_z | own_y)
    row = ly + O
    number = lax.broadcasted_iota(jnp.int32, lz.shape, 1)
    codes_v[...] = (
        ((row & 7) * 128 + (x & 127)) | ((x >> 7) << 10) | ((row >> 3) << 12) | ((lz + 2) << 15) | (number << 18)
    )
    m = near.astype(jnp.int32)
    for i in range(32):
        bits[i : i + 1, :] = m[:, 128 * i : 128 * i + 128] << i
    words_v[...] = jnp.sum(bits[...], axis=0, keepdims=True)
    copies = [pltpu.make_async_copy(codes_v, codes, sem.at[0]), pltpu.make_async_copy(words_v, words, sem.at[1])]
    for copy in copies:
        copy.start()
    for copy in copies:
        copy.wait()

    def word_step(w, count):
        def bit_step(carry):
            word, count = carry
            low = word & (-word)
            found[0, count + 1] = codes[0, (31 - lax.clz(low)) * 128 + w]
            return word ^ low, count + 1

        return lax.while_loop(lambda carry: carry[0] != 0, bit_step, (words[0, w], count))[1]

    count = lax.fori_loop(0, 128, word_step, 0)
    found[0, 0] = count
    for k in range(GROUP - 1):
        found[0, count + 1 + k] = 0
    copy = pltpu.make_async_copy(found.at[:, 0:128], short, sem.at[0])
    copy.start()
    copy.wait()

    @pl.when(count > 128 - GROUP)
    def _():
        copy = pltpu.make_async_copy(found, long, sem.at[1])
        copy.start()
        copy.wait()


def fetch_list(short, long, found, sem):
    copy = pltpu.make_async_copy(short, found.at[:, 0:128], sem)
    copy.start()

    def finish():
        copy.wait()

        @pl.when(found[0, 0] > 128 - GROUP)
        def _():
            rest = pltpu.make_async_copy(long, found, sem)
            rest.start()
            rest.wait()

    return finish


def cell_place():
    return lax.broadcasted_iota(jnp.int32, (8, 128), 0) * 128 + lax.broadcasted_iota(jnp.int32, (8, 128), 1)


def cell_at(place, layer, row, x):
    rows = pl.ds(pl.multiple_of((row >> 3) << 3, 8), 8)
    cols = pl.ds(pl.multiple_of((x >> 7) << 7, 128), 128)
    return (layer, rows, cols), place == ((row & 7) * 128 + (x & 127))


def wave_step(
    u, a, u1, v, u0p, a0p, ut, at, rc, rb, src, amp, short, long,
    u2, u0o, w, gp, ep, a0f,
    uf, u0f, af, vf, ef, sf, u1s, corners, u2s, ws, gs, found, sem, store_sem,
):
    e = O + CY
    z0, y0, yh, core = place_in_mesh()
    own = (slice(2, 6), slice(O, e), slice(None))
    into = [(u1, u1s), (u0p, u0f.at[own]), (a0p, a0f.at[own]), (u, uf.at[own]), (a, af.at[own]), (v, vf.at[own])]
    for j, r in enumerate((rc, rb)):
        k = 6 * (1 - core) if j == 0 else 6 * core
        for i, f in enumerate((uf, af, u0f, a0f, vf)):
            into.append((r.at[:, i * CY : (i + 1) * CY, :], f.at[pl.ds(k, 2), O:e, :]))
        into.append((r.at[:, 5 * CY : ZROWS, :], corners.at[j]))
    fetches = [pltpu.make_async_copy(part, whole, sem.at[i]) for i, (part, whole) in enumerate(into)]
    for fetch in fetches:
        fetch.start()
    finish = fetch_list(short, long, found, sem.at[len(into)])
    for l in range(CZ):
        sf[l] = jnp.zeros((CY, NX), jnp.float32)
    for fetch in fetches:
        fetch.wait()
    for f0, t in ((u0f, ut), (a0f, at)):
        f0[2:6, O - 2 : O + 2, :] = t[0, :, 2:6, :]
        f0[2:6, e - 2 : e + 2, :] = t[1, :, 2:6, :]
    uf[2:6, O - 2 : O, :] = ut[0, :, 0:2, :]
    uf[2:6, e : e + 2, :] = ut[1, :, 6:8, :]
    vf[2:6, O - 2 : O, :] = ut[0, :, 6:8, :]
    vf[2:6, e : e + 2, :] = ut[1, :, 0:2, :]

    def fill_corners(j, k):
        m = slice(k, k + 2)
        for i, f in enumerate((uf, af)):
            f[m, O - 2 : O, :] = corners[j, :, 4 * i : 4 * i + 2, :]
            f[m, e : e + 2, :] = corners[j, :, 4 * i + 2 : 4 * i + 4, :]

    @pl.when(core == 0)
    def _():
        fill_corners(1, 0)
        fill_corners(0, 6)

    @pl.when(core != 0)
    def _():
        fill_corners(0, 0)
        fill_corners(1, 6)

    lacks = ((0, None, 2), (1, 2, 3), (2, 1, 0), (3, None, 1), (4, None, 6), (5, 6, 7), (6, 5, 4), (7, None, 5))
    for k, near, far in lacks:
        edge = 2 <= k < 6
        iu, ia = sponge(z0 + k - 2, (2, 3))

        def rows(t, carry):
            s = pl.multiple_of(t * 8, 8)
            c = vf[k, pl.ds(s, 8), :] * RATIO
            c = c * c
            for f, f0, scale in ((uf, u0f, iu), (af, a0f, ia)):
                lap = FAR * f[far, pl.ds(s, 8), :]
                if near is not None:
                    lap = lap + NEAR * f[near, pl.ds(s, 8), :]
                f0[k, pl.ds(s, 8), :] = f0[k, pl.ds(s, 8), :] + (c * scale) * lap
            return carry

        first = O // 8
        lax.fori_loop(first - edge, first + CY // 8 + edge, rows, 0)

    place = cell_place()

    def add_source(i, carry):
        lz = src[0, i] - z0
        ly = ((src[1, i] - y0 + 16) & (NY - 1)) - 16
        own_z = (lz >= 0) & (lz < CZ)
        own_y = (ly >= 0) & (ly < CY)
        near = (lz >= -2) & (lz < CZ + 2) & (ly >= -2) & (ly < CY + 2) & (own_z | own_y)

        @pl.when(near)
        def _():
            at, hit = cell_at(place, lz + 2, ly + O, src[2, i])
            c = vf[at] * RATIO
            u0f[at] = u0f[at] + jnp.where(hit, (c * c) * (amp[0, i] * sponge(z0 + lz, (2,))[0]), 0.0)

        @pl.when(own_z & own_y)
        def _():
            at, hit = cell_at(place, lz, ly, src[2, i])
            sf[at] = sf[at] + jnp.where(hit, amp[1, i], 0.0)

        return carry

    lax.fori_loop(0, src.shape[1], add_source, 0)
    for l in range(CZ):
        ef[l + 2, O:e, :] = -sponge(z0 + l, (1,))[0] * af[l + 2, O:e, :]

    def sample(r, at, z, hit):
        a0f[at] = a0f[at] + jnp.where(hit, uf[at] * sponge(z0 + z - 2, (3,))[0], 0.0)
        ef[at] = ef[at] + jnp.where(hit, u0f[at], 0.0)

    finish()
    each_receiver(found, place, sample)

    stores = []
    for l in range(CZ):
        up, iu = sponge(z0 + l, (0, 2))
        for s in range(O, e, 8):
            y = slice(s - O, s - O + 8)
            vel = vf[l + 2, s : s + 8, :]
            c = vel * RATIO
            c = c * c
            un = uf[l + 2, s : s + 8, :]
            q, lap = laplace(u0f, l + 2, s)
            new = (2.0 * q - up * un + c * (lap + sf[l, y, :])) * iu
            u2s[l, y, :] = new
            slow = 2.0 / vel
            ws[l, y, :] = slow * (un - 2.0 * q + new)
            gs[l, y, :] = slow * af[l + 2, s : s + 8, :] * (u1s[l, y, :] - 2.0 * un + q)
        done = ((u2s.at[l], u2), (u0f.at[l + 2, O:e, :], u0o), (ws.at[l], w), (gs.at[l], gp), (ef.at[l + 2, O:e, :], ep))
        for i, (part, whole) in enumerate(done):
            stores.append(pltpu.make_async_copy(part, whole.at[l], store_sem.at[5 * l + i]))
            stores[-1].start()
    for store in stores:
        store.wait()


def each_receiver(found, place, one):
    count = found[0, 0]

    def group(b, carry):
        for k in range(GROUP):
            n = b * GROUP + k
            code = found[0, n + 1]
            z = (code >> 15) & 7
            rows = pl.ds(pl.multiple_of(((code >> 12) & 7) * 8, 8), 8)
            cols = pl.ds(pl.multiple_of(((code >> 10) & 3) * 128, 128), 128)
            one(code >> 18, (z, rows, cols), z, place == jnp.where(n < count, code & 1023, -1))
        return carry

    lax.fori_loop(0, (count + GROUP - 1) // GROUP, group, 0)


def adjoint_step(v, a0p, w, gp, ep, short, long, table, a2, a0o, grad, a0f, ef, vs, ws, gs, a2s, a0s, found, obs, sem):
    own = (slice(2, 6), slice(O, O + CY), slice(None))
    into = ((table, obs), (ep, ef.at[own]), (a0p, a0f), (v, vs), (w, ws), (gp, gs))
    fetches = [pltpu.make_async_copy(src, dst, sem.at[i]) for i, (src, dst) in enumerate(into)]
    finish = fetch_list(short, long, found, sem.at[6])
    for fetch in fetches:
        fetch.start()
    z0, _, _, _ = place_in_mesh()
    place = cell_place()
    finish()
    for fetch in fetches[:3]:
        fetch.wait()

    def subtract(r, at, z, hit):
        col = ((r >> 4) & 3) * 32 + (r & 15)
        first = obs[r >> 6, col] * sponge(z0 + z - 2, (3,))[0]
        second = obs[r >> 6, col + 16]
        a0f[at] = a0f[at] - jnp.where(hit, first, 0.0)
        ef[at] = ef[at] - jnp.where(hit, second, 0.0)

    each_receiver(found, place, subtract)
    for fetch in fetches[3:]:
        fetch.wait()

    stores = []
    for l in range(CZ):
        ia = sponge(z0 + l, (3,))[0]
        for s in range(O, O + CY, 8):
            y = slice(s - O, s - O + 8)
            c = vs[l, y, :] * RATIO
            c = c * c
            q, lap = laplace(a0f, l + 2, s)
            a2s[l, y, :] = (2.0 * q + ef[l + 2, s : s + 8, :] + c * lap) * ia
            a0s[l, y, :] = q
            gs[l, y, :] = gs[l, y, :] + ws[l, y, :] * q
        for i, (src, dst) in enumerate(((a2s, a2), (a0s, a0o), (gs, grad))):
            stores.append(pltpu.make_async_copy(src.at[l], dst.at[l], sem.at[7 + 3 * l + i]))
            stores[-1].start()
    for store in stores:
        store.wait()


def f32(*shape):
    return jax.ShapeDtypeStruct(shape, jnp.float32)


def hbm(*args):
    return tuple(pltpu.with_memory_space_constraint(x, pltpu.HBM) for x in args)


def call(kernel, out_shape, in_specs, scratch_shapes=(), out_specs=None):
    return pl.pallas_call(
        kernel,
        out_shape=out_shape,
        in_specs=in_specs,
        out_specs=tuple(out_specs) if out_specs else (vmem(),) * len(out_shape),
        scratch_shapes=scratch_shapes,
        compiler_params=pltpu.CompilerParams(vmem_limit_bytes=VMEM_LIMIT),
        name=kernel.__name__,
    )


def swap(value, axis, size, first):
    pairs = [(i, (first + ((i - first) % size ^ 1)) % size) for i in range(size)]
    return lax.ppermute(value, axis, pairs)


def swap_open(value, axis, size):
    pairs = [(i, i + 1) for i in range(1, size - 1, 2)]
    return lax.ppermute(value, axis, pairs + [(j, i) for i, j in pairs])


def shards(u, u1, a, a1, v, obs, rec, src, amp):
    assert u.shape == (CZ, CY, NX)
    block, edge = f32(CZ, CY, NX), f32(2, CZ, 8, NX)
    block_hbm = pltpu.HBM(block.shape, block.dtype)
    frame, zpack = f32(8, FR, NX), f32(2, ZROWS, NX)
    part = pltpu.VMEM((2, CZ, 8, NX), jnp.float32)
    full = pltpu.VMEM((8, FR, NX), jnp.float32)
    whole = pltpu.VMEM((CZ, CY, NX), jnp.float32)
    entries = rec.shape[1] + 128
    found_smem = pltpu.SMEM((1, entries), jnp.int32)
    dmas = lambda n: pltpu.SemaphoreType.DMA((n,))

    h, g, own = call(
        pack_y,
        (f32(CZ, 16, NX), f32(CZ, 16, NX), f32(1, 128)),
        [anywhere()] * 6,
        [pltpu.VMEM((5, CZ, 8, NX), jnp.float32)] * 2
        + [pltpu.VMEM((2, 16), jnp.float32), pltpu.VMEM((1, 128), jnp.float32), dmas(11)],
    )(*hbm(u, a, u1, a1, v, obs))
    rh = swap(h, GY, NY_DEV, 0)
    rg = swap(g, GY, NY_DEV, 1)
    two = own + rh[0, 14:15, 0:128]

    u0p, a0p = call(own_step, (block, block), [vmem()] * 5)(u, a, u1, a1, v)

    short, long = call(
        list_receivers,
        (jax.ShapeDtypeStruct((1, 128), jnp.int32), jax.ShapeDtypeStruct((1, entries), jnp.int32)),
        [vmem()],
        [
            pltpu.VMEM((32, 128), jnp.int32),
            pltpu.VMEM((1, 128), jnp.int32),
            pltpu.VMEM(rec[:1].shape, jnp.int32),
            pltpu.SMEM((1, 128), jnp.int32),
            pltpu.SMEM(rec[:1].shape, jnp.int32),
            found_smem,
            dmas(2),
        ],
        [anywhere()] * 2,
    )(rec)

    two, short, long = lax.optimization_barrier((two, short, long))
    four = two + swap(two, "xl", 2, 0)
    ut, at, zc, zb = call(
        edge_step,
        (edge,) * 2 + (pltpu.VMEM(zpack.shape, zpack.dtype),) * 2,
        [vmem()] * 9,
        [part] * 5,
    )(u, a, u1, a1, v, rh, rg, u0p, a0p)

    zc, zb, four = lax.optimization_barrier((zc, zb, four))
    rc = swap(zc, GZ, NZ_DEV, 0)
    rb = swap_open(zb, GZ, NZ_DEV)
    table = lax.all_to_all(jnp.broadcast_to(four, (64, 128)), GZ + ("xh",), 0, 0, tiled=True)

    u2, u0, w, gp, ep, a0f = call(
        wave_step,
        (block,) * 2 + (block_hbm,) * 3 + (frame,),
        [anywhere()] * 6 + [vmem()] * 2 + [anywhere()] * 2 + [smem()] * 2 + [anywhere()] * 2,
        [full] * 5
        + [whole] * 2
        + [pltpu.VMEM((2, 2, 8, NX), jnp.float32)]
        + [whole] * 3
        + [found_smem, dmas(19), dmas(20)],
        [anywhere()] * 5 + [vmem()],
    )(*hbm(u, a, u1, v), u0p, a0p, ut, at, *hbm(rc, rb, src, amp), short, long)

    a2, a0, grad = call(
        adjoint_step,
        (block,) * 3,
        [anywhere()] * 8,
        [full] * 2 + [whole] * 5 + [found_smem, pltpu.SMEM((64, 128), jnp.float32), dmas(19)],
        [anywhere()] * 3,
    )(*hbm(v), a0f, *hbm(w, gp, ep), short, long, table)
    return u2, u0, a2, a0, grad


def solution(mesh):
    fine = Mesh(mesh.devices.reshape(2, 8, 2, 2, 2, 2), ("yl", "z", "c", "xh", "xl", "yh"))
    field = P(GZ, GY, None)
    return jax.shard_map(
        shards,
        mesh=fine,
        in_specs=(field,) * 5 + (P(None, GZ + GY), P(), P(), P()),
        out_specs=(field,) * 5,
        check_vma=False,
    )
```

time: 48.1 us -> 45 us (0.936); the launches traced: 47.8 us -> 44.2 us
  Pallas kernels: 19 us -> 14.7 us
  waiting for transfers between devices: 7.27 us -> 4.87 us
  local copies, waits for them, and re-layouts: 0.71 us -> 2.35 us
  starting transfers between devices: 20 us -> 21.4 us
    pallas_call x6, Pallas kernels: 19 us -> 14.7 us  [the longest x1 5.11 us: shards(): call(wave_step, (block,) * 2 + (block_hbm,) * 3 + (frame,), [anywhere()]...]
    ppermute x3 -> x4, starting transfers between devices: 6.7 us -> 8.47 us  [swap(): return lax.ppermute(value, axis, pairs)]
    ppermute x3 -> x4, waiting for transfers between devices: 2.13 us -> 0.53 us  [swap(): return lax.ppermute(value, axis, pairs)]
    all_to_all x1, starting transfers between devices: 11 us -> 9.51 us  [shards(): lax.all_to_all(jnp.broadcast_to(four, (64, 128)), GZ + ('xh',), 0, 0, til...]
    ppermute x1, starting transfers between devices: 2.23 us -> 3.47 us  [swap_open(): return lax.ppermute(value, axis, pairs + [(j, i) for i, j in pairs])]
    unnamed x18 -> x14, local copies, waits for them, and re-layouts: 0.71 us -> 1.72 us
    all_to_all x1, waiting for transfers between devices: 5.13 us -> 4.34 us  [shards(): lax.all_to_all(jnp.broadcast_to(four, (64, 128)), GZ + ('xh',), 0, 0, til...]
    broadcast_in_dim x0 -> x1, local copies, waits for them, and re-layouts: none -> 0.63 us  [shards(): jnp.broadcast_to(four, (64, 128))]
  transfers between devices with their start and end apart: 5 -> 6, of which waited for: 2 -> 2; matrix products, arithmetic and copies ran while one was open for 0% -> 1% of each run, Pallas kernels for 21% -> 24%
where the time goes in v5:
time: 45 us; the launch traced here: 44.2 us
  starting transfers between devices  21.4 us (48%)
  Pallas kernels  14.7 us (33%)
  waiting for transfers between devices  4.87 us (11%)
  local copies, waits for them, and re-layouts  2.35 us (5%)
  between operations  0.83 us (2%)
    all_to_all x1, starting transfers between devices, shards(): lax.all_to_all(jnp.broadcast_to(four, (64, 128)), GZ + ('xh',), 0, 0, til...  9.51 us
    ppermute x4, starting transfers between devices, swap(): return lax.ppermute(value, axis, pairs)  8.47 us
    pallas_call x1, Pallas kernels, shards(): call(wave_step, (block,) * 2 + (block_hbm,) * 3 + (frame,), [anywhere()]...  5.11 us
    all_to_all x1, waiting for transfers between devices, shards(): lax.all_to_all(jnp.broadcast_to(four, (64, 128)), GZ + ('xh',), 0, 0, til...  4.34 us
    ppermute x1, starting transfers between devices, swap_open(): return lax.ppermute(value, axis, pairs + [(j, i) for i, j in pairs])  3.47 us
    pallas_call x1, Pallas kernels, shards(): call(list_receivers, (jax.ShapeDtypeStruct((1, 128), jnp.int32), jax.Shap...  3.42 us
    pallas_call x1, Pallas kernels, shards(): call(adjoint_step, (block,) * 3, [anywhere()] * 8, [full] * 2 + [whole] *...  2.9 us
    unnamed x14, local copies, waits for them, and re-layouts  1.72 us
  transfers between devices with their start and end apart: 6, of which 2 were waited for; matrix products, arithmetic and copies ran while one was open for 1% of the time, Pallas kernels for 24%

profile of v5, /device:TPU:1, one launch (start us, length us, event | category | flops | bytes accessed | tf_op | source)
XLA Modules:
  0.0 44.2 jit_solution(6639695626634219632)
XLA Ops:
  0.6 0.0 copy-start.3
  0.6 0.0 copy-start.2
  0.7 0.0 copy-start.4
  0.7 0.0 copy-start
  0.7 0.0 copy-start.1
  0.7 1.4 %pack_y.1 = (f32[4,16,512]{2,1,0:T(8,128)S(1)}, f32[4,16,512]{2,1,0:T(8,128)S(1)}, f32[1,128]{1,0:T(1,128)S(1)}) custom-call(f32[4,32,512]{2,1,0:T(8,128)} %u.7, f32[4,32,512]{2,1,0:T(8,128)} %a.7, f32[4,32,512]{2,1,0:T(8,128)} %u1_.7, f32[4,32,512]{2,1,0:T(8,128)} %a1.5, f32[4,32,512]{2,1,0:T(8,128)} %v.9, f32[2,16]{1,0:T(2,128)} %obs.1), custom_call_target="tpu_custom_call" | custom-call | tf_op jit(solution)/shard_map/pack_y/pallas_call | solution.py:545
  2.1 3.9 %collective-permute-start = (f32[4,16,512]{2,1,0:T(8,128)S(1)}, f32[4,16,512]{2,1,0:T(8,128)S(1)}, u32[]{:S(2)}, u32[]{:S(2)}) collective-permute-start(f32[4,16,512]{2,1,0:T(8,128)S(1)} %get-tuple-element.33), channel_id=1, source_target_pairs={{0,1},{1,0},{2,3},{3,2},{4,5},{5,4},{6,7},{7,6},{8,9},{9,8},{10,11... | collective-permute-start | bytes 393224 | tf_op jit(solution)/shard_map/ppermute | solution.py:525
  6.0 2.3 %collective-permute-start.1 = (f32[4,16,512]{2,1,0:T(8,128)S(1)}, f32[4,16,512]{2,1,0:T(8,128)S(1)}, u32[]{:S(2)}, u32[]{:S(2)}) collective-permute-start(f32[4,16,512]{2,1,0:T(8,128)S(1)} %get-tuple-element.34), channel_id=1, source_target_pairs={{0,7},{1,2},{2,1},{3,4},{4,3},{5,6},{6,5},{7,0},{8,15},{9,10},{10,... | collective-permute-start | bytes 393224 | tf_op jit(solution)/shard_map/ppermute | solution.py:525
  8.3 0.8 %copy-done.5 = s32[3,4096]{1,0:T(4,128)S(1)} copy-done((s32[3,4096]{1,0:T(4,128)S(1)}, s32[3,4096]{1,0:T(4,128)}, u32[]{:S(2)}) %copy-start.5) | copy-done | bytes 49176
  9.1 3.4 %list_receivers.1 = (s32[1,128]{1,0:T(1,128)S(1)}, s32[1,4224]{1,0:T(1,128)S(1)}) custom-call(s32[3,4096]{1,0:T(4,128)S(1)} %copy-done.5), custom_call_target="tpu_custom_call" | custom-call | tf_op jit(solution)/shard_map/list_receivers/pallas_call | solution.py:558
  12.6 0.0 collective-permute-done.rh
  12.6 0.1 collective-permute-start.2
  12.7 0.0 copy-done.3
  12.7 0.0 copy-done.2
  12.7 0.0 copy-done.4
  12.7 0.0 copy-done
  12.7 0.0 copy-done.1
  12.7 0.9 %own_step.1 = (f32[4,32,512]{2,1,0:T(8,128)S(1)}, f32[4,32,512]{2,1,0:T(8,128)S(1)}) custom-call(f32[4,32,512]{2,1,0:T(8,128)S(1)} %copy-done.1, f32[4,32,512]{2,1,0:T(8,128)S(1)} %copy-done.2, f32[4,32,512]{2,1,0:T(8,128)S(1)} %copy-done.3, f32[4,32,512]{2,1,0:T(8,128)S(1)} %copy-done.4, f32[4,32,512]{2,1,0:T(8,128)S(1)} %copy-done), custom_call_target="tpu_custom_call" | custom-call | tf_op jit(solution)/shard_map/own_step/pallas_call | solution.py:556
  13.7 0.0 collective-permute-done.1.rg
  13.7 0.9 %edge_step.1 = (f32[2,4,8,512]{3,2,1,0:T(8,128)S(1)}, f32[2,4,8,512]{3,2,1,0:T(8,128)S(1)}, f32[2,168,512]{2,1,0:T(8,128)S(1)}, f32[2,168,512]{2,1,0:T(8,128)S(1)}) custom-call(f32[4,32,512]{2,1,0:T(8,128)S(1)} %copy-done.1, f32[4,32,512]{2,1,0:T(8,128)S(1)} %copy-done.2, f32[4,32,512]{2,1,0:T(8,128)S(1)} %copy-done.3, f32[4,32,512]{2,1,0:T(8,128)S(1)} %copy-done.4, ...), custom_call_target="tpu_custom_call" | custom-call | tf_op jit(solution)/shard_map/edge_step/pallas_call | solution.py:576
  14.6 0.5 %collective-permute-done.2 = f32[1,128]{1,0:T(1,128)S(1)} collective-permute-done((f32[1,128]{1,0:T(1,128)S(1)}, f32[1,128]{1,0:T(1,128)S(1)}, u32[]{:S(2)}, u32[]{:S(2)}) %collective-permute-start.2) | collective-permute-done | bytes 544 | tf_op jit(solution)/shard_map/ppermute | solution.py:525
  15.1 2.2 %collective-permute-start.3 = (f32[2,168,512]{2,1,0:T(8,128)S(1)}, f32[2,168,512]{2,1,0:T(8,128)S(1)}, u32[]{:S(2)}, u32[]{:S(2)}) collective-permute-start(f32[2,168,512]{2,1,0:T(8,128)S(1)} %get-tuple-element.43), channel_id=1, source_target_pairs={{0,8},{8,0},{16,24},{24,16},{32,40},{40,32},{48,56},{56,48},{64,72... | collective-permute-start | bytes 2064392 | tf_op jit(solution)/shard_map/ppermute | solution.py:525
  17.3 3.5 %collective-permute-start.4 = (f32[2,168,512]{2,1,0:T(8,128)S(1)}, f32[2,168,512]{2,1,0:T(8,128)}, u32[]{:S(2)}, u32[]{:S(2)}) collective-permute-start(f32[2,168,512]{2,1,0:T(8,128)S(1)} %get-tuple-element.44), channel_id=1, source_target_pairs={{8,16},{24,32},{40,48},{56,64},{72,80},{88,96},{104,112},{120,128}... | collective-permute-start | bytes 2064392 | tf_op jit(solution)/shard_map/ppermute | solution.py:530
  20.8 0.6 %broadcast_in_dim.2 = f32[64,1,128]{2,1,0:T(1,128)} broadcast(f32[128]{0:T(128)S(1)} %bitcast.7), dimensions={2} | broadcast | bytes 33280 | tf_op jit(solution)/shard_map/broadcast_in_dim | solution.py:586
  21.4 9.5 %all-to-all-start = ((f32[64,1,128]{2,1,0:T(1,128)}), f32[64,1,128]{2,1,0:T(1,128)S(1)}, u32[]{:S(2)}, u32[]{:S(2)}) async-start(f32[64,1,128]{2,1,0:T(1,128)} %broadcast_in_dim.2), calls=%async_computation | async-start | bytes 65536 | tf_op jit(solution)/shard_map/all_to_all | solution.py:586
  30.9 0.0 collective-permute-done.3.rc
  31.0 0.0 copy-start.6
  31.0 0.0 collective-permute-done.4.rb
  31.0 0.8 %copy-done.6 = f32[2,168,512]{2,1,0:T(8,128)} copy-done((f32[2,168,512]{2,1,0:T(8,128)}, f32[2,168,512]{2,1,0:T(8,128)S(1)}, u32[]{:S(2)}) %copy-start.6) | copy-done | bytes 688152
  31.8 5.1 %wave_step.1 = (f32[4,32,512]{2,1,0:T(8,128)}, f32[4,32,512]{2,1,0:T(8,128)}, f32[4,32,512]{2,1,0:T(8,128)}, f32[4,32,512]{2,1,0:T(8,128)}, f32[4,32,512]{2,1,0:T(8,128)}, /*index=5*/f32[8,48,512]{2,1,0:T(8,128)S(1)}) custom-call(f32[4,32,512]{2,1,0:T(8,128)} %u.7, f32[4,32,512]{2,1,0:T(8,128)} %a.7, f32[4,32,512]{2,1,0:T(8,128)} %u1_.7, f32[4,32,512]{2,1,0:T(8,128)} %v.9, ...), custom_call_target="tpu_custom_call" | custom-call | tf_op jit(solution)/shard_map/wave_step/pallas_call | solution.py:588
  36.9 4.3 %all-to-all-done = f32[64,1,128]{2,1,0:T(1,128)S(1)} async-done(((f32[64,1,128]{2,1,0:T(1,128)}), f32[64,1,128]{2,1,0:T(1,128)S(1)}, u32[]{:S(2)}, u32[]{:S(2)}) %all-to-all-start) | async-done | bytes 32800 | tf_op jit(solution)/shard_map/all_to_all | solution.py:586
  41.3 2.9 %adjoint_step.1 = (f32[4,32,512]{2,1,0:T(8,128)}, f32[4,32,512]{2,1,0:T(8,128)}, f32[4,32,512]{2,1,0:T(8,128)}) custom-call(f32[4,32,512]{2,1,0:T(8,128)} %v.9, f32[8,48,512]{2,1,0:T(8,128)S(1)} %get-tuple-element.49.a0p, f32[4,32,512]{2,1,0:T(8,128)} %get-tuple-element.50.w, f32[4,32,512]{2,1,0:T(8,128)} %get-tuple-element.51.gp, ...), custom_call_target="tpu_custom_call" | custom-call | tf_op jit(solution)/shard_map/adjoint_step/pallas_call | solution.py:600
  (3 shorter events, 0.0 us)
Async XLA Ops:
  0.6 12.0 %copy-start.3 = (f32[4,32,512]{2,1,0:T(8,128)S(1)}, f32[4,32,512]{2,1,0:T(8,128)}, u32[]{:S(2)}) copy-start(f32[4,32,512]{2,1,0:T(8,128)} %u1_.7) | copy-start | bytes 786436
  0.6 12.0 %copy-start.2 = (f32[4,32,512]{2,1,0:T(8,128)S(1)}, f32[4,32,512]{2,1,0:T(8,128)}, u32[]{:S(2)}) copy-start(f32[4,32,512]{2,1,0:T(8,128)} %a.7) | copy-start | bytes 786436
  0.7 12.0 %copy-start.4 = (f32[4,32,512]{2,1,0:T(8,128)S(1)}, f32[4,32,512]{2,1,0:T(8,128)}, u32[]{:S(2)}) copy-start(f32[4,32,512]{2,1,0:T(8,128)} %a1.5) | copy-start | bytes 786436
  0.7 12.0 %copy-start = (f32[4,32,512]{2,1,0:T(8,128)S(1)}, f32[4,32,512]{2,1,0:T(8,128)}, u32[]{:S(2)}) copy-start(f32[4,32,512]{2,1,0:T(8,128)} %v.9) | copy-start | bytes 786436
  0.7 12.0 %copy-start.1 = (f32[4,32,512]{2,1,0:T(8,128)S(1)}, f32[4,32,512]{2,1,0:T(8,128)}, u32[]{:S(2)}) copy-start(f32[4,32,512]{2,1,0:T(8,128)} %u.7) | copy-start | bytes 786436
  2.1 10.5 %collective-permute-start = (f32[4,16,512]{2,1,0:T(8,128)S(1)}, f32[4,16,512]{2,1,0:T(8,128)S(1)}, u32[]{:S(2)}, u32[]{:S(2)}) collective-permute-start(f32[4,16,512]{2,1,0:T(8,128)S(1)} %get-tuple-element.33), channel_id=1, source_target_pairs={{0,1},{1,0},{2,3},{3,2},{4,5},{5,4},{6,7},{7,6},{8,9},{9,8},{10,11... | collective-permute-start | bytes 393224 | tf_op jit(solution)/shard_map/ppermute | solution.py:525
  6.0 7.7 %collective-permute-start.1 = (f32[4,16,512]{2,1,0:T(8,128)S(1)}, f32[4,16,512]{2,1,0:T(8,128)S(1)}, u32[]{:S(2)}, u32[]{:S(2)}) collective-permute-start(f32[4,16,512]{2,1,0:T(8,128)S(1)} %get-tuple-element.34), channel_id=1, source_target_pairs={{0,7},{1,2},{2,1},{3,4},{4,3},{5,6},{6,5},{7,0},{8,15},{9,10},{10,... | collective-permute-start | bytes 393224 | tf_op jit(solution)/shard_map/ppermute | solution.py:525
  8.3 0.8 %copy-start.5 = (s32[3,4096]{1,0:T(4,128)S(1)}, s32[3,4096]{1,0:T(4,128)}, u32[]{:S(2)}) copy-start(s32[3,4096]{1,0:T(4,128)} %rec.1) | copy-start | bytes 147460
  12.6 2.6 %collective-permute-start.2 = (f32[1,128]{1,0:T(1,128)S(1)}, f32[1,128]{1,0:T(1,128)S(1)}, u32[]{:S(2)}, u32[]{:S(2)}) collective-permute-start(f32[1,128]{1,0:T(1,128)S(1)} %fusion), channel_id=1, source_target_pairs={{0,2},{2,0},{1,3},{3,1},{4,6},{6,4},{5,7},{7,5},{8,10},{10,8},{9,1... | collective-permute-start | bytes 1544 | tf_op jit(solution)/shard_map/ppermute | solution.py:525
  15.1 15.8 %collective-permute-start.3 = (f32[2,168,512]{2,1,0:T(8,128)S(1)}, f32[2,168,512]{2,1,0:T(8,128)S(1)}, u32[]{:S(2)}, u32[]{:S(2)}) collective-permute-start(f32[2,168,512]{2,1,0:T(8,128)S(1)} %get-tuple-element.43), channel_id=1, source_target_pairs={{0,8},{8,0},{16,24},{24,16},{32,40},{40,32},{48,56},{56,48},{64,72... | collective-permute-start | bytes 2064392 | tf_op jit(solution)/shard_map/ppermute | solution.py:525
  17.3 13.6 %collective-permute-start.4 = (f32[2,168,512]{2,1,0:T(8,128)S(1)}, f32[2,168,512]{2,1,0:T(8,128)}, u32[]{:S(2)}, u32[]{:S(2)}) collective-permute-start(f32[2,168,512]{2,1,0:T(8,128)S(1)} %get-tuple-element.44), channel_id=1, source_target_pairs={{8,16},{24,32},{40,48},{56,64},{72,80},{88,96},{104,112},{120,128}... | collective-permute-start | bytes 2064392 | tf_op jit(solution)/shard_map/ppermute | solution.py:530
  21.4 19.9 %all-to-all-start = ((f32[64,1,128]{2,1,0:T(1,128)}), f32[64,1,128]{2,1,0:T(1,128)S(1)}, u32[]{:S(2)}, u32[]{:S(2)}) async-start(f32[64,1,128]{2,1,0:T(1,128)} %broadcast_in_dim.2), calls=%async_computation | async-start | bytes 65536 | tf_op jit(solution)/shard_map/all_to_all | solution.py:586
  31.0 0.9 %copy-start.6 = (f32[2,168,512]{2,1,0:T(8,128)}, f32[2,168,512]{2,1,0:T(8,128)S(1)}, u32[]{:S(2)}) copy-start(f32[2,168,512]{2,1,0:T(8,128)S(1)} %collective-permute-done.3.rc) | copy-start | bytes 2064388

commit v6 on v5

--- a/solution.py
+++ b/solution.py
@@ -88,13 +88,15 @@
     return tuple(zip(layers, (near_up, near_dn, far_up, far_dn)))
 
 
-def partial_laplace(f, l, s, size, factors):
+def partial_laplace(f, l, s, factors):
     u = f[l, s : s + 8, :]
+    row = lax.broadcasted_iota(jnp.int32, u.shape, 0) + s
 
     def shifted(shift):
-        if 0 <= s + shift and s + shift + 8 <= size:
+        if 0 <= s + shift and s + shift + 8 <= CY:
             return f[l, s + shift : s + shift + 8, :]
-        return pltpu.roll(u, (-shift) % 8, 0)
+        inside = (row + shift >= 0) & (row + shift < CY)
+        return jnp.where(inside, pltpu.roll(u, (-shift) % 8, 0), 0.0)
 
     near, far = x_terms(u)
     lap = CENTRE * u + NEAR * (near + (shifted(-1) + shifted(1))) + FAR * (far + (shifted(-2) + shifted(2)))
@@ -103,61 +105,20 @@
     return u, lap
 
 
-def pack_y(u, a, u1, a1, v, obs, h, g, own, first, last, obs_v, row, sem):
-    _, y0, yh, _ = place_in_mesh()
-    copies = []
-    for i, ref in enumerate((u, a, u1, a1, v)):
-        copies.append(pltpu.make_async_copy(ref.at[:, 0:8, :], first.at[i], sem.at[2 * i]))
-        copies.append(pltpu.make_async_copy(ref.at[:, CY - 8 : CY, :], last.at[i], sem.at[2 * i + 1]))
-    copies.append(pltpu.make_async_copy(obs, obs_v, sem.at[10]))
-    for copy in copies:
-        copy.start()
-    for copy in copies:
-        copy.wait()
+def own_step(u_hbm, a_hbm, u1_hbm, a1_hbm, v_hbm, obs, u0p, a0p, h, g, own, u, a, u1, a1, v, obs_v, row, sem):
+    z0, y0, yh, _ = place_in_mesh()
+    into = ((u_hbm, u), (a_hbm, a), (u1_hbm, u1), (a1_hbm, a1), (v_hbm, v), (obs, obs_v))
+    fetches = [pltpu.make_async_copy(src, dst, sem.at[i]) for i, (src, dst) in enumerate(into)]
+    for fetch in fetches:
+        fetch.start()
+    for fetch in fetches:
+        fetch.wait()
     for k in range(4):
         for t in range(2):
             row[0:1, 32 * k + 16 * t : 32 * k + 16 * t + 16] = obs_v[t : t + 1, :]
     slot = lax.broadcasted_iota(jnp.int32, (1, 128), 1) >> 5
     mine = jnp.where(slot == ((y0 // CY) & 3), row[0:1, :], 0.0)
     own[...] = mine
-
-    def pack(dst, high):
-        rows = last if high else first
-        four = slice(4, 8) if high else slice(0, 4)
-        two = slice(6, 8) if high else slice(0, 2)
-        dst[:, 0:4, :] = rows[0, :, four, :]
-        dst[:, 4:8, :] = rows[1, :, four, :]
-        dst[:, 8:10, :] = rows[2, :, two, :]
-        dst[:, 10:12, :] = rows[3, :, two, :]
-        dst[:, 12:14, :] = rows[4, :, two, :]
-        dst[:, 14:16, :] = jnp.zeros((CZ, 2, NX), jnp.float32)
-        dst[0, 14:15, 0:128] = mine
-
-    @pl.when(yh == 0)
-    def _():
-        pack(h, True)
-        pack(g, False)
-
-    @pl.when(yh != 0)
-    def _():
-        pack(h, False)
-        pack(g, True)
-
-
-def pick_y(yh, rh, rg, low, high):
-    @pl.when(yh == 0)
-    def _():
-        high(rh)
-        low(rg)
-
-    @pl.when(yh != 0)
-    def _():
-        low(rh)
-        high(rg)
-
-
-def own_step(u, a, u1, a1, v, u0p, a0p):
-    z0, _, yh, core = place_in_mesh()
 
     def layer(l, carry):
         up, dn, iu, ia = sponge(z0 + l, range(4))
@@ -166,54 +127,77 @@
             y = slice(s, s + 8)
             c = v[l, y, :] * RATIO
             c = c * c
-            p, lap = partial_laplace(u, l, s, CY, factors)
+            p, lap = partial_laplace(u, l, s, factors)
             u0p[l, y, :] = (2.0 * p - up * u1[l, y, :] + c * lap) * iu
-            q, lap = partial_laplace(a, l, s, CY, factors)
+            q, lap = partial_laplace(a, l, s, factors)
             a0p[l, y, :] = (2.0 * q - dn * a1[l, y, :] + c * lap) * ia
         return carry
 
     lax.fori_loop(0, CZ, layer, 0)
 
-
-def edge_step(
-    u, a, u1, a1, v, rh, rg, u0p, a0p, ut, at, zc, zb,
-    pu, pa, pu1, pa1, pv,
-):
+    def pack(dst, high):
+        two = slice(CY - 2, CY) if high else slice(0, 2)
+        for i, f in enumerate((u, a, u0p, a0p)):
+            dst[:, 2 * i : 2 * i + 2, 0:NX] = f[:, two, :]
+        for i in range(4):
+            dst[:, 2 * i : 2 * i + 2, NX : NX + 128] = v[:, two, 128 * i : 128 * i + 128]
+
+    @pl.when(yh == 0)
+    def _():
+        pack(h, True)
+        pack(g, False)
+
+    @pl.when(yh != 0)
+    def _():
+        pack(h, False)
+        pack(g, True)
+
+    h[:, :, NX + 128 : NX + 256] = jnp.zeros((CZ, 8, 128), jnp.float32)
+    h[0, 0:1, NX + 128 : NX + 256] = mine
+
+
+def pick_y(yh, rh, rg, low, high):
+    @pl.when(yh == 0)
+    def _():
+        high(rh)
+        low(rg)
+
+    @pl.when(yh != 0)
+    def _():
+        low(rh)
+        high(rg)
+
+
+def beyond(u):
+    row = lax.broadcasted_iota(jnp.int32, u.shape, 0)
+    near = jnp.where(row == 3, pltpu.roll(u, 7, 0), 0.0) + jnp.where(row == 4, pltpu.roll(u, 1, 0), 0.0)
+    far = jnp.where(row < 4, pltpu.roll(u, 6, 0), pltpu.roll(u, 2, 0))
+    return NEAR * near + FAR * far
+
+
+def edge_step(u, a, v, rh, rg, u0p, a0p, ut, at, zc, zb, pu, pa, pv, pu0, pa0):
     z0, _, yh, core = place_in_mesh()
-    pu[0, :, 4:8, :] = u[:, 0:4, :]
-    pu[1, :, 0:4, :] = u[:, CY - 4 : CY, :]
-    pa[0, :, 4:8, :] = a[:, 0:4, :]
-    pa[1, :, 0:4, :] = a[:, CY - 4 : CY, :]
-    for part, block in ((pu1, u1), (pa1, a1), (pv, v)):
+    parts = (pu, pa, pu0, pa0)
+    for part, block in zip(parts + (pv,), (u, a, u0p, a0p, v)):
         part[0, :, 4:6, :] = block[:, 0:2, :]
         part[1, :, 2:4, :] = block[:, CY - 2 : CY, :]
 
-    def low(r):
-        pu[0, :, 0:4, :] = r[:, 0:4, :]
-        pa[0, :, 0:4, :] = r[:, 4:8, :]
-        pu1[0, :, 2:4, :] = r[:, 8:10, :]
-        pa1[0, :, 2:4, :] = r[:, 10:12, :]
-        pv[0, :, 2:4, :] = r[:, 12:14, :]
-
-    def high(r):
-        pu[1, :, 4:8, :] = r[:, 0:4, :]
-        pa[1, :, 4:8, :] = r[:, 4:8, :]
-        pu1[1, :, 4:6, :] = r[:, 8:10, :]
-        pa1[1, :, 4:6, :] = r[:, 10:12, :]
-        pv[1, :, 4:6, :] = r[:, 12:14, :]
-
-    pick_y(yh, rh, rg, low, high)
+    def received(r, side, first):
+        rows = slice(first, first + 2)
+        for i, part in enumerate(parts):
+            part[side, :, rows, :] = r[:, 2 * i : 2 * i + 2, 0:NX]
+        for i in range(4):
+            pv[side, :, rows, 128 * i : 128 * i + 128] = r[:, 2 * i : 2 * i + 2, NX : NX + 128]
+
+    pick_y(yh, rh, rg, lambda r: received(r, 0, 2), lambda r: received(r, 1, 4))
 
     def layer(l, carry):
-        up, dn, iu, ia = sponge(z0 + l, range(4))
-        factors = depth_factors(l)
+        iu, ia = sponge(z0 + l, (2, 3))
         for side in range(2):
             c = pv[side, l] * RATIO
             c = c * c
-            p, lap = partial_laplace(pu.at[side], l, 0, 8, factors)
-            ut[side, l] = (2.0 * p - up * pu1[side, l] + c * lap) * iu
-            q, lap = partial_laplace(pa.at[side], l, 0, 8, factors)
-            at[side, l] = (2.0 * q - dn * pa1[side, l] + c * lap) * ia
+            ut[side, l] = pu0[side, l] + (c * iu) * beyond(pu[side, l])
+            at[side, l] = pa0[side, l] + (c * ia) * beyond(pa[side, l])
         return carry
 
     lax.fori_loop(0, CZ, layer, 0)
@@ -542,18 +526,15 @@
     found_smem = pltpu.SMEM((1, entries), jnp.int32)
     dmas = lambda n: pltpu.SemaphoreType.DMA((n,))
 
-    h, g, own = call(
-        pack_y,
-        (f32(CZ, 16, NX), f32(CZ, 16, NX), f32(1, 128)),
+    u0p, a0p, h, g, own = call(
+        own_step,
+        (block, block, f32(CZ, 8, NX + 256), f32(CZ, 8, NX + 128), f32(1, 128)),
         [anywhere()] * 6,
-        [pltpu.VMEM((5, CZ, 8, NX), jnp.float32)] * 2
-        + [pltpu.VMEM((2, 16), jnp.float32), pltpu.VMEM((1, 128), jnp.float32), dmas(11)],
+        [whole] * 5 + [pltpu.VMEM((2, 16), jnp.float32), pltpu.VMEM((1, 128), jnp.float32), dmas(6)],
     )(*hbm(u, a, u1, a1, v, obs))
     rh = swap(h, GY, NY_DEV, 0)
     rg = swap(g, GY, NY_DEV, 1)
-    two = own + rh[0, 14:15, 0:128]
-
-    u0p, a0p = call(own_step, (block, block), [vmem()] * 5)(u, a, u1, a1, v)
+    two = own + rh[0, 0:1, NX + 128 : NX + 256]
 
     short, long = call(
         list_receivers,
@@ -571,14 +552,13 @@
         [anywhere()] * 2,
     )(rec)
 
-    two, short, long = lax.optimization_barrier((two, short, long))
     four = two + swap(two, "xl", 2, 0)
     ut, at, zc, zb = call(
         edge_step,
         (edge,) * 2 + (pltpu.VMEM(zpack.shape, zpack.dtype),) * 2,
-        [vmem()] * 9,
+        [vmem()] * 7,
         [part] * 5,
-    )(u, a, u1, a1, v, rh, rg, u0p, a0p)
+    )(u, a, v, rh, rg, u0p, a0p)
 
     zc, zb, four = lax.optimization_barrier((zc, zb, four))
     rc = swap(zc, GZ, NZ_DEV, 0)

time: 45 us -> 44 us (0.978); the launches traced: 44.2 us -> 43.8 us
  starting transfers between devices: 21.4 us -> 22.3 us
  local copies, waits for them, and re-layouts: 2.35 us -> 1.49 us
  waiting for transfers between devices: 4.87 us -> 4.29 us
    all_to_all x1, waiting for transfers between devices: 4.34 us -> 0.65 us  [shards(): lax.all_to_all(jnp.broadcast_to(four, (64, 128)), GZ + ('xh',), 0, 0, til...]
    ppermute x4, waiting for transfers between devices: 0.53 us -> 3.64 us  [swap(): return lax.ppermute(value, axis, pairs)]
    unnamed x14 -> x10, local copies, waits for them, and re-layouts: 1.72 us -> 0.85 us
    ppermute x4, starting transfers between devices: 8.47 us -> 9.29 us  [swap(): return lax.ppermute(value, axis, pairs)]
    pallas_call x1, Pallas kernels: 0.94 us -> 0.48 us  [shards(): call(edge_step, (edge,) * 2 + (pltpu.VMEM(zpack.shape, zpack.dtype),) * 2...]
    pallas_call x2 -> x1, Pallas kernels: 2.32 us -> 2.44 us  [shards(): call(own_step, (block, block, f32(CZ, 8, NX + 256), f32(CZ, 8, NX + 128),...]
  transfers between devices with their start and end apart: 6 -> 6, of which waited for: 2 -> 2; matrix products, arithmetic and copies ran while one was open for 1% -> 1% of each run, Pallas kernels for 24% -> 21%
where the time goes in v6:
time: 44 us; the launch traced here: 43.8 us
  starting transfers between devices  22.3 us (51%)
  Pallas kernels  14.9 us (34%)
  waiting for transfers between devices  4.29 us (10%)
  local copies, waits for them, and re-layouts  1.49 us (3%)
  between operations  0.77 us (2%)
    all_to_all x1, starting transfers between devices, shards(): lax.all_to_all(jnp.broadcast_to(four, (64, 128)), GZ + ('xh',), 0, 0, til...  9.6 us
    ppermute x4, starting transfers between devices, swap(): return lax.ppermute(value, axis, pairs)  9.29 us
    pallas_call x1, Pallas kernels, shards(): call(wave_step, (block,) * 2 + (block_hbm,) * 3 + (frame,), [anywhere()]...  5.31 us
    ppermute x4, waiting for transfers between devices, swap(): return lax.ppermute(value, axis, pairs)  3.64 us
    pallas_call x1, Pallas kernels, shards(): call(list_receivers, (jax.ShapeDtypeStruct((1, 128), jnp.int32), jax.Shap...  3.49 us
    ppermute x1, starting transfers between devices, swap_open(): return lax.ppermute(value, axis, pairs + [(j, i) for i, j in pairs])  3.45 us
    pallas_call x1, Pallas kernels, shards(): call(adjoint_step, (block,) * 3, [anywhere()] * 8, [full] * 2 + [whole] *...  3.18 us
    pallas_call x1, Pallas kernels, shards(): call(own_step, (block, block, f32(CZ, 8, NX + 256), f32(CZ, 8, NX + 128),...  2.44 us
  transfers between devices with their start and end apart: 6, of which 2 were waited for; matrix products, arithmetic and copies ran while one was open for 1% of the time, Pallas kernels for 21%

profile of v6, /device:TPU:1, one launch (start us, length us, event | category | flops | bytes accessed | tf_op | source)
XLA Modules:
  0.0 43.8 jit_solution(5859877407684422439)
XLA Ops:
  0.6 0.0 copy-start.2
  0.6 0.0 copy-start
  0.7 0.0 copy-start.1
  0.7 2.4 %own_step.1 = (f32[4,32,512]{2,1,0:T(8,128)S(1)}, f32[4,32,512]{2,1,0:T(8,128)S(1)}, f32[4,8,768]{2,1,0:T(8,128)S(1)}, f32[4,8,640]{2,1,0:T(8,128)S(1)}, f32[1,128]{1,0:T(1,128)S(1)}) custom-call(f32[4,32,512]{2,1,0:T(8,128)} %u.3, f32[4,32,512]{2,1,0:T(8,128)} %a.3, f32[4,32,512]{2,1,0:T(8,128)} %u1_.1, f32[4,32,512]{2,1,0:T(8,128)} %a1_hbm.1, ...), custom_call_target="tpu_custom_call" | custom-call | tf_op jit(solution)/shard_map/own_step/pallas_call | solution.py:529
  3.1 3.8 %collective-permute-start = (f32[4,8,768]{2,1,0:T(8,128)S(1)}, f32[4,8,768]{2,1,0:T(8,128)S(1)}, u32[]{:S(2)}, u32[]{:S(2)}) collective-permute-start(f32[4,8,768]{2,1,0:T(8,128)S(1)} %get-tuple-element.30), channel_id=1, source_target_pairs={{0,1},{1,0},{2,3},{3,2},{4,5},{5,4},{6,7},{7,6},{8,9},{9,8},{10,11... | collective-permute-start | bytes 294920 | tf_op jit(solution)/shard_map/ppermute | solution.py:509
  6.9 2.3 %collective-permute-start.1 = (f32[4,8,640]{2,1,0:T(8,128)S(1)}, f32[4,8,640]{2,1,0:T(8,128)S(1)}, u32[]{:S(2)}, u32[]{:S(2)}) collective-permute-start(f32[4,8,640]{2,1,0:T(8,128)S(1)} %get-tuple-element.31), channel_id=1, source_target_pairs={{0,7},{1,2},{2,1},{3,4},{4,3},{5,6},{6,5},{7,0},{8,15},{9,10},{10,... | collective-permute-start | bytes 245768 | tf_op jit(solution)/shard_map/ppermute | solution.py:509
  9.2 0.0 collective-permute-done.rh
  9.2 1.0 %collective-permute-start.2 = (f32[1,128]{1,0:T(1,128)S(1)}, f32[1,128]{1,0:T(1,128)S(1)}, u32[]{:S(2)}, u32[]{:S(2)}) collective-permute-start(f32[1,128]{1,0:T(1,128)S(1)} %fusion), channel_id=1, source_target_pairs={{0,2},{2,0},{1,3},{3,1},{4,6},{6,4},{5,7},{7,5},{8,10},{10,8},{9,1... | collective-permute-start | bytes 1544 | tf_op jit(solution)/shard_map/ppermute | solution.py:509
  10.2 3.6 %collective-permute-done.1.rg = f32[4,8,640]{2,1,0:T(8,128)S(1)} collective-permute-done((f32[4,8,640]{2,1,0:T(8,128)S(1)}, f32[4,8,640]{2,1,0:T(8,128)S(1)}, u32[]{:S(2)}, u32[]{:S(2)}) %collective-permute-start.1) | collective-permute-done | bytes 81952 | tf_op jit(solution)/shard_map/ppermute | solution.py:509
  13.9 0.0 copy-done.2
  13.9 0.0 copy-done
  13.9 0.0 copy-done.1
  13.9 0.5 %edge_step.1 = (f32[2,4,8,512]{3,2,1,0:T(8,128)S(1)}, f32[2,4,8,512]{3,2,1,0:T(8,128)S(1)}, f32[2,168,512]{2,1,0:T(8,128)S(1)}, f32[2,168,512]{2,1,0:T(8,128)S(1)}) custom-call(f32[4,32,512]{2,1,0:T(8,128)S(1)} %copy-done.1, f32[4,32,512]{2,1,0:T(8,128)S(1)} %copy-done.2, f32[4,32,512]{2,1,0:T(8,128)S(1)} %copy-done, ...), custom_call_target="tpu_custom_call" | custom-call | tf_op jit(solution)/shard_map/edge_step/pallas_call | solution.py:556
  14.3 0.0 copy-start.3
  14.4 0.0 collective-permute-done.2
  14.4 2.2 %collective-permute-start.3 = (f32[2,168,512]{2,1,0:T(8,128)S(1)}, f32[2,168,512]{2,1,0:T(8,128)S(1)}, u32[]{:S(2)}, u32[]{:S(2)}) collective-permute-start(f32[2,168,512]{2,1,0:T(8,128)S(1)} %get-tuple-element.37), channel_id=1, source_target_pairs={{0,8},{8,0},{16,24},{24,16},{32,40},{40,32},{48,56},{56,48},{64,72... | collective-permute-start | bytes 2064392 | tf_op jit(solution)/shard_map/ppermute | solution.py:509
  16.6 3.4 %collective-permute-start.4 = (f32[2,168,512]{2,1,0:T(8,128)S(1)}, f32[2,168,512]{2,1,0:T(8,128)}, u32[]{:S(2)}, u32[]{:S(2)}) collective-permute-start(f32[2,168,512]{2,1,0:T(8,128)S(1)} %get-tuple-element.38), channel_id=1, source_target_pairs={{8,16},{24,32},{40,48},{56,64},{72,80},{88,96},{104,112},{120,128}... | collective-permute-start | bytes 2064392 | tf_op jit(solution)/shard_map/ppermute | solution.py:514
  20.0 0.6 %broadcast_in_dim.2 = f32[64,1,128]{2,1,0:T(1,128)} broadcast(f32[128]{0:T(128)S(1)} %bitcast.7), dimensions={2} | broadcast | bytes 33280 | tf_op jit(solution)/shard_map/broadcast_in_dim | solution.py:566
  20.7 9.6 %all-to-all-start = ((f32[64,1,128]{2,1,0:T(1,128)}), f32[64,1,128]{2,1,0:T(1,128)S(1)}, u32[]{:S(2)}, u32[]{:S(2)}) async-start(f32[64,1,128]{2,1,0:T(1,128)} %broadcast_in_dim.2), calls=%async_computation | async-start | bytes 65536 | tf_op jit(solution)/shard_map/all_to_all | solution.py:566
  30.3 0.0 copy-done.3
  30.3 3.5 %list_receivers.1 = (s32[1,128]{1,0:T(1,128)S(1)}, s32[1,4224]{1,0:T(1,128)S(1)}) custom-call(s32[3,4096]{1,0:T(4,128)S(1)} %copy-done.3), custom_call_target="tpu_custom_call" | custom-call | tf_op jit(solution)/shard_map/list_receivers/pallas_call | solution.py:539
  33.8 0.0 collective-permute-done.3.rc
  33.8 0.0 copy-start.4
  33.8 0.0 collective-permute-done.4.rb
  33.8 0.8 %copy-done.4 = f32[2,168,512]{2,1,0:T(8,128)} copy-done((f32[2,168,512]{2,1,0:T(8,128)}, f32[2,168,512]{2,1,0:T(8,128)S(1)}, u32[]{:S(2)}) %copy-start.4) | copy-done | bytes 688152
  34.6 5.3 %wave_step.1 = (f32[4,32,512]{2,1,0:T(8,128)}, f32[4,32,512]{2,1,0:T(8,128)}, f32[4,32,512]{2,1,0:T(8,128)}, f32[4,32,512]{2,1,0:T(8,128)}, f32[4,32,512]{2,1,0:T(8,128)}, /*index=5*/f32[8,48,512]{2,1,0:T(8,128)S(1)}) custom-call(f32[4,32,512]{2,1,0:T(8,128)} %u.3, f32[4,32,512]{2,1,0:T(8,128)} %a.3, f32[4,32,512]{2,1,0:T(8,128)} %u1_.1, f32[4,32,512]{2,1,0:T(8,128)} %v.5, ...), custom_call_target="tpu_custom_call" | custom-call | tf_op jit(solution)/shard_map/wave_step/pallas_call | solution.py:568
  40.0 0.7 %all-to-all-done = f32[64,1,128]{2,1,0:T(1,128)S(1)} async-done(((f32[64,1,128]{2,1,0:T(1,128)}), f32[64,1,128]{2,1,0:T(1,128)S(1)}, u32[]{:S(2)}, u32[]{:S(2)}) %all-to-all-start) | async-done | bytes 32800 | tf_op jit(solution)/shard_map/all_to_all | solution.py:566
  40.6 3.2 %adjoint_step.1 = (f32[4,32,512]{2,1,0:T(8,128)}, f32[4,32,512]{2,1,0:T(8,128)}, f32[4,32,512]{2,1,0:T(8,128)}) custom-call(f32[4,32,512]{2,1,0:T(8,128)} %v.5, f32[8,48,512]{2,1,0:T(8,128)S(1)} %get-tuple-element.43.a0p, f32[4,32,512]{2,1,0:T(8,128)} %get-tuple-element.44.w, f32[4,32,512]{2,1,0:T(8,128)} %get-tuple-element.45.gp, ...), custom_call_target="tpu_custom_call" | custom-call | tf_op jit(solution)/shard_map/adjoint_step/pallas_call | solution.py:580
  (2 shorter events, 0.0 us)
Async XLA Ops:
  0.6 13.2 %copy-start.2 = (f32[4,32,512]{2,1,0:T(8,128)S(1)}, f32[4,32,512]{2,1,0:T(8,128)}, u32[]{:S(2)}) copy-start(f32[4,32,512]{2,1,0:T(8,128)} %a.3) | copy-start | bytes 786436
  0.6 13.2 %copy-start = (f32[4,32,512]{2,1,0:T(8,128)S(1)}, f32[4,32,512]{2,1,0:T(8,128)}, u32[]{:S(2)}) copy-start(f32[4,32,512]{2,1,0:T(8,128)} %v.5) | copy-start | bytes 786436
  0.7 13.2 %copy-start.1 = (f32[4,32,512]{2,1,0:T(8,128)S(1)}, f32[4,32,512]{2,1,0:T(8,128)}, u32[]{:S(2)}) copy-start(f32[4,32,512]{2,1,0:T(8,128)} %u.3) | copy-start | bytes 786436
  3.1 6.1 %collective-permute-start = (f32[4,8,768]{2,1,0:T(8,128)S(1)}, f32[4,8,768]{2,1,0:T(8,128)S(1)}, u32[]{:S(2)}, u32[]{:S(2)}) collective-permute-start(f32[4,8,768]{2,1,0:T(8,128)S(1)} %get-tuple-element.30), channel_id=1, source_target_pairs={{0,1},{1,0},{2,3},{3,2},{4,5},{5,4},{6,7},{7,6},{8,9},{9,8},{10,11... | collective-permute-start | bytes 294920 | tf_op jit(solution)/shard_map/ppermute | solution.py:509
  6.9 6.9 %collective-permute-start.1 = (f32[4,8,640]{2,1,0:T(8,128)S(1)}, f32[4,8,640]{2,1,0:T(8,128)S(1)}, u32[]{:S(2)}, u32[]{:S(2)}) collective-permute-start(f32[4,8,640]{2,1,0:T(8,128)S(1)} %get-tuple-element.31), channel_id=1, source_target_pairs={{0,7},{1,2},{2,1},{3,4},{4,3},{5,6},{6,5},{7,0},{8,15},{9,10},{10,... | collective-permute-start | bytes 245768 | tf_op jit(solution)/shard_map/ppermute | solution.py:509
  9.2 5.1 %collective-permute-start.2 = (f32[1,128]{1,0:T(1,128)S(1)}, f32[1,128]{1,0:T(1,128)S(1)}, u32[]{:S(2)}, u32[]{:S(2)}) collective-permute-start(f32[1,128]{1,0:T(1,128)S(1)} %fusion), channel_id=1, source_target_pairs={{0,2},{2,0},{1,3},{3,1},{4,6},{6,4},{5,7},{7,5},{8,10},{10,8},{9,1... | collective-permute-start | bytes 1544 | tf_op jit(solution)/shard_map/ppermute | solution.py:509
  14.3 15.9 %copy-start.3 = (s32[3,4096]{1,0:T(4,128)S(1)}, s32[3,4096]{1,0:T(4,128)}, u32[]{:S(2)}) copy-start(s32[3,4096]{1,0:T(4,128)} %rec.1) | copy-start | bytes 147460
  14.4 19.4 %collective-permute-start.3 = (f32[2,168,512]{2,1,0:T(8,128)S(1)}, f32[2,168,512]{2,1,0:T(8,128)S(1)}, u32[]{:S(2)}, u32[]{:S(2)}) collective-permute-start(f32[2,168,512]{2,1,0:T(8,128)S(1)} %get-tuple-element.37), channel_id=1, source_target_pairs={{0,8},{8,0},{16,24},{24,16},{32,40},{40,32},{48,56},{56,48},{64,72... | collective-permute-start | bytes 2064392 | tf_op jit(solution)/shard_map/ppermute | solution.py:509
  16.6 17.2 %collective-permute-start.4 = (f32[2,168,512]{2,1,0:T(8,128)S(1)}, f32[2,168,512]{2,1,0:T(8,128)}, u32[]{:S(2)}, u32[]{:S(2)}) collective-permute-start(f32[2,168,512]{2,1,0:T(8,128)S(1)} %get-tuple-element.38), channel_id=1, source_target_pairs={{8,16},{24,32},{40,48},{56,64},{72,80},{88,96},{104,112},{120,128}... | collective-permute-start | bytes 2064392 | tf_op jit(solution)/shard_map/ppermute | solution.py:514
  20.7 19.9 %all-to-all-start = ((f32[64,1,128]{2,1,0:T(1,128)}), f32[64,1,128]{2,1,0:T(1,128)S(1)}, u32[]{:S(2)}, u32[]{:S(2)}) async-start(f32[64,1,128]{2,1,0:T(1,128)} %broadcast_in_dim.2), calls=%async_computation | async-start | bytes 65536 | tf_op jit(solution)/shard_map/all_to_all | solution.py:566
  33.8 0.8 %copy-start.4 = (f32[2,168,512]{2,1,0:T(8,128)}, f32[2,168,512]{2,1,0:T(8,128)S(1)}, u32[]{:S(2)}) copy-start(f32[2,168,512]{2,1,0:T(8,128)S(1)} %collective-permute-done.3.rc) | copy-start | bytes 2064388

commit v7 on v6

--- a/solution.py
+++ b/solution.py
@@ -105,10 +105,26 @@
     return u, lap
 
 
-def own_step(u_hbm, a_hbm, u1_hbm, a1_hbm, v_hbm, obs, u0p, a0p, h, g, own, u, a, u1, a1, v, obs_v, row, sem):
+def outer_laplace(f, l, factors):
+    u = f[l]
+    row = lax.broadcasted_iota(jnp.int32, u.shape, 0)
+
+    def shifted(shift):
+        return jnp.where((row + shift >= 0) & (row + shift < 8), pltpu.roll(u, (-shift) % 8, 0), 0.0)
+
+    near, far = x_terms(u)
+    lap = CENTRE * u + NEAR * (near + (shifted(-1) + shifted(1))) + FAR * (far + (shifted(-2) + shifted(2)))
+    for layer, factor in factors:
+        lap = lap + factor * f[layer]
+    return u, lap
+
+
+def pack_y(u_hbm, a_hbm, u1_hbm, a1_hbm, v_hbm, obs, h, g, own, outer, both, first_step, obs_v, row, sem):
     z0, y0, yh, _ = place_in_mesh()
-    into = ((u_hbm, u), (a_hbm, a), (u1_hbm, u1), (a1_hbm, a1), (v_hbm, v), (obs, obs_v))
-    fetches = [pltpu.make_async_copy(src, dst, sem.at[i]) for i, (src, dst) in enumerate(into)]
+    fetches = [pltpu.make_async_copy(obs, obs_v, sem.at[10])]
+    for i, f in enumerate((u_hbm, a_hbm, u1_hbm, a1_hbm, v_hbm)):
+        fetches.append(pltpu.make_async_copy(f.at[:, 0:8, :], outer.at[0, i], sem.at[2 * i]))
+        fetches.append(pltpu.make_async_copy(f.at[:, CY - 8 : CY, :], outer.at[1, i], sem.at[2 * i + 1]))
     for fetch in fetches:
         fetch.start()
     for fetch in fetches:
@@ -119,6 +135,46 @@
     slot = lax.broadcasted_iota(jnp.int32, (1, 128), 1) >> 5
     mine = jnp.where(slot == ((y0 // CY) & 3), row[0:1, :], 0.0)
     own[...] = mine
+    both[:, :, 0:4, :] = outer[0, :, :, 0:4, :]
+    both[:, :, 4:8, :] = outer[1, :, :, 4:8, :]
+
+    def layer(l, carry):
+        up, dn, iu, ia = sponge(z0 + l, range(4))
+        factors = depth_factors(l)
+        c = both[4, l] * RATIO
+        c = c * c
+        p, lap = outer_laplace(both.at[0], l, factors)
+        first_step[0, l] = (2.0 * p - up * both[2, l] + c * lap) * iu
+        q, lap = outer_laplace(both.at[1], l, factors)
+        first_step[1, l] = (2.0 * q - dn * both[3, l] + c * lap) * ia
+        return carry
+
+    lax.fori_loop(0, CZ, layer, 0)
+
+    def pack(dst, side):
+        two = slice(6, 8) if side else slice(0, 2)
+        for i in range(2):
+            dst[:, 2 * i : 2 * i + 2, 0:NX] = both[i, :, two, :]
+            dst[:, 4 + 2 * i : 6 + 2 * i, 0:NX] = first_step[i, :, two, :]
+        for i in range(4):
+            dst[:, 2 * i : 2 * i + 2, NX : NX + 128] = both[4, :, two, 128 * i : 128 * i + 128]
+
+    @pl.when(yh == 0)
+    def _():
+        pack(h, 1)
+        pack(g, 0)
+
+    @pl.when(yh != 0)
+    def _():
+        pack(h, 0)
+        pack(g, 1)
+
+    h[:, :, NX + 128 : NX + 256] = jnp.zeros((CZ, 8, 128), jnp.float32)
+    h[0, 0:1, NX + 128 : NX + 256] = mine
+
+
+def own_step(u, a, u1, a1, v, u0p, a0p):
+    z0, _, _, _ = place_in_mesh()
 
     def layer(l, carry):
         up, dn, iu, ia = sponge(z0 + l, range(4))
@@ -134,26 +190,6 @@
         return carry
 
     lax.fori_loop(0, CZ, layer, 0)
-
-    def pack(dst, high):
-        two = slice(CY - 2, CY) if high else slice(0, 2)
-        for i, f in enumerate((u, a, u0p, a0p)):
-            dst[:, 2 * i : 2 * i + 2, 0:NX] = f[:, two, :]
-        for i in range(4):
-            dst[:, 2 * i : 2 * i + 2, NX : NX + 128] = v[:, two, 128 * i : 128 * i + 128]
-
-    @pl.when(yh == 0)
-    def _():
-        pack(h, True)
-        pack(g, False)
-
-    @pl.when(yh != 0)
-    def _():
-        pack(h, False)
-        pack(g, True)
-
-    h[:, :, NX + 128 : NX + 256] = jnp.zeros((CZ, 8, 128), jnp.float32)
-    h[0, 0:1, NX + 128 : NX + 256] = mine
 
 
 def pick_y(yh, rh, rg, low, high):
@@ -308,7 +344,7 @@
 def wave_step(
     u, a, u1, v, u0p, a0p, ut, at, rc, rb, src, amp, short, long,
     u2, u0o, w, gp, ep, a0f,
-    uf, u0f, af, vf, ef, sf, u1s, corners, u2s, ws, gs, found, sem, store_sem,
+    uf, u0f, af, vf, ef, sf, u1s, corners, u2s, ws, gs, found, scales, sem, store_sem,
 ):
     e = O + CY
     z0, y0, yh, core = place_in_mesh()
@@ -397,9 +433,11 @@
         ef[l + 2, O:e, :] = -sponge(z0 + l, (1,))[0] * af[l + 2, O:e, :]
 
     def sample(r, at, z, hit):
-        a0f[at] = a0f[at] + jnp.where(hit, uf[at] * sponge(z0 + z - 2, (3,))[0], 0.0)
+        a0f[at] = a0f[at] + jnp.where(hit, uf[at] * scales[0, z], 0.0)
         ef[at] = ef[at] + jnp.where(hit, u0f[at], 0.0)
 
+    for k in range(8):
+        scales[0, k] = sponge(z0 + k - 2, (3,))[0]
     finish()
     each_receiver(found, place, sample)
 
@@ -442,28 +480,31 @@
     lax.fori_loop(0, (count + GROUP - 1) // GROUP, group, 0)
 
 
-def adjoint_step(v, a0p, w, gp, ep, short, long, table, a2, a0o, grad, a0f, ef, vs, ws, gs, a2s, a0s, found, obs, sem):
+def adjoint_step(v, a0p, w, gp, ep, short, long, table, a2, a0o, grad, a0f, ef, vs, ws, gs, a2s, a0s, found, obs, scales, sem):
     own = (slice(2, 6), slice(O, O + CY), slice(None))
-    into = ((table, obs), (ep, ef.at[own]), (a0p, a0f), (v, vs), (w, ws), (gp, gs))
+    into = ((table, obs), (ep, ef.at[own]), (v, vs), (w, ws), (gp, gs))
     fetches = [pltpu.make_async_copy(src, dst, sem.at[i]) for i, (src, dst) in enumerate(into)]
     finish = fetch_list(short, long, found, sem.at[6])
     for fetch in fetches:
         fetch.start()
     z0, _, _, _ = place_in_mesh()
     place = cell_place()
+    for k in range(8):
+        scales[0, k] = sponge(z0 + k - 2, (3,))[0]
+        a0f[k] = a0p[k]
     finish()
-    for fetch in fetches[:3]:
+    for fetch in fetches[:2]:
         fetch.wait()
 
     def subtract(r, at, z, hit):
         col = ((r >> 4) & 3) * 32 + (r & 15)
-        first = obs[r >> 6, col] * sponge(z0 + z - 2, (3,))[0]
+        first = obs[r >> 6, col] * scales[0, z]
         second = obs[r >> 6, col + 16]
         a0f[at] = a0f[at] - jnp.where(hit, first, 0.0)
         ef[at] = ef[at] - jnp.where(hit, second, 0.0)
 
     each_receiver(found, place, subtract)
-    for fetch in fetches[3:]:
+    for fetch in fetches[2:]:
         fetch.wait()
 
     stores = []
@@ -524,13 +565,15 @@
     whole = pltpu.VMEM((CZ, CY, NX), jnp.float32)
     entries = rec.shape[1] + 128
     found_smem = pltpu.SMEM((1, entries), jnp.int32)
+    eight_smem = pltpu.SMEM((1, 8), jnp.float32)
     dmas = lambda n: pltpu.SemaphoreType.DMA((n,))
 
-    u0p, a0p, h, g, own = call(
-        own_step,
-        (block, block, f32(CZ, 8, NX + 256), f32(CZ, 8, NX + 128), f32(1, 128)),
+    h, g, own = call(
+        pack_y,
+        (f32(CZ, 8, NX + 256), f32(CZ, 8, NX + 128), f32(1, 128)),
         [anywhere()] * 6,
-        [whole] * 5 + [pltpu.VMEM((2, 16), jnp.float32), pltpu.VMEM((1, 128), jnp.float32), dmas(6)],
+        [pltpu.VMEM((2, 5, CZ, 8, NX), jnp.float32), pltpu.VMEM((5, CZ, 8, NX), jnp.float32), pltpu.VMEM((2, CZ, 8, NX), jnp.float32)]
+        + [pltpu.VMEM((2, 16), jnp.float32), pltpu.VMEM((1, 128), jnp.float32), dmas(11)],
     )(*hbm(u, a, u1, a1, v, obs))
     rh = swap(h, GY, NY_DEV, 0)
     rg = swap(g, GY, NY_DEV, 1)
@@ -553,6 +596,7 @@
     )(rec)
 
     four = two + swap(two, "xl", 2, 0)
+    u0p, a0p = call(own_step, (block, block), [vmem()] * 5)(u, a, u1, a1, v)
     ut, at, zc, zb = call(
         edge_step,
         (edge,) * 2 + (pltpu.VMEM(zpack.shape, zpack.dtype),) * 2,
@@ -573,15 +617,15 @@
         + [whole] * 2
         + [pltpu.VMEM((2, 2, 8, NX), jnp.float32)]
         + [whole] * 3
-        + [found_smem, dmas(19), dmas(20)],
+        + [found_smem, eight_smem, dmas(19), dmas(20)],
         [anywhere()] * 5 + [vmem()],
     )(*hbm(u, a, u1, v), u0p, a0p, ut, at, *hbm(rc, rb, src, amp), short, long)
 
     a2, a0, grad = call(
         adjoint_step,
         (block,) * 3,
-        [anywhere()] * 8,
-        [full] * 2 + [whole] * 5 + [found_smem, pltpu.SMEM((64, 128), jnp.float32), dmas(19)],
+        [anywhere(), vmem()] + [anywhere()] * 6,
+        [full] * 2 + [whole] * 5 + [found_smem, pltpu.SMEM((64, 128), jnp.float32), eight_smem, dmas(19)],
         [anywhere()] * 3,
     )(*hbm(v), a0f, *hbm(w, gp, ep), short, long, table)
     return u2, u0, a2, a0, grad

time: 44 us -> 43.1 us (0.980)
  waiting for transfers between devices: 4.29 us -> 3.75 us
    ppermute x4, waiting for transfers between devices: 3.64 us -> 2.65 us  [swap(): return lax.ppermute(value, axis, pairs)]
    all_to_all x1, waiting for transfers between devices: 0.65 us -> 1.1 us  [shards(): lax.all_to_all(jnp.broadcast_to(four, (64, 128)), GZ + ('xh',), 0, 0, til...]
    pallas_call x2 -> x3, Pallas kernels: 5.62 us -> 5.68 us  [the longest x1 2.74 us: shards(): call(adjoint_step, (block,) * 3, [anywhere(), vmem()] + [anywhere()] * 6,...]
    unnamed x10 -> x14, local copies, waits for them, and re-layouts: 0.85 us -> 0.89 us
  transfers between devices with their start and end apart: 6 -> 6, of which waited for: 2 -> 2; matrix products, arithmetic and copies ran while one was open for 1% -> 1% of each run, Pallas kernels for 21% -> 23%
where the time goes in v7:
time: 43.1 us; the launch traced here: 42.9 us
  starting transfers between devices  22.3 us (52%)
  Pallas kernels  14.5 us (34%)
  waiting for transfers between devices  3.75 us (9%)
  local copies, waits for them, and re-layouts  1.52 us (4%)
  between operations  0.8 us (2%)
    all_to_all x1, starting transfers between devices, shards(): lax.all_to_all(jnp.broadcast_to(four, (64, 128)), GZ + ('xh',), 0, 0, til...  9.6 us
    ppermute x4, starting transfers between devices, swap(): return lax.ppermute(value, axis, pairs)  9.29 us
    pallas_call x1, Pallas kernels, shards(): call(wave_step, (block,) * 2 + (block_hbm,) * 3 + (frame,), [anywhere()]...  4.93 us
    ppermute x1, starting transfers between devices, swap_open(): return lax.ppermute(value, axis, pairs + [(j, i) for i, j in pairs])  3.45 us
    pallas_call x1, Pallas kernels, shards(): call(list_receivers, (jax.ShapeDtypeStruct((1, 128), jnp.int32), jax.Shap...  3.4 us
    pallas_call x1, Pallas kernels, shards(): call(adjoint_step, (block,) * 3, [anywhere(), vmem()] + [anywhere()] * 6,...  2.74 us
    ppermute x4, waiting for transfers between devices, swap(): return lax.ppermute(value, axis, pairs)  2.65 us
    pallas_call x1, Pallas kernels, shards(): call(pack_y, (f32(CZ, 8, NX + 256), f32(CZ, 8, NX + 128), f32(1, 128)), [...  1.99 us
  transfers between devices with their start and end apart: 6, of which 2 were waited for; matrix products, arithmetic and copies ran while one was open for 1% of the time, Pallas kernels for 23%

profile of v7, /device:TPU:1, one launch (start us, length us, event | category | flops | bytes accessed | tf_op | source)
XLA Modules:
  0.0 42.9 jit_solution(3474846314557101094)
XLA Ops:
  0.6 0.0 copy-start.3
  0.6 0.0 copy-start.2
  0.7 0.0 copy-start.4
  0.7 0.0 copy-start
  0.7 0.0 copy-start.1
  0.7 2.0 %pack_y.1 = (f32[4,8,768]{2,1,0:T(8,128)S(1)}, f32[4,8,640]{2,1,0:T(8,128)S(1)}, f32[1,128]{1,0:T(1,128)S(1)}) custom-call(f32[4,32,512]{2,1,0:T(8,128)} %u.5, f32[4,32,512]{2,1,0:T(8,128)} %a.5, f32[4,32,512]{2,1,0:T(8,128)} %u1_.3, f32[4,32,512]{2,1,0:T(8,128)} %a1_hbm.1, f32[4,32,512]{2,1,0:T(8,128)} %v.7, f32[2,16]{1,0:T(2,128)} %obs.1), custom_call_target="tpu_custom_call" | custom-call | tf_op jit(solution)/shard_map/pack_y/pallas_call | solution.py:571
  2.7 3.8 %collective-permute-start = (f32[4,8,768]{2,1,0:T(8,128)S(1)}, f32[4,8,768]{2,1,0:T(8,128)S(1)}, u32[]{:S(2)}, u32[]{:S(2)}) collective-permute-start(f32[4,8,768]{2,1,0:T(8,128)S(1)} %get-tuple-element.30), channel_id=1, source_target_pairs={{0,1},{1,0},{2,3},{3,2},{4,5},{5,4},{6,7},{7,6},{8,9},{9,8},{10,11... | collective-permute-start | bytes 294920 | tf_op jit(solution)/shard_map/ppermute | solution.py:550
  6.5 2.3 %collective-permute-start.1 = (f32[4,8,640]{2,1,0:T(8,128)S(1)}, f32[4,8,640]{2,1,0:T(8,128)S(1)}, u32[]{:S(2)}, u32[]{:S(2)}) collective-permute-start(f32[4,8,640]{2,1,0:T(8,128)S(1)} %get-tuple-element.31), channel_id=1, source_target_pairs={{0,7},{1,2},{2,1},{3,4},{4,3},{5,6},{6,5},{7,0},{8,15},{9,10},{10,... | collective-permute-start | bytes 245768 | tf_op jit(solution)/shard_map/ppermute | solution.py:550
  8.8 0.0 collective-permute-done.rh
  8.8 1.0 %collective-permute-start.2 = (f32[1,128]{1,0:T(1,128)S(1)}, f32[1,128]{1,0:T(1,128)S(1)}, u32[]{:S(2)}, u32[]{:S(2)}) collective-permute-start(f32[1,128]{1,0:T(1,128)S(1)} %fusion), channel_id=1, source_target_pairs={{0,2},{2,0},{1,3},{3,1},{4,6},{6,4},{5,7},{7,5},{8,10},{10,8},{9,1... | collective-permute-start | bytes 1544 | tf_op jit(solution)/shard_map/ppermute | solution.py:550
  9.8 0.0 copy-done.3
  9.8 0.0 copy-done.2
  9.8 0.0 copy-done.4
  9.8 0.0 copy-done
  9.8 0.0 copy-done.1
  9.8 1.0 %own_step.1 = (f32[4,32,512]{2,1,0:T(8,128)S(1)}, f32[4,32,512]{2,1,0:T(8,128)S(1)}) custom-call(f32[4,32,512]{2,1,0:T(8,128)S(1)} %copy-done.1, f32[4,32,512]{2,1,0:T(8,128)S(1)} %copy-done.2, f32[4,32,512]{2,1,0:T(8,128)S(1)} %copy-done.3, f32[4,32,512]{2,1,0:T(8,128)S(1)} %copy-done.4, f32[4,32,512]{2,1,0:T(8,128)S(1)} %copy-done), custom_call_target="tpu_custom_call" | custom-call | tf_op jit(solution)/shard_map/own_step/pallas_call | solution.py:599
  10.8 2.6 %collective-permute-done.1.rg = f32[4,8,640]{2,1,0:T(8,128)S(1)} collective-permute-done((f32[4,8,640]{2,1,0:T(8,128)S(1)}, f32[4,8,640]{2,1,0:T(8,128)S(1)}, u32[]{:S(2)}, u32[]{:S(2)}) %collective-permute-start.1) | collective-permute-done | bytes 81952 | tf_op jit(solution)/shard_map/ppermute | solution.py:550
  13.4 0.5 %edge_step.1 = (f32[2,4,8,512]{3,2,1,0:T(8,128)S(1)}, f32[2,4,8,512]{3,2,1,0:T(8,128)S(1)}, f32[2,168,512]{2,1,0:T(8,128)S(1)}, f32[2,168,512]{2,1,0:T(8,128)S(1)}) custom-call(f32[4,32,512]{2,1,0:T(8,128)S(1)} %copy-done.1, f32[4,32,512]{2,1,0:T(8,128)S(1)} %copy-done.2, f32[4,32,512]{2,1,0:T(8,128)S(1)} %copy-done, ...), custom_call_target="tpu_custom_call" | custom-call | tf_op jit(solution)/shard_map/edge_step/pallas_call | solution.py:600
  13.9 0.0 copy-start.5
  13.9 0.0 collective-permute-done.2
  13.9 2.2 %collective-permute-start.3 = (f32[2,168,512]{2,1,0:T(8,128)S(1)}, f32[2,168,512]{2,1,0:T(8,128)S(1)}, u32[]{:S(2)}, u32[]{:S(2)}) collective-permute-start(f32[2,168,512]{2,1,0:T(8,128)S(1)} %get-tuple-element.37), channel_id=1, source_target_pairs={{0,8},{8,0},{16,24},{24,16},{32,40},{40,32},{48,56},{56,48},{64,72... | collective-permute-start | bytes 2064392 | tf_op jit(solution)/shard_map/ppermute | solution.py:550
  16.1 3.4 %collective-permute-start.4 = (f32[2,168,512]{2,1,0:T(8,128)S(1)}, f32[2,168,512]{2,1,0:T(8,128)}, u32[]{:S(2)}, u32[]{:S(2)}) collective-permute-start(f32[2,168,512]{2,1,0:T(8,128)S(1)} %get-tuple-element.38), channel_id=1, source_target_pairs={{8,16},{24,32},{40,48},{56,64},{72,80},{88,96},{104,112},{120,128}... | collective-permute-start | bytes 2064392 | tf_op jit(solution)/shard_map/ppermute | solution.py:555
  19.6 0.6 %broadcast_in_dim.2 = f32[64,1,128]{2,1,0:T(1,128)} broadcast(f32[128]{0:T(128)S(1)} %bitcast.7), dimensions={2} | broadcast | bytes 33280 | tf_op jit(solution)/shard_map/broadcast_in_dim | solution.py:610
  20.2 9.6 %all-to-all-start = ((f32[64,1,128]{2,1,0:T(1,128)}), f32[64,1,128]{2,1,0:T(1,128)S(1)}, u32[]{:S(2)}, u32[]{:S(2)}) async-start(f32[64,1,128]{2,1,0:T(1,128)} %broadcast_in_dim.2), calls=%async_computation | async-start | bytes 65536 | tf_op jit(solution)/shard_map/all_to_all | solution.py:610
  29.8 0.0 copy-done.5
  29.8 3.4 %list_receivers.1 = (s32[1,128]{1,0:T(1,128)S(1)}, s32[1,4224]{1,0:T(1,128)S(1)}) custom-call(s32[3,4096]{1,0:T(4,128)S(1)} %copy-done.5), custom_call_target="tpu_custom_call" | custom-call | tf_op jit(solution)/shard_map/list_receivers/pallas_call | solution.py:582
  33.2 0.0 collective-permute-done.3.rc
  33.3 0.0 collective-permute-done.4.rb
  33.3 0.8 %copy-done.6 = f32[2,168,512]{2,1,0:T(8,128)} copy-done((f32[2,168,512]{2,1,0:T(8,128)}, f32[2,168,512]{2,1,0:T(8,128)S(1)}, u32[]{:S(2)}) %copy-start.6) | copy-done | bytes 688152
  34.1 4.9 %wave_step.1 = (f32[4,32,512]{2,1,0:T(8,128)}, f32[4,32,512]{2,1,0:T(8,128)}, f32[4,32,512]{2,1,0:T(8,128)}, f32[4,32,512]{2,1,0:T(8,128)}, f32[4,32,512]{2,1,0:T(8,128)}, /*index=5*/f32[8,48,512]{2,1,0:T(8,128)S(1)}) custom-call(f32[4,32,512]{2,1,0:T(8,128)} %u.5, f32[4,32,512]{2,1,0:T(8,128)} %a.5, f32[4,32,512]{2,1,0:T(8,128)} %u1_.3, f32[4,32,512]{2,1,0:T(8,128)} %v.7, ...), custom_call_target="tpu_custom_call" | custom-call | tf_op jit(solution)/shard_map/wave_step/pallas_call | solution.py:612
  39.1 1.1 %all-to-all-done = f32[64,1,128]{2,1,0:T(1,128)S(1)} async-done(((f32[64,1,128]{2,1,0:T(1,128)}), f32[64,1,128]{2,1,0:T(1,128)S(1)}, u32[]{:S(2)}, u32[]{:S(2)}) %all-to-all-start) | async-done | bytes 32800 | tf_op jit(solution)/shard_map/all_to_all | solution.py:610
  40.2 2.7 %adjoint_step.1 = (f32[4,32,512]{2,1,0:T(8,128)}, f32[4,32,512]{2,1,0:T(8,128)}, f32[4,32,512]{2,1,0:T(8,128)}) custom-call(f32[4,32,512]{2,1,0:T(8,128)} %v.7, f32[8,48,512]{2,1,0:T(8,128)S(1)} %get-tuple-element.43.a0p, f32[4,32,512]{2,1,0:T(8,128)} %get-tuple-element.44.w, f32[4,32,512]{2,1,0:T(8,128)} %get-tuple-element.45.gp, ...), custom_call_target="tpu_custom_call" | custom-call | tf_op jit(solution)/shard_map/adjoint_step/pallas_call | solution.py:624
  (3 shorter events, 0.0 us)
Async XLA Ops:
  0.6 9.2 %copy-start.3 = (f32[4,32,512]{2,1,0:T(8,128)S(1)}, f32[4,32,512]{2,1,0:T(8,128)}, u32[]{:S(2)}) copy-start(f32[4,32,512]{2,1,0:T(8,128)} %u1_.3) | copy-start | bytes 786436
  0.6 9.1 %copy-start.2 = (f32[4,32,512]{2,1,0:T(8,128)S(1)}, f32[4,32,512]{2,1,0:T(8,128)}, u32[]{:S(2)}) copy-start(f32[4,32,512]{2,1,0:T(8,128)} %a.5) | copy-start | bytes 786436
  0.7 9.1 %copy-start.4 = (f32[4,32,512]{2,1,0:T(8,128)S(1)}, f32[4,32,512]{2,1,0:T(8,128)}, u32[]{:S(2)}) copy-start(f32[4,32,512]{2,1,0:T(8,128)} %a1_hbm.1) | copy-start | bytes 786436
  0.7 9.1 %copy-start = (f32[4,32,512]{2,1,0:T(8,128)S(1)}, f32[4,32,512]{2,1,0:T(8,128)}, u32[]{:S(2)}) copy-start(f32[4,32,512]{2,1,0:T(8,128)} %v.7) | copy-start | bytes 786436
  0.7 9.1 %copy-start.1 = (f32[4,32,512]{2,1,0:T(8,128)S(1)}, f32[4,32,512]{2,1,0:T(8,128)}, u32[]{:S(2)}) copy-start(f32[4,32,512]{2,1,0:T(8,128)} %u.5) | copy-start | bytes 786436
  2.7 6.1 %collective-permute-start = (f32[4,8,768]{2,1,0:T(8,128)S(1)}, f32[4,8,768]{2,1,0:T(8,128)S(1)}, u32[]{:S(2)}, u32[]{:S(2)}) collective-permute-start(f32[4,8,768]{2,1,0:T(8,128)S(1)} %get-tuple-element.30), channel_id=1, source_target_pairs={{0,1},{1,0},{2,3},{3,2},{4,5},{5,4},{6,7},{7,6},{8,9},{9,8},{10,11... | collective-permute-start | bytes 294920 | tf_op jit(solution)/shard_map/ppermute | solution.py:550
  6.5 6.9 %collective-permute-start.1 = (f32[4,8,640]{2,1,0:T(8,128)S(1)}, f32[4,8,640]{2,1,0:T(8,128)S(1)}, u32[]{:S(2)}, u32[]{:S(2)}) collective-permute-start(f32[4,8,640]{2,1,0:T(8,128)S(1)} %get-tuple-element.31), channel_id=1, source_target_pairs={{0,7},{1,2},{2,1},{3,4},{4,3},{5,6},{6,5},{7,0},{8,15},{9,10},{10,... | collective-permute-start | bytes 245768 | tf_op jit(solution)/shard_map/ppermute | solution.py:550
  8.8 5.1 %collective-permute-start.2 = (f32[1,128]{1,0:T(1,128)S(1)}, f32[1,128]{1,0:T(1,128)S(1)}, u32[]{:S(2)}, u32[]{:S(2)}) collective-permute-start(f32[1,128]{1,0:T(1,128)S(1)} %fusion), channel_id=1, source_target_pairs={{0,2},{2,0},{1,3},{3,1},{4,6},{6,4},{5,7},{7,5},{8,10},{10,8},{9,1... | collective-permute-start | bytes 1544 | tf_op jit(solution)/shard_map/ppermute | solution.py:550
  13.9 15.9 %copy-start.5 = (s32[3,4096]{1,0:T(4,128)S(1)}, s32[3,4096]{1,0:T(4,128)}, u32[]{:S(2)}) copy-start(s32[3,4096]{1,0:T(4,128)} %rec.1) | copy-start | bytes 147460
  13.9 19.3 %collective-permute-start.3 = (f32[2,168,512]{2,1,0:T(8,128)S(1)}, f32[2,168,512]{2,1,0:T(8,128)S(1)}, u32[]{:S(2)}, u32[]{:S(2)}) collective-permute-start(f32[2,168,512]{2,1,0:T(8,128)S(1)} %get-tuple-element.37), channel_id=1, source_target_pairs={{0,8},{8,0},{16,24},{24,16},{32,40},{40,32},{48,56},{56,48},{64,72... | collective-permute-start | bytes 2064392 | tf_op jit(solution)/shard_map/ppermute | solution.py:550
  16.1 17.1 %collective-permute-start.4 = (f32[2,168,512]{2,1,0:T(8,128)S(1)}, f32[2,168,512]{2,1,0:T(8,128)}, u32[]{:S(2)}, u32[]{:S(2)}) collective-permute-start(f32[2,168,512]{2,1,0:T(8,128)S(1)} %get-tuple-element.38), channel_id=1, source_target_pairs={{8,16},{24,32},{40,48},{56,64},{72,80},{88,96},{104,112},{120,128}... | collective-permute-start | bytes 2064392 | tf_op jit(solution)/shard_map/ppermute | solution.py:555
  20.2 19.9 %all-to-all-start = ((f32[64,1,128]{2,1,0:T(1,128)}), f32[64,1,128]{2,1,0:T(1,128)S(1)}, u32[]{:S(2)}, u32[]{:S(2)}) async-start(f32[64,1,128]{2,1,0:T(1,128)} %broadcast_in_dim.2), calls=%async_computation | async-start | bytes 65536 | tf_op jit(solution)/shard_map/all_to_all | solution.py:610
  33.2 0.9 %copy-start.6 = (f32[2,168,512]{2,1,0:T(8,128)}, f32[2,168,512]{2,1,0:T(8,128)S(1)}, u32[]{:S(2)}) copy-start(f32[2,168,512]{2,1,0:T(8,128)S(1)} %collective-permute-done.3.rc) | copy-start | bytes 2064388

commit v8 on v7

--- a/solution.py
+++ b/solution.py
@@ -14,7 +14,7 @@
 DAMP = 0.3
 
 GZ = ("yl", "z", "c")
-GY = ("xh", "xl", "yh")
+GY = ("x", "yh")
 O = 8
 NZ_DEV, NY_DEV = 32, 8
 CZ, CY, NX = 4, 32, 512
@@ -120,7 +120,7 @@
 
 
 def pack_y(u_hbm, a_hbm, u1_hbm, a1_hbm, v_hbm, obs, h, g, own, outer, both, first_step, obs_v, row, sem):
-    z0, y0, yh, _ = place_in_mesh()
+    z0, _, yh, core = place_in_mesh()
     fetches = [pltpu.make_async_copy(obs, obs_v, sem.at[10])]
     for i, f in enumerate((u_hbm, a_hbm, u1_hbm, a1_hbm, v_hbm)):
         fetches.append(pltpu.make_async_copy(f.at[:, 0:8, :], outer.at[0, i], sem.at[2 * i]))
@@ -133,7 +133,7 @@
         for t in range(2):
             row[0:1, 32 * k + 16 * t : 32 * k + 16 * t + 16] = obs_v[t : t + 1, :]
     slot = lax.broadcasted_iota(jnp.int32, (1, 128), 1) >> 5
-    mine = jnp.where(slot == ((y0 // CY) & 3), row[0:1, :], 0.0)
+    mine = jnp.where(slot == core * 2 + yh, row[0:1, :], 0.0)
     own[...] = mine
     both[:, :, 0:4, :] = outer[0, :, :, 0:4, :]
     both[:, :, 4:8, :] = outer[1, :, :, 4:8, :]
@@ -300,7 +300,7 @@
 
         return lax.while_loop(lambda carry: carry[0] != 0, bit_step, (words[0, w], count))[1]
 
-    count = lax.fori_loop(0, 128, word_step, 0)
+    count = lax.fori_loop(0, 128, word_step, 0, unroll=8)
     found[0, 0] = count
     for k in range(GROUP - 1):
         found[0, count + 1 + k] = 0
@@ -497,9 +497,10 @@
         fetch.wait()
 
     def subtract(r, at, z, hit):
-        col = ((r >> 4) & 3) * 32 + (r & 15)
-        first = obs[r >> 6, col] * scales[0, z]
-        second = obs[r >> 6, col + 16]
+        slot = (r >> 8) * 4 + ((r >> 5) & 3)
+        col = ((r >> 7) & 1) * 64 + ((r >> 4) & 1) * 32 + (r & 15)
+        first = obs[slot, col] * scales[0, z]
+        second = obs[slot, col + 16]
         a0f[at] = a0f[at] - jnp.where(hit, first, 0.0)
         ef[at] = ef[at] - jnp.where(hit, second, 0.0)
 
@@ -595,7 +596,7 @@
         [anywhere()] * 2,
     )(rec)
 
-    four = two + swap(two, "xl", 2, 0)
+    four = two + swap(two, "c", 2, 0)
     u0p, a0p = call(own_step, (block, block), [vmem()] * 5)(u, a, u1, a1, v)
     ut, at, zc, zb = call(
         edge_step,
@@ -607,7 +608,7 @@
     zc, zb, four = lax.optimization_barrier((zc, zb, four))
     rc = swap(zc, GZ, NZ_DEV, 0)
     rb = swap_open(zb, GZ, NZ_DEV)
-    table = lax.all_to_all(jnp.broadcast_to(four, (64, 128)), GZ + ("xh",), 0, 0, tiled=True)
+    table = lax.all_to_all(jnp.broadcast_to(four, (64, 128)), ("yl", "z", "x"), 0, 0, tiled=True)
 
     u2, u0, w, gp, ep, a0f = call(
         wave_step,
@@ -632,7 +633,7 @@
 
 
 def solution(mesh):
-    fine = Mesh(mesh.devices.reshape(2, 8, 2, 2, 2, 2), ("yl", "z", "c", "xh", "xl", "yh"))
+    fine = Mesh(mesh.devices.reshape(2, 8, 2, 4, 2), ("yl", "z", "c", "x", "yh"))
     field = P(GZ, GY, None)
     return jax.shard_map(
         shards,

time: 43.1 us -> 42.4 us (0.984)
  waiting for transfers between devices: 3.75 us -> 0.85 us
  starting transfers between devices: 22.3 us -> 24.7 us
    ppermute x4, starting transfers between devices: 9.29 us -> 11.6 us  [swap(): return lax.ppermute(value, axis, pairs)]
    ppermute x4, waiting for transfers between devices: 2.65 us -> 0.3 us  [swap(): return lax.ppermute(value, axis, pairs)]
    all_to_all x1, waiting for transfers between devices: 1.1 us -> 0.54 us  [shards(): lax.all_to_all(jnp.broadcast_to(four, (64, 128)), ('yl', 'z', 'x'), 0, 0,...]
    pallas_call x1, Pallas kernels: 3.4 us -> 2.86 us  [shards(): call(list_receivers, (jax.ShapeDtypeStruct((1, 128), jnp.int32), jax.Shap...]
  transfers between devices with their start and end apart: 6 -> 6, of which waited for: 2 -> 2; matrix products, arithmetic and copies ran while one was open for 1% -> 2% of each run, Pallas kernels for 23% -> 22%
where the time goes in v8:
time: 42.4 us; the launch traced here: 42.2 us
  starting transfers between devices  24.7 us (58%)
  Pallas kernels  14.3 us (34%)
  local copies, waits for them, and re-layouts  1.52 us (4%)
  waiting for transfers between devices  0.85 us (2%)
  between operations  0.8 us (2%)
    ppermute x4, starting transfers between devices, swap(): return lax.ppermute(value, axis, pairs)  11.6 us
    all_to_all x1, starting transfers between devices, shards(): lax.all_to_all(jnp.broadcast_to(four, (64, 128)), ('yl', 'z', 'x'), 0, 0,...  9.66 us
    pallas_call x1, Pallas kernels, shards(): call(wave_step, (block,) * 2 + (block_hbm,) * 3 + (frame,), [anywhere()]...  5.03 us
    ppermute x1, starting transfers between devices, swap_open(): return lax.ppermute(value, axis, pairs + [(j, i) for i, j in pairs])  3.45 us
    pallas_call x1, Pallas kernels, shards(): call(adjoint_step, (block,) * 3, [anywhere(), vmem()] + [anywhere()] * 6,...  2.99 us
    pallas_call x1, Pallas kernels, shards(): call(list_receivers, (jax.ShapeDtypeStruct((1, 128), jnp.int32), jax.Shap...  2.86 us
    pallas_call x1, Pallas kernels, shards(): call(pack_y, (f32(CZ, 8, NX + 256), f32(CZ, 8, NX + 128), f32(1, 128)), [...  1.99 us
    pallas_call x1, Pallas kernels, shards(): u0p, a0p = call(own_step, (block, block), [vmem()] * 5)(u, a, u1, a1, v)  0.96 us
  transfers between devices with their start and end apart: 6, of which 2 were waited for; matrix products, arithmetic and copies ran while one was open for 2% of the time, Pallas kernels for 22%

profile of v8, /device:TPU:1, one launch (start us, length us, event | category | flops | bytes accessed | tf_op | source)
XLA Modules:
  0.0 42.2 jit_solution(370613394126697436)
XLA Ops:
  0.6 0.0 copy-start.3
  0.6 0.0 copy-start.2
  0.7 0.0 copy-start.4
  0.7 0.0 copy-start
  0.7 0.0 copy-start.1
  0.7 2.0 %pack_y.1 = (f32[4,8,768]{2,1,0:T(8,128)S(1)}, f32[4,8,640]{2,1,0:T(8,128)S(1)}, f32[1,128]{1,0:T(1,128)S(1)}) custom-call(f32[4,32,512]{2,1,0:T(8,128)} %u.5, f32[4,32,512]{2,1,0:T(8,128)} %a.5, f32[4,32,512]{2,1,0:T(8,128)} %u1_.3, f32[4,32,512]{2,1,0:T(8,128)} %a1_hbm.1, f32[4,32,512]{2,1,0:T(8,128)} %v.7, f32[2,16]{1,0:T(2,128)} %obs.1), custom_call_target="tpu_custom_call" | custom-call | tf_op jit(solution)/shard_map/pack_y/pallas_call | solution.py:572
  2.7 3.8 %collective-permute-start = (f32[4,8,768]{2,1,0:T(8,128)S(1)}, f32[4,8,768]{2,1,0:T(8,128)S(1)}, u32[]{:S(2)}, u32[]{:S(2)}) collective-permute-start(f32[4,8,768]{2,1,0:T(8,128)S(1)} %get-tuple-element.30), channel_id=1, source_target_pairs={{0,1},{1,0},{2,3},{3,2},{4,5},{5,4},{6,7},{7,6},{8,9},{9,8},{10,11... | collective-permute-start | bytes 294920 | tf_op jit(solution)/shard_map/ppermute | solution.py:551
  6.5 2.3 %collective-permute-start.1 = (f32[4,8,640]{2,1,0:T(8,128)S(1)}, f32[4,8,640]{2,1,0:T(8,128)S(1)}, u32[]{:S(2)}, u32[]{:S(2)}) collective-permute-start(f32[4,8,640]{2,1,0:T(8,128)S(1)} %get-tuple-element.31), channel_id=1, source_target_pairs={{0,7},{1,2},{2,1},{3,4},{4,3},{5,6},{6,5},{7,0},{8,15},{9,10},{10,... | collective-permute-start | bytes 245768 | tf_op jit(solution)/shard_map/ppermute | solution.py:551
  8.8 0.0 collective-permute-done.rh
  8.8 3.3 %collective-permute-start.2 = (f32[1,128]{1,0:T(1,128)S(1)}, f32[1,128]{1,0:T(1,128)S(1)}, u32[]{:S(2)}, u32[]{:S(2)}) collective-permute-start(f32[1,128]{1,0:T(1,128)S(1)} %fusion), channel_id=1, source_target_pairs={{0,8},{8,0},{1,9},{9,1},{2,10},{10,2},{3,11},{11,3},{4,12},{12,4},... | collective-permute-start | bytes 1544 | tf_op jit(solution)/shard_map/ppermute | solution.py:551
  12.1 0.0 copy-done.3
  12.1 0.0 copy-done.2
  12.1 0.0 copy-done.4
  12.1 0.0 copy-done
  12.1 0.0 copy-done.1
  12.2 1.0 %own_step.1 = (f32[4,32,512]{2,1,0:T(8,128)S(1)}, f32[4,32,512]{2,1,0:T(8,128)S(1)}) custom-call(f32[4,32,512]{2,1,0:T(8,128)S(1)} %copy-done.1, f32[4,32,512]{2,1,0:T(8,128)S(1)} %copy-done.2, f32[4,32,512]{2,1,0:T(8,128)S(1)} %copy-done.3, f32[4,32,512]{2,1,0:T(8,128)S(1)} %copy-done.4, f32[4,32,512]{2,1,0:T(8,128)S(1)} %copy-done), custom_call_target="tpu_custom_call" | custom-call | tf_op jit(solution)/shard_map/own_step/pallas_call | solution.py:600
  13.1 0.3 collective-permute-done.1.rg
  13.4 0.5 %edge_step.1 = (f32[2,4,8,512]{3,2,1,0:T(8,128)S(1)}, f32[2,4,8,512]{3,2,1,0:T(8,128)S(1)}, f32[2,168,512]{2,1,0:T(8,128)S(1)}, f32[2,168,512]{2,1,0:T(8,128)S(1)}) custom-call(f32[4,32,512]{2,1,0:T(8,128)S(1)} %copy-done.1, f32[4,32,512]{2,1,0:T(8,128)S(1)} %copy-done.2, f32[4,32,512]{2,1,0:T(8,128)S(1)} %copy-done, ...), custom_call_target="tpu_custom_call" | custom-call | tf_op jit(solution)/shard_map/edge_step/pallas_call | solution.py:601
  13.9 0.0 copy-start.5
  13.9 0.0 collective-permute-done.2
  13.9 2.2 %collective-permute-start.3 = (f32[2,168,512]{2,1,0:T(8,128)S(1)}, f32[2,168,512]{2,1,0:T(8,128)S(1)}, u32[]{:S(2)}, u32[]{:S(2)}) collective-permute-start(f32[2,168,512]{2,1,0:T(8,128)S(1)} %get-tuple-element.37), channel_id=1, source_target_pairs={{0,8},{8,0},{16,24},{24,16},{32,40},{40,32},{48,56},{56,48},{64,72... | collective-permute-start | bytes 2064392 | tf_op jit(solution)/shard_map/ppermute | solution.py:551
  16.1 3.4 %collective-permute-start.4 = (f32[2,168,512]{2,1,0:T(8,128)S(1)}, f32[2,168,512]{2,1,0:T(8,128)}, u32[]{:S(2)}, u32[]{:S(2)}) collective-permute-start(f32[2,168,512]{2,1,0:T(8,128)S(1)} %get-tuple-element.38), channel_id=1, source_target_pairs={{8,16},{24,32},{40,48},{56,64},{72,80},{88,96},{104,112},{120,128}... | collective-permute-start | bytes 2064392 | tf_op jit(solution)/shard_map/ppermute | solution.py:556
  19.6 0.6 %broadcast_in_dim.2 = f32[64,1,128]{2,1,0:T(1,128)} broadcast(f32[128]{0:T(128)S(1)} %bitcast.7), dimensions={2} | broadcast | bytes 33280 | tf_op jit(solution)/shard_map/broadcast_in_dim | solution.py:611
  20.2 9.7 %all-to-all-start = ((f32[64,1,128]{2,1,0:T(1,128)}), f32[64,1,128]{2,1,0:T(1,128)S(1)}, u32[]{:S(2)}, u32[]{:S(2)}) async-start(f32[64,1,128]{2,1,0:T(1,128)} %broadcast_in_dim.2), calls=%async_computation | async-start | bytes 65536 | tf_op jit(solution)/shard_map/all_to_all | solution.py:611
  29.9 0.0 copy-done.5
  29.9 2.9 %list_receivers.1 = (s32[1,128]{1,0:T(1,128)S(1)}, s32[1,4224]{1,0:T(1,128)S(1)}) custom-call(s32[3,4096]{1,0:T(4,128)S(1)} %copy-done.5), custom_call_target="tpu_custom_call" | custom-call | tf_op jit(solution)/shard_map/list_receivers/pallas_call | solution.py:583
  32.8 0.0 collective-permute-done.3.rc
  32.8 0.0 collective-permute-done.4.rb
  32.8 0.8 %copy-done.6 = f32[2,168,512]{2,1,0:T(8,128)} copy-done((f32[2,168,512]{2,1,0:T(8,128)}, f32[2,168,512]{2,1,0:T(8,128)S(1)}, u32[]{:S(2)}) %copy-start.6) | copy-done | bytes 688152
  33.6 5.0 %wave_step.1 = (f32[4,32,512]{2,1,0:T(8,128)}, f32[4,32,512]{2,1,0:T(8,128)}, f32[4,32,512]{2,1,0:T(8,128)}, f32[4,32,512]{2,1,0:T(8,128)}, f32[4,32,512]{2,1,0:T(8,128)}, /*index=5*/f32[8,48,512]{2,1,0:T(8,128)S(1)}) custom-call(f32[4,32,512]{2,1,0:T(8,128)} %u.5, f32[4,32,512]{2,1,0:T(8,128)} %a.5, f32[4,32,512]{2,1,0:T(8,128)} %u1_.3, f32[4,32,512]{2,1,0:T(8,128)} %v.7, ...), custom_call_target="tpu_custom_call" | custom-call | tf_op jit(solution)/shard_map/wave_step/pallas_call | solution.py:613
  38.7 0.5 %all-to-all-done = f32[64,1,128]{2,1,0:T(1,128)S(1)} async-done(((f32[64,1,128]{2,1,0:T(1,128)}), f32[64,1,128]{2,1,0:T(1,128)S(1)}, u32[]{:S(2)}, u32[]{:S(2)}) %all-to-all-start) | async-done | bytes 32800 | tf_op jit(solution)/shard_map/all_to_all | solution.py:611
  39.2 3.0 %adjoint_step.1 = (f32[4,32,512]{2,1,0:T(8,128)}, f32[4,32,512]{2,1,0:T(8,128)}, f32[4,32,512]{2,1,0:T(8,128)}) custom-call(f32[4,32,512]{2,1,0:T(8,128)} %v.7, f32[8,48,512]{2,1,0:T(8,128)S(1)} %get-tuple-element.43.a0p, f32[4,32,512]{2,1,0:T(8,128)} %get-tuple-element.44.w, f32[4,32,512]{2,1,0:T(8,128)} %get-tuple-element.45.gp, ...), custom_call_target="tpu_custom_call" | custom-call | tf_op jit(solution)/shard_map/adjoint_step/pallas_call | solution.py:625
  (3 shorter events, 0.0 us)
Async XLA Ops:
  0.6 11.5 %copy-start.3 = (f32[4,32,512]{2,1,0:T(8,128)S(1)}, f32[4,32,512]{2,1,0:T(8,128)}, u32[]{:S(2)}) copy-start(f32[4,32,512]{2,1,0:T(8,128)} %u1_.3) | copy-start | bytes 786436
  0.6 11.5 %copy-start.2 = (f32[4,32,512]{2,1,0:T(8,128)S(1)}, f32[4,32,512]{2,1,0:T(8,128)}, u32[]{:S(2)}) copy-start(f32[4,32,512]{2,1,0:T(8,128)} %a.5) | copy-start | bytes 786436
  0.7 11.5 %copy-start.4 = (f32[4,32,512]{2,1,0:T(8,128)S(1)}, f32[4,32,512]{2,1,0:T(8,128)}, u32[]{:S(2)}) copy-start(f32[4,32,512]{2,1,0:T(8,128)} %a1_hbm.1) | copy-start | bytes 786436
  0.7 11.5 %copy-start = (f32[4,32,512]{2,1,0:T(8,128)S(1)}, f32[4,32,512]{2,1,0:T(8,128)}, u32[]{:S(2)}) copy-start(f32[4,32,512]{2,1,0:T(8,128)} %v.7) | copy-start | bytes 786436
  0.7 11.5 %copy-start.1 = (f32[4,32,512]{2,1,0:T(8,128)S(1)}, f32[4,32,512]{2,1,0:T(8,128)}, u32[]{:S(2)}) copy-start(f32[4,32,512]{2,1,0:T(8,128)} %u.5) | copy-start | bytes 786436
  2.7 6.1 %collective-permute-start = (f32[4,8,768]{2,1,0:T(8,128)S(1)}, f32[4,8,768]{2,1,0:T(8,128)S(1)}, u32[]{:S(2)}, u32[]{:S(2)}) collective-permute-start(f32[4,8,768]{2,1,0:T(8,128)S(1)} %get-tuple-element.30), channel_id=1, source_target_pairs={{0,1},{1,0},{2,3},{3,2},{4,5},{5,4},{6,7},{7,6},{8,9},{9,8},{10,11... | collective-permute-start | bytes 294920 | tf_op jit(solution)/shard_map/ppermute | solution.py:551
  6.5 6.9 %collective-permute-start.1 = (f32[4,8,640]{2,1,0:T(8,128)S(1)}, f32[4,8,640]{2,1,0:T(8,128)S(1)}, u32[]{:S(2)}, u32[]{:S(2)}) collective-permute-start(f32[4,8,640]{2,1,0:T(8,128)S(1)} %get-tuple-element.31), channel_id=1, source_target_pairs={{0,7},{1,2},{2,1},{3,4},{4,3},{5,6},{6,5},{7,0},{8,15},{9,10},{10,... | collective-permute-start | bytes 245768 | tf_op jit(solution)/shard_map/ppermute | solution.py:551
  8.8 5.1 %collective-permute-start.2 = (f32[1,128]{1,0:T(1,128)S(1)}, f32[1,128]{1,0:T(1,128)S(1)}, u32[]{:S(2)}, u32[]{:S(2)}) collective-permute-start(f32[1,128]{1,0:T(1,128)S(1)} %fusion), channel_id=1, source_target_pairs={{0,8},{8,0},{1,9},{9,1},{2,10},{10,2},{3,11},{11,3},{4,12},{12,4},... | collective-permute-start | bytes 1544 | tf_op jit(solution)/shard_map/ppermute | solution.py:551
  13.9 16.0 %copy-start.5 = (s32[3,4096]{1,0:T(4,128)S(1)}, s32[3,4096]{1,0:T(4,128)}, u32[]{:S(2)}) copy-start(s32[3,4096]{1,0:T(4,128)} %rec.1) | copy-start | bytes 147460
  13.9 18.8 %collective-permute-start.3 = (f32[2,168,512]{2,1,0:T(8,128)S(1)}, f32[2,168,512]{2,1,0:T(8,128)S(1)}, u32[]{:S(2)}, u32[]{:S(2)}) collective-permute-start(f32[2,168,512]{2,1,0:T(8,128)S(1)} %get-tuple-element.37), channel_id=1, source_target_pairs={{0,8},{8,0},{16,24},{24,16},{32,40},{40,32},{48,56},{56,48},{64,72... | collective-permute-start | bytes 2064392 | tf_op jit(solution)/shard_map/ppermute | solution.py:551
  16.1 16.7 %collective-permute-start.4 = (f32[2,168,512]{2,1,0:T(8,128)S(1)}, f32[2,168,512]{2,1,0:T(8,128)}, u32[]{:S(2)}, u32[]{:S(2)}) collective-permute-start(f32[2,168,512]{2,1,0:T(8,128)S(1)} %get-tuple-element.38), channel_id=1, source_target_pairs={{8,16},{24,32},{40,48},{56,64},{72,80},{88,96},{104,112},{120,128}... | collective-permute-start | bytes 2064392 | tf_op jit(solution)/shard_map/ppermute | solution.py:556
  20.2 19.0 %all-to-all-start = ((f32[64,1,128]{2,1,0:T(1,128)}), f32[64,1,128]{2,1,0:T(1,128)S(1)}, u32[]{:S(2)}, u32[]{:S(2)}) async-start(f32[64,1,128]{2,1,0:T(1,128)} %broadcast_in_dim.2), calls=%async_computation | async-start | bytes 65536 | tf_op jit(solution)/shard_map/all_to_all | solution.py:611
  32.8 0.9 %copy-start.6 = (f32[2,168,512]{2,1,0:T(8,128)}, f32[2,168,512]{2,1,0:T(8,128)S(1)}, u32[]{:S(2)}) copy-start(f32[2,168,512]{2,1,0:T(8,128)S(1)} %collective-permute-done.3.rc) | copy-start | bytes 2064388

commit v9 on v8

--- a/solution.py
+++ b/solution.py
@@ -22,6 +22,7 @@
 FR = CY + 2 * O
 VMEM_LIMIT = 8 * 1024 * 1024
 ZROWS = 5 * CY + 8
+YROWS = CZ * 5 * 8
 GROUP = 4
 
 
@@ -153,11 +154,16 @@
 
     def pack(dst, side):
         two = slice(6, 8) if side else slice(0, 2)
-        for i in range(2):
-            dst[:, 2 * i : 2 * i + 2, 0:NX] = both[i, :, two, :]
-            dst[:, 4 + 2 * i : 6 + 2 * i, 0:NX] = first_step[i, :, two, :]
-        for i in range(4):
-            dst[:, 2 * i : 2 * i + 2, NX : NX + 128] = both[4, :, two, 128 * i : 128 * i + 128]
+        for l in range(CZ):
+            for t in range(5):
+                b = 8 * (5 * l + t)
+                for i in range(4):
+                    if t == 4:
+                        part = both[4, l, two, 128 * i : 128 * i + 128]
+                    else:
+                        f = both if i < 2 else first_step
+                        part = f[i % 2, l, two, 128 * t : 128 * t + 128]
+                    dst[b + 2 * i : b + 2 * i + 2, :] = part
 
     @pl.when(yh == 0)
     def _():
@@ -169,8 +175,7 @@
         pack(h, 0)
         pack(g, 1)
 
-    h[:, :, NX + 128 : NX + 256] = jnp.zeros((CZ, 8, 128), jnp.float32)
-    h[0, 0:1, NX + 128 : NX + 256] = mine
+    h[YROWS : YROWS + 8, :] = jnp.broadcast_to(mine, (8, 128))
 
 
 def own_step(u, a, u1, a1, v, u0p, a0p):
@@ -220,10 +225,12 @@
 
     def received(r, side, first):
         rows = slice(first, first + 2)
-        for i, part in enumerate(parts):
-            part[side, :, rows, :] = r[:, 2 * i : 2 * i + 2, 0:NX]
-        for i in range(4):
-            pv[side, :, rows, 128 * i : 128 * i + 128] = r[:, 2 * i : 2 * i + 2, NX : NX + 128]
+        for l in range(CZ):
+            for t in range(5):
+                b = 8 * (5 * l + t)
+                for i in range(4):
+                    part, k = (pv, i) if t == 4 else (parts[i], t)
+                    part[side, l, rows, 128 * k : 128 * k + 128] = r[b + 2 * i : b + 2 * i + 2, :]
 
     pick_y(yh, rh, rg, lambda r: received(r, 0, 2), lambda r: received(r, 1, 4))
 
@@ -571,14 +578,14 @@
 
     h, g, own = call(
         pack_y,
-        (f32(CZ, 8, NX + 256), f32(CZ, 8, NX + 128), f32(1, 128)),
+        (f32(YROWS + 8, 128), f32(YROWS, 128), f32(1, 128)),
         [anywhere()] * 6,
         [pltpu.VMEM((2, 5, CZ, 8, NX), jnp.float32), pltpu.VMEM((5, CZ, 8, NX), jnp.float32), pltpu.VMEM((2, CZ, 8, NX), jnp.float32)]
         + [pltpu.VMEM((2, 16), jnp.float32), pltpu.VMEM((1, 128), jnp.float32), dmas(11)],
     )(*hbm(u, a, u1, a1, v, obs))
     rh = swap(h, GY, NY_DEV, 0)
     rg = swap(g, GY, NY_DEV, 1)
-    two = own + rh[0, 0:1, NX + 128 : NX + 256]
+    two = own + rh[YROWS : YROWS + 1, :]
 
     short, long = call(
         list_receivers,
@@ -596,8 +603,9 @@
         [anywhere()] * 2,
     )(rec)
 
+    u0p, a0p = call(own_step, (block, block), [vmem()] * 5)(u, a, u1, a1, v)
+    two, u0p, a0p, short, long = lax.optimization_barrier((two, u0p, a0p, short, long))
     four = two + swap(two, "c", 2, 0)
-    u0p, a0p = call(own_step, (block, block), [vmem()] * 5)(u, a, u1, a1, v)
     ut, at, zc, zb = call(
         edge_step,
         (edge,) * 2 + (pltpu.VMEM(zpack.shape, zpack.dtype),) * 2,

time: 42.4 us -> 42.3 us (level)
  waiting for transfers between devices: 0.85 us -> 3.83 us
  starting transfers between devices: 24.7 us -> 21.9 us
    all_to_all x1, waiting for transfers between devices: 0.54 us -> 3.48 us  [shards(): lax.all_to_all(jnp.broadcast_to(four, (64, 128)), ('yl', 'z', 'x'), 0, 0,...]
    ppermute x4, starting transfers between devices: 11.6 us -> 8.75 us  [swap(): return lax.ppermute(value, axis, pairs)]
where the time goes in v9:
time: 42.3 us; the launch traced here: 42.1 us
  starting transfers between devices  21.9 us (52%)
  Pallas kernels  14 us (33%)
  waiting for transfers between devices  3.83 us (9%)
  local copies, waits for them, and re-layouts  1.52 us (4%)
  between operations  0.79 us (2%)
    all_to_all x1, starting transfers between devices, shards(): lax.all_to_all(jnp.broadcast_to(four, (64, 128)), ('yl', 'z', 'x'), 0, 0,...  9.66 us
    ppermute x4, starting transfers between devices, swap(): return lax.ppermute(value, axis, pairs)  8.75 us
    pallas_call x1, Pallas kernels, shards(): call(wave_step, (block,) * 2 + (block_hbm,) * 3 + (frame,), [anywhere()]...  4.97 us
    all_to_all x1, waiting for transfers between devices, shards(): lax.all_to_all(jnp.broadcast_to(four, (64, 128)), ('yl', 'z', 'x'), 0, 0,...  3.48 us
    ppermute x1, starting transfers between devices, swap_open(): return lax.ppermute(value, axis, pairs + [(j, i) for i, j in pairs])  3.45 us
    pallas_call x1, Pallas kernels, shards(): call(adjoint_step, (block,) * 3, [anywhere(), vmem()] + [anywhere()] * 6,...  2.86 us
    pallas_call x1, Pallas kernels, shards(): call(list_receivers, (jax.ShapeDtypeStruct((1, 128), jnp.int32), jax.Shap...  2.82 us
    pallas_call x1, Pallas kernels, shards(): call(pack_y, (f32(YROWS + 8, 128), f32(YROWS, 128), f32(1, 128)), [anywhe...  1.97 us
  transfers between devices with their start and end apart: 6, of which 2 were waited for; matrix products, arithmetic and copies ran while one was open for 2% of the time, Pallas kernels for 22%

profile of v9, /device:TPU:1, one launch (start us, length us, event | category | flops | bytes accessed | tf_op | source)
XLA Modules:
  0.0 42.1 jit_solution(11107820578166890)
XLA Ops:
  0.6 0.0 copy-start.3
  0.6 0.0 copy-start.2
  0.7 0.0 copy-start.4
  0.7 0.0 copy-start
  0.7 0.0 copy-start.1
  0.7 2.0 %pack_y.1 = (f32[168,128]{1,0:T(8,128)S(1)}, f32[160,128]{1,0:T(8,128)S(1)}, f32[1,128]{1,0:T(1,128)S(1)}) custom-call(f32[4,32,512]{2,1,0:T(8,128)} %u.5, f32[4,32,512]{2,1,0:T(8,128)} %a.5, f32[4,32,512]{2,1,0:T(8,128)} %u1_.3, f32[4,32,512]{2,1,0:T(8,128)} %a1.1, f32[4,32,512]{2,1,0:T(8,128)} %v.7, f32[2,16]{1,0:T(2,128)} %obs.1), custom_call_target="tpu_custom_call" | custom-call | tf_op jit(solution)/shard_map/pack_y/pallas_call | solution.py:579
  2.7 3.8 %collective-permute-start = (f32[168,128]{1,0:T(8,128)S(1)}, f32[168,128]{1,0:T(8,128)S(1)}, u32[]{:S(2)}, u32[]{:S(2)}) collective-permute-start(f32[168,128]{1,0:T(8,128)S(1)} %get-tuple-element.34), channel_id=1, source_target_pairs={{0,1},{1,0},{2,3},{3,2},{4,5},{5,4},{6,7},{7,6},{8,9},{9,8},{10,11... | collective-permute-start | bytes 258056 | tf_op jit(solution)/shard_map/ppermute | solution.py:558
  6.5 2.3 %collective-permute-start.1 = (f32[160,128]{1,0:T(8,128)S(1)}, f32[160,128]{1,0:T(8,128)S(1)}, u32[]{:S(2)}, u32[]{:S(2)}) collective-permute-start(f32[160,128]{1,0:T(8,128)S(1)} %get-tuple-element.41), channel_id=1, source_target_pairs={{0,7},{1,2},{2,1},{3,4},{4,3},{5,6},{6,5},{7,0},{8,15},{9,10},{10,... | collective-permute-start | bytes 245768 | tf_op jit(solution)/shard_map/ppermute | solution.py:558
  8.8 0.0 copy-done.3
  8.8 0.0 copy-done.2
  8.8 0.0 copy-done.4
  8.8 0.0 copy-done
  8.8 0.0 copy-done.1
  8.8 1.0 %own_step.1 = (f32[4,32,512]{2,1,0:T(8,128)S(1)}, f32[4,32,512]{2,1,0:T(8,128)S(1)}) custom-call(f32[4,32,512]{2,1,0:T(8,128)S(1)} %copy-done.1, f32[4,32,512]{2,1,0:T(8,128)S(1)} %copy-done.2, f32[4,32,512]{2,1,0:T(8,128)S(1)} %copy-done.3, f32[4,32,512]{2,1,0:T(8,128)S(1)} %copy-done.4, f32[4,32,512]{2,1,0:T(8,128)S(1)} %copy-done), custom_call_target="tpu_custom_call" | custom-call | tf_op jit(solution)/shard_map/own_step/pallas_call | solution.py:606
  9.8 0.0 copy-done.5
  9.8 2.8 %list_receivers.1 = (s32[1,128]{1,0:T(1,128)S(1)}, s32[1,4224]{1,0:T(1,128)S(1)}) custom-call(s32[3,4096]{1,0:T(4,128)S(1)} %copy-done.5), custom_call_target="tpu_custom_call" | custom-call | tf_op jit(solution)/shard_map/list_receivers/pallas_call | solution.py:590
  12.6 0.0 collective-permute-done.rh
  12.7 1.3 %collective-permute-start.2 = (f32[1,128]{1,0:T(1,128)S(1)}, f32[1,128]{1,0:T(1,128)S(1)}, u32[]{:S(2)}, u32[]{:S(2)}) collective-permute-start(f32[1,128]{1,0:T(1,128)S(1)} %slice_add_fusion), channel_id=1, source_target_pairs={{0,8},{8,0},{1,9},{9,1},{2,10},{10,2},{3,11},{11,3},{4,12},{12,4},... | collective-permute-start | bytes 1544 | tf_op jit(solution)/shard_map/ppermute | solution.py:558
  13.9 0.0 collective-permute-done.1.rg
  13.9 0.5 %edge_step.1 = (f32[2,4,8,512]{3,2,1,0:T(8,128)S(1)}, f32[2,4,8,512]{3,2,1,0:T(8,128)S(1)}, f32[2,168,512]{2,1,0:T(8,128)S(1)}, f32[2,168,512]{2,1,0:T(8,128)S(1)}) custom-call(f32[4,32,512]{2,1,0:T(8,128)S(1)} %copy-done.1, f32[4,32,512]{2,1,0:T(8,128)S(1)} %copy-done.2, f32[4,32,512]{2,1,0:T(8,128)S(1)} %copy-done, ...), custom_call_target="tpu_custom_call" | custom-call | tf_op jit(solution)/shard_map/edge_step/pallas_call | solution.py:609
  14.4 0.3 collective-permute-done.2
  14.8 1.3 %collective-permute-start.3 = (f32[2,168,512]{2,1,0:T(8,128)S(1)}, f32[2,168,512]{2,1,0:T(8,128)S(1)}, u32[]{:S(2)}, u32[]{:S(2)}) collective-permute-start(f32[2,168,512]{2,1,0:T(8,128)S(1)} %get-tuple-element.47), channel_id=1, source_target_pairs={{0,8},{8,0},{16,24},{24,16},{32,40},{40,32},{48,56},{56,48},{64,72... | collective-permute-start | bytes 2064392 | tf_op jit(solution)/shard_map/ppermute | solution.py:558
  16.1 3.4 %collective-permute-start.4 = (f32[2,168,512]{2,1,0:T(8,128)S(1)}, f32[2,168,512]{2,1,0:T(8,128)}, u32[]{:S(2)}, u32[]{:S(2)}) collective-permute-start(f32[2,168,512]{2,1,0:T(8,128)S(1)} %get-tuple-element.48), channel_id=1, source_target_pairs={{8,16},{24,32},{40,48},{56,64},{72,80},{88,96},{104,112},{120,128}... | collective-permute-start | bytes 2064392 | tf_op jit(solution)/shard_map/ppermute | solution.py:563
  19.6 0.6 %broadcast_in_dim.2 = f32[64,1,128]{2,1,0:T(1,128)} broadcast(f32[128]{0:T(128)S(1)} %bitcast.3), dimensions={2} | broadcast | bytes 33280 | tf_op jit(solution)/shard_map/broadcast_in_dim | solution.py:619
  20.2 9.7 %all-to-all-start = ((f32[64,1,128]{2,1,0:T(1,128)}), f32[64,1,128]{2,1,0:T(1,128)S(1)}, u32[]{:S(2)}, u32[]{:S(2)}) async-start(f32[64,1,128]{2,1,0:T(1,128)} %broadcast_in_dim.2), calls=%async_computation | async-start | bytes 65536 | tf_op jit(solution)/shard_map/all_to_all | solution.py:619
  29.9 0.0 collective-permute-done.3.rc
  29.9 0.0 copy-start.6
  29.9 0.0 collective-permute-done.4.rb
  29.9 0.8 %copy-done.6 = f32[2,168,512]{2,1,0:T(8,128)} copy-done((f32[2,168,512]{2,1,0:T(8,128)}, f32[2,168,512]{2,1,0:T(8,128)S(1)}, u32[]{:S(2)}) %copy-start.6) | copy-done | bytes 688152
  30.7 5.0 %wave_step.1 = (f32[4,32,512]{2,1,0:T(8,128)}, f32[4,32,512]{2,1,0:T(8,128)}, f32[4,32,512]{2,1,0:T(8,128)}, f32[4,32,512]{2,1,0:T(8,128)}, f32[4,32,512]{2,1,0:T(8,128)}, /*index=5*/f32[8,48,512]{2,1,0:T(8,128)S(1)}) custom-call(f32[4,32,512]{2,1,0:T(8,128)} %u.5, f32[4,32,512]{2,1,0:T(8,128)} %a.5, f32[4,32,512]{2,1,0:T(8,128)} %u1_.3, f32[4,32,512]{2,1,0:T(8,128)} %v.7, ...), custom_call_target="tpu_custom_call" | custom-call | tf_op jit(solution)/shard_map/wave_step/pallas_call | solution.py:621
  35.7 3.5 %all-to-all-done = f32[64,1,128]{2,1,0:T(1,128)S(1)} async-done(((f32[64,1,128]{2,1,0:T(1,128)}), f32[64,1,128]{2,1,0:T(1,128)S(1)}, u32[]{:S(2)}, u32[]{:S(2)}) %all-to-all-start) | async-done | bytes 32800 | tf_op jit(solution)/shard_map/all_to_all | solution.py:619
  39.2 2.9 %adjoint_step.1 = (f32[4,32,512]{2,1,0:T(8,128)}, f32[4,32,512]{2,1,0:T(8,128)}, f32[4,32,512]{2,1,0:T(8,128)}) custom-call(f32[4,32,512]{2,1,0:T(8,128)} %v.7, f32[8,48,512]{2,1,0:T(8,128)S(1)} %get-tuple-element.53.a0p, f32[4,32,512]{2,1,0:T(8,128)} %get-tuple-element.54.w, f32[4,32,512]{2,1,0:T(8,128)} %get-tuple-element.55.gp, ...), custom_call_target="tpu_custom_call" | custom-call | tf_op jit(solution)/shard_map/adjoint_step/pallas_call | solution.py:633
  (3 shorter events, 0.0 us)
Async XLA Ops:
  0.6 8.2 %copy-start.3 = (f32[4,32,512]{2,1,0:T(8,128)S(1)}, f32[4,32,512]{2,1,0:T(8,128)}, u32[]{:S(2)}) copy-start(f32[4,32,512]{2,1,0:T(8,128)} %u1_.3) | copy-start | bytes 786436
  0.6 8.2 %copy-start.2 = (f32[4,32,512]{2,1,0:T(8,128)S(1)}, f32[4,32,512]{2,1,0:T(8,128)}, u32[]{:S(2)}) copy-start(f32[4,32,512]{2,1,0:T(8,128)} %a.5) | copy-start | bytes 786436
  0.7 8.2 %copy-start.4 = (f32[4,32,512]{2,1,0:T(8,128)S(1)}, f32[4,32,512]{2,1,0:T(8,128)}, u32[]{:S(2)}) copy-start(f32[4,32,512]{2,1,0:T(8,128)} %a1.1) | copy-start | bytes 786436
  0.7 8.2 %copy-start = (f32[4,32,512]{2,1,0:T(8,128)S(1)}, f32[4,32,512]{2,1,0:T(8,128)}, u32[]{:S(2)}) copy-start(f32[4,32,512]{2,1,0:T(8,128)} %v.7) | copy-start | bytes 786436
  0.7 8.1 %copy-start.1 = (f32[4,32,512]{2,1,0:T(8,128)S(1)}, f32[4,32,512]{2,1,0:T(8,128)}, u32[]{:S(2)}) copy-start(f32[4,32,512]{2,1,0:T(8,128)} %u.5) | copy-start | bytes 786436
  2.7 10.0 %collective-permute-start = (f32[168,128]{1,0:T(8,128)S(1)}, f32[168,128]{1,0:T(8,128)S(1)}, u32[]{:S(2)}, u32[]{:S(2)}) collective-permute-start(f32[168,128]{1,0:T(8,128)S(1)} %get-tuple-element.34), channel_id=1, source_target_pairs={{0,1},{1,0},{2,3},{3,2},{4,5},{5,4},{6,7},{7,6},{8,9},{9,8},{10,11... | collective-permute-start | bytes 258056 | tf_op jit(solution)/shard_map/ppermute | solution.py:558
  6.5 3.3 %copy-start.5 = (s32[3,4096]{1,0:T(4,128)S(1)}, s32[3,4096]{1,0:T(4,128)}, u32[]{:S(2)}) copy-start(s32[3,4096]{1,0:T(4,128)} %rec.1) | copy-start | bytes 147460
  6.5 7.4 %collective-permute-start.1 = (f32[160,128]{1,0:T(8,128)S(1)}, f32[160,128]{1,0:T(8,128)S(1)}, u32[]{:S(2)}, u32[]{:S(2)}) collective-permute-start(f32[160,128]{1,0:T(8,128)S(1)} %get-tuple-element.41), channel_id=1, source_target_pairs={{0,7},{1,2},{2,1},{3,4},{4,3},{5,6},{6,5},{7,0},{8,15},{9,10},{10,... | collective-permute-start | bytes 245768 | tf_op jit(solution)/shard_map/ppermute | solution.py:558
  12.7 2.1 %collective-permute-start.2 = (f32[1,128]{1,0:T(1,128)S(1)}, f32[1,128]{1,0:T(1,128)S(1)}, u32[]{:S(2)}, u32[]{:S(2)}) collective-permute-start(f32[1,128]{1,0:T(1,128)S(1)} %slice_add_fusion), channel_id=1, source_target_pairs={{0,8},{8,0},{1,9},{9,1},{2,10},{10,2},{3,11},{11,3},{4,12},{12,4},... | collective-permute-start | bytes 1544 | tf_op jit(solution)/shard_map/ppermute | solution.py:558
  14.8 15.1 %collective-permute-start.3 = (f32[2,168,512]{2,1,0:T(8,128)S(1)}, f32[2,168,512]{2,1,0:T(8,128)S(1)}, u32[]{:S(2)}, u32[]{:S(2)}) collective-permute-start(f32[2,168,512]{2,1,0:T(8,128)S(1)} %get-tuple-element.47), channel_id=1, source_target_pairs={{0,8},{8,0},{16,24},{24,16},{32,40},{40,32},{48,56},{56,48},{64,72... | collective-permute-start | bytes 2064392 | tf_op jit(solution)/shard_map/ppermute | solution.py:558
  16.1 13.8 %collective-permute-start.4 = (f32[2,168,512]{2,1,0:T(8,128)S(1)}, f32[2,168,512]{2,1,0:T(8,128)}, u32[]{:S(2)}, u32[]{:S(2)}) collective-permute-start(f32[2,168,512]{2,1,0:T(8,128)S(1)} %get-tuple-element.48), channel_id=1, source_target_pairs={{8,16},{24,32},{40,48},{56,64},{72,80},{88,96},{104,112},{120,128}... | collective-permute-start | bytes 2064392 | tf_op jit(solution)/shard_map/ppermute | solution.py:563
  20.2 19.0 %all-to-all-start = ((f32[64,1,128]{2,1,0:T(1,128)}), f32[64,1,128]{2,1,0:T(1,128)S(1)}, u32[]{:S(2)}, u32[]{:S(2)}) async-start(f32[64,1,128]{2,1,0:T(1,128)} %broadcast_in_dim.2), calls=%async_computation | async-start | bytes 65536 | tf_op jit(solution)/shard_map/all_to_all | solution.py:619
  29.9 0.9 %copy-start.6 = (f32[2,168,512]{2,1,0:T(8,128)}, f32[2,168,512]{2,1,0:T(8,128)S(1)}, u32[]{:S(2)}) copy-start(f32[2,168,512]{2,1,0:T(8,128)S(1)} %collective-permute-done.3.rc) | copy-start | bytes 2064388

commit v10 on v9

--- a/solution.py
+++ b/solution.py
@@ -23,7 +23,7 @@
 VMEM_LIMIT = 8 * 1024 * 1024
 ZROWS = 5 * CY + 8
 YROWS = CZ * 5 * 8
-GROUP = 4
+GROUP = 8
 
 
 def sponge_table():
@@ -487,7 +487,7 @@
     lax.fori_loop(0, (count + GROUP - 1) // GROUP, group, 0)
 
 
-def adjoint_step(v, a0p, w, gp, ep, short, long, table, a2, a0o, grad, a0f, ef, vs, ws, gs, a2s, a0s, found, obs, scales, sem):
+def adjoint_step(v, a0p, w, gp, ep, short, long, table, a2, a0o, grad, a0f, ef, vs, ws, gs, a2s, found, obs, scales, sem):
     own = (slice(2, 6), slice(O, O + CY), slice(None))
     into = ((table, obs), (ep, ef.at[own]), (v, vs), (w, ws), (gp, gs))
     fetches = [pltpu.make_async_copy(src, dst, sem.at[i]) for i, (src, dst) in enumerate(into)]
@@ -512,10 +512,14 @@
         ef[at] = ef[at] - jnp.where(hit, second, 0.0)
 
     each_receiver(found, place, subtract)
+    stores = [
+        pltpu.make_async_copy(a0f.at[l + 2, O : O + CY, :], a0o.at[l], sem.at[7 + 3 * l + 2]) for l in range(CZ)
+    ]
+    for store in stores:
+        store.start()
     for fetch in fetches[2:]:
         fetch.wait()
 
-    stores = []
     for l in range(CZ):
         ia = sponge(z0 + l, (3,))[0]
         for s in range(O, O + CY, 8):
@@ -524,10 +528,9 @@
             c = c * c
             q, lap = laplace(a0f, l + 2, s)
             a2s[l, y, :] = (2.0 * q + ef[l + 2, s : s + 8, :] + c * lap) * ia
-            a0s[l, y, :] = q
             gs[l, y, :] = gs[l, y, :] + ws[l, y, :] * q
-        for i, (src, dst) in enumerate(((a2s, a2), (a0s, a0o), (gs, grad))):
-            stores.append(pltpu.make_async_copy(src.at[l], dst.at[l], sem.at[7 + 3 * l + i]))
+        for i, (src, dst) in enumerate(((a2s.at[l], a2), (gs.at[l], grad))):
+            stores.append(pltpu.make_async_copy(src, dst.at[l], sem.at[7 + 3 * l + i]))
             stores[-1].start()
     for store in stores:
         store.wait()
@@ -613,8 +616,8 @@
         [part] * 5,
     )(u, a, v, rh, rg, u0p, a0p)
 
-    zc, zb, four = lax.optimization_barrier((zc, zb, four))
     rc = swap(zc, GZ, NZ_DEV, 0)
+    zb, four = lax.optimization_barrier((zb, four))
     rb = swap_open(zb, GZ, NZ_DEV)
     table = lax.all_to_all(jnp.broadcast_to(four, (64, 128)), ("yl", "z", "x"), 0, 0, tiled=True)
 
@@ -634,7 +637,7 @@
         adjoint_step,
         (block,) * 3,
         [anywhere(), vmem()] + [anywhere()] * 6,
-        [full] * 2 + [whole] * 5 + [found_smem, pltpu.SMEM((64, 128), jnp.float32), eight_smem, dmas(19)],
+        [full] * 2 + [whole] * 4 + [found_smem, pltpu.SMEM((64, 128), jnp.float32), eight_smem, dmas(19)],
         [anywhere()] * 3,
     )(*hbm(v), a0f, *hbm(w, gp, ep), short, long, table)
     return u2, u0, a2, a0, grad

time: 42.3 us -> 42.3 us (level)
  transfers between devices with their start and end apart: 6 -> 6, of which waited for: 2 -> 1; matrix products, arithmetic and copies ran while one was open for 2% -> 2% of each run, Pallas kernels for 22% -> 22%
where the time goes in v10:
time: 42.3 us; the launch traced here: 42.1 us
  starting transfers between devices  22.2 us (52%)
  Pallas kernels  14.2 us (34%)
  waiting for transfers between devices  3.46 us (8%)
  local copies, waits for them, and re-layouts  1.52 us (4%)
  between operations  0.79 us (2%)
    all_to_all x1, starting transfers between devices, shards(): lax.all_to_all(jnp.broadcast_to(four, (64, 128)), ('yl', 'z', 'x'), 0, 0,...  9.66 us
    ppermute x4, starting transfers between devices, swap(): return lax.ppermute(value, axis, pairs)  9.04 us
    pallas_call x1, Pallas kernels, shards(): call(wave_step, (block,) * 2 + (block_hbm,) * 3 + (frame,), [anywhere()]...  5.01 us
    ppermute x1, starting transfers between devices, swap_open(): return lax.ppermute(value, axis, pairs + [(j, i) for i, j in pairs])  3.46 us
    all_to_all x1, waiting for transfers between devices, shards(): lax.all_to_all(jnp.broadcast_to(four, (64, 128)), ('yl', 'z', 'x'), 0, 0,...  3.44 us
    pallas_call x1, Pallas kernels, shards(): call(adjoint_step, (block,) * 3, [anywhere(), vmem()] + [anywhere()] * 6,...  2.93 us
    pallas_call x1, Pallas kernels, shards(): call(list_receivers, (jax.ShapeDtypeStruct((1, 128), jnp.int32), jax.Shap...  2.86 us
    pallas_call x1, Pallas kernels, shards(): call(pack_y, (f32(YROWS + 8, 128), f32(YROWS, 128), f32(1, 128)), [anywhe...  1.97 us
  transfers between devices with their start and end apart: 6, of which 1 were waited for; matrix products, arithmetic and copies ran while one was open for 2% of the time, Pallas kernels for 22%

profile of v10, /device:TPU:1, one launch (start us, length us, event | category | flops | bytes accessed | tf_op | source)
XLA Modules:
  0.0 42.1 jit_solution(3598196262134639498)
XLA Ops:
  0.6 0.0 copy-start.3
  0.6 0.0 copy-start.2
  0.7 0.0 copy-start.4
  0.7 0.0 copy-start
  0.7 0.0 copy-start.1
  0.7 2.0 %pack_y.1 = (f32[168,128]{1,0:T(8,128)S(1)}, f32[160,128]{1,0:T(8,128)S(1)}, f32[1,128]{1,0:T(1,128)S(1)}) custom-call(f32[4,32,512]{2,1,0:T(8,128)} %u.5, f32[4,32,512]{2,1,0:T(8,128)} %a.5, f32[4,32,512]{2,1,0:T(8,128)} %u1_.3, f32[4,32,512]{2,1,0:T(8,128)} %a1.1, f32[4,32,512]{2,1,0:T(8,128)} %v.7, f32[2,16]{1,0:T(2,128)} %obs.1), custom_call_target="tpu_custom_call" | custom-call | tf_op jit(solution)/shard_map/pack_y/pallas_call | solution.py:582
  2.7 3.8 %collective-permute-start = (f32[168,128]{1,0:T(8,128)S(1)}, f32[168,128]{1,0:T(8,128)S(1)}, u32[]{:S(2)}, u32[]{:S(2)}) collective-permute-start(f32[168,128]{1,0:T(8,128)S(1)} %get-tuple-element.33), channel_id=1, source_target_pairs={{0,1},{1,0},{2,3},{3,2},{4,5},{5,4},{6,7},{7,6},{8,9},{9,8},{10,11... | collective-permute-start | bytes 258056 | tf_op jit(solution)/shard_map/ppermute | solution.py:561
  6.5 2.3 %collective-permute-start.1 = (f32[160,128]{1,0:T(8,128)S(1)}, f32[160,128]{1,0:T(8,128)S(1)}, u32[]{:S(2)}, u32[]{:S(2)}) collective-permute-start(f32[160,128]{1,0:T(8,128)S(1)} %get-tuple-element.40), channel_id=1, source_target_pairs={{0,7},{1,2},{2,1},{3,4},{4,3},{5,6},{6,5},{7,0},{8,15},{9,10},{10,... | collective-permute-start | bytes 245768 | tf_op jit(solution)/shard_map/ppermute | solution.py:561
  8.8 0.0 copy-done.3
  8.8 0.0 copy-done.2
  8.8 0.0 copy-done.4
  8.8 0.0 copy-done
  8.8 0.0 copy-done.1
  8.8 1.0 %own_step.1 = (f32[4,32,512]{2,1,0:T(8,128)S(1)}, f32[4,32,512]{2,1,0:T(8,128)S(1)}) custom-call(f32[4,32,512]{2,1,0:T(8,128)S(1)} %copy-done.1, f32[4,32,512]{2,1,0:T(8,128)S(1)} %copy-done.2, f32[4,32,512]{2,1,0:T(8,128)S(1)} %copy-done.3, f32[4,32,512]{2,1,0:T(8,128)S(1)} %copy-done.4, f32[4,32,512]{2,1,0:T(8,128)S(1)} %copy-done), custom_call_target="tpu_custom_call" | custom-call | tf_op jit(solution)/shard_map/own_step/pallas_call | solution.py:609
  9.8 0.0 copy-done.5
  9.8 2.9 %list_receivers.1 = (s32[1,128]{1,0:T(1,128)S(1)}, s32[1,4224]{1,0:T(1,128)S(1)}) custom-call(s32[3,4096]{1,0:T(4,128)S(1)} %copy-done.5), custom_call_target="tpu_custom_call" | custom-call | tf_op jit(solution)/shard_map/list_receivers/pallas_call | solution.py:593
  12.7 0.0 collective-permute-done.rh
  12.7 1.2 %collective-permute-start.3 = (f32[1,128]{1,0:T(1,128)S(1)}, f32[1,128]{1,0:T(1,128)S(1)}, u32[]{:S(2)}, u32[]{:S(2)}) collective-permute-start(f32[1,128]{1,0:T(1,128)S(1)} %slice_add_fusion), channel_id=1, source_target_pairs={{0,8},{8,0},{1,9},{9,1},{2,10},{10,2},{3,11},{11,3},{4,12},{12,4},... | collective-permute-start | bytes 1544 | tf_op jit(solution)/shard_map/ppermute | solution.py:561
  13.9 0.0 collective-permute-done.1.rg
  13.9 0.5 %edge_step.1 = (f32[2,4,8,512]{3,2,1,0:T(8,128)S(1)}, f32[2,4,8,512]{3,2,1,0:T(8,128)S(1)}, f32[2,168,512]{2,1,0:T(8,128)S(1)}, f32[2,168,512]{2,1,0:T(8,128)S(1)}) custom-call(f32[4,32,512]{2,1,0:T(8,128)S(1)} %copy-done.1, f32[4,32,512]{2,1,0:T(8,128)S(1)} %copy-done.2, f32[4,32,512]{2,1,0:T(8,128)S(1)} %copy-done, ...), custom_call_target="tpu_custom_call" | custom-call | tf_op jit(solution)/shard_map/edge_step/pallas_call | solution.py:612
  14.4 1.7 %collective-permute-start.2 = (f32[2,168,512]{2,1,0:T(8,128)S(1)}, f32[2,168,512]{2,1,0:T(8,128)S(1)}, u32[]{:S(2)}, u32[]{:S(2)}) collective-permute-start(f32[2,168,512]{2,1,0:T(8,128)S(1)} %get-tuple-element.43), channel_id=1, source_target_pairs={{0,8},{8,0},{16,24},{24,16},{32,40},{40,32},{48,56},{56,48},{64,72... | collective-permute-start | bytes 2064392 | tf_op jit(solution)/shard_map/ppermute | solution.py:561
  16.1 0.0 collective-permute-done.3
  16.1 3.5 %collective-permute-start.4 = (f32[2,168,512]{2,1,0:T(8,128)S(1)}, f32[2,168,512]{2,1,0:T(8,128)}, u32[]{:S(2)}, u32[]{:S(2)}) collective-permute-start(f32[2,168,512]{2,1,0:T(8,128)S(1)} %get-tuple-element.46), channel_id=1, source_target_pairs={{8,16},{24,32},{40,48},{56,64},{72,80},{88,96},{104,112},{120,128}... | collective-permute-start | bytes 2064392 | tf_op jit(solution)/shard_map/ppermute | solution.py:566
  19.6 0.6 %broadcast_in_dim.2 = f32[64,1,128]{2,1,0:T(1,128)} broadcast(f32[128]{0:T(128)S(1)} %bitcast.3), dimensions={2} | broadcast | bytes 33280 | tf_op jit(solution)/shard_map/broadcast_in_dim | solution.py:622
  20.2 9.7 %all-to-all-start = ((f32[64,1,128]{2,1,0:T(1,128)}), f32[64,1,128]{2,1,0:T(1,128)S(1)}, u32[]{:S(2)}, u32[]{:S(2)}) async-start(f32[64,1,128]{2,1,0:T(1,128)} %broadcast_in_dim.2), calls=%async_computation | async-start | bytes 65536 | tf_op jit(solution)/shard_map/all_to_all | solution.py:622
  29.9 0.0 collective-permute-done.2.rc
  29.9 0.0 copy-start.6
  29.9 0.0 collective-permute-done.4.rb
  29.9 0.8 %copy-done.6 = f32[2,168,512]{2,1,0:T(8,128)} copy-done((f32[2,168,512]{2,1,0:T(8,128)}, f32[2,168,512]{2,1,0:T(8,128)S(1)}, u32[]{:S(2)}) %copy-start.6) | copy-done | bytes 688152
  30.7 5.0 %wave_step.1 = (f32[4,32,512]{2,1,0:T(8,128)}, f32[4,32,512]{2,1,0:T(8,128)}, f32[4,32,512]{2,1,0:T(8,128)}, f32[4,32,512]{2,1,0:T(8,128)}, f32[4,32,512]{2,1,0:T(8,128)}, /*index=5*/f32[8,48,512]{2,1,0:T(8,128)S(1)}) custom-call(f32[4,32,512]{2,1,0:T(8,128)} %u.5, f32[4,32,512]{2,1,0:T(8,128)} %a.5, f32[4,32,512]{2,1,0:T(8,128)} %u1_.3, f32[4,32,512]{2,1,0:T(8,128)} %v.7, ...), custom_call_target="tpu_custom_call" | custom-call | tf_op jit(solution)/shard_map/wave_step/pallas_call | solution.py:624
  35.8 3.4 %all-to-all-done = f32[64,1,128]{2,1,0:T(1,128)S(1)} async-done(((f32[64,1,128]{2,1,0:T(1,128)}), f32[64,1,128]{2,1,0:T(1,128)S(1)}, u32[]{:S(2)}, u32[]{:S(2)}) %all-to-all-start) | async-done | bytes 32800 | tf_op jit(solution)/shard_map/all_to_all | solution.py:622
  39.2 2.9 %adjoint_step.1 = (f32[4,32,512]{2,1,0:T(8,128)}, f32[4,32,512]{2,1,0:T(8,128)}, f32[4,32,512]{2,1,0:T(8,128)}) custom-call(f32[4,32,512]{2,1,0:T(8,128)} %v.7, f32[8,48,512]{2,1,0:T(8,128)S(1)} %get-tuple-element.51.a0p, f32[4,32,512]{2,1,0:T(8,128)} %get-tuple-element.52.w, f32[4,32,512]{2,1,0:T(8,128)} %get-tuple-element.53.gp, ...), custom_call_target="tpu_custom_call" | custom-call | tf_op jit(solution)/shard_map/adjoint_step/pallas_call | solution.py:636
  (3 shorter events, 0.0 us)
Async XLA Ops:
  0.6 8.2 %copy-start.3 = (f32[4,32,512]{2,1,0:T(8,128)S(1)}, f32[4,32,512]{2,1,0:T(8,128)}, u32[]{:S(2)}) copy-start(f32[4,32,512]{2,1,0:T(8,128)} %u1_.3) | copy-start | bytes 786436
  0.6 8.2 %copy-start.2 = (f32[4,32,512]{2,1,0:T(8,128)S(1)}, f32[4,32,512]{2,1,0:T(8,128)}, u32[]{:S(2)}) copy-start(f32[4,32,512]{2,1,0:T(8,128)} %a.5) | copy-start | bytes 786436
  0.7 8.2 %copy-start.4 = (f32[4,32,512]{2,1,0:T(8,128)S(1)}, f32[4,32,512]{2,1,0:T(8,128)}, u32[]{:S(2)}) copy-start(f32[4,32,512]{2,1,0:T(8,128)} %a1.1) | copy-start | bytes 786436
  0.7 8.2 %copy-start = (f32[4,32,512]{2,1,0:T(8,128)S(1)}, f32[4,32,512]{2,1,0:T(8,128)}, u32[]{:S(2)}) copy-start(f32[4,32,512]{2,1,0:T(8,128)} %v.7) | copy-start | bytes 786436
  0.7 8.1 %copy-start.1 = (f32[4,32,512]{2,1,0:T(8,128)S(1)}, f32[4,32,512]{2,1,0:T(8,128)}, u32[]{:S(2)}) copy-start(f32[4,32,512]{2,1,0:T(8,128)} %u.5) | copy-start | bytes 786436
  2.7 10.0 %collective-permute-start = (f32[168,128]{1,0:T(8,128)S(1)}, f32[168,128]{1,0:T(8,128)S(1)}, u32[]{:S(2)}, u32[]{:S(2)}) collective-permute-start(f32[168,128]{1,0:T(8,128)S(1)} %get-tuple-element.33), channel_id=1, source_target_pairs={{0,1},{1,0},{2,3},{3,2},{4,5},{5,4},{6,7},{7,6},{8,9},{9,8},{10,11... | collective-permute-start | bytes 258056 | tf_op jit(solution)/shard_map/ppermute | solution.py:561
  6.5 3.3 %copy-start.5 = (s32[3,4096]{1,0:T(4,128)S(1)}, s32[3,4096]{1,0:T(4,128)}, u32[]{:S(2)}) copy-start(s32[3,4096]{1,0:T(4,128)} %rec.1) | copy-start | bytes 147460
  6.5 7.4 %collective-permute-start.1 = (f32[160,128]{1,0:T(8,128)S(1)}, f32[160,128]{1,0:T(8,128)S(1)}, u32[]{:S(2)}, u32[]{:S(2)}) collective-permute-start(f32[160,128]{1,0:T(8,128)S(1)} %get-tuple-element.40), channel_id=1, source_target_pairs={{0,7},{1,2},{2,1},{3,4},{4,3},{5,6},{6,5},{7,0},{8,15},{9,10},{10,... | collective-permute-start | bytes 245768 | tf_op jit(solution)/shard_map/ppermute | solution.py:561
  12.7 3.4 %collective-permute-start.3 = (f32[1,128]{1,0:T(1,128)S(1)}, f32[1,128]{1,0:T(1,128)S(1)}, u32[]{:S(2)}, u32[]{:S(2)}) collective-permute-start(f32[1,128]{1,0:T(1,128)S(1)} %slice_add_fusion), channel_id=1, source_target_pairs={{0,8},{8,0},{1,9},{9,1},{2,10},{10,2},{3,11},{11,3},{4,12},{12,4},... | collective-permute-start | bytes 1544 | tf_op jit(solution)/shard_map/ppermute | solution.py:561
  14.4 15.5 %collective-permute-start.2 = (f32[2,168,512]{2,1,0:T(8,128)S(1)}, f32[2,168,512]{2,1,0:T(8,128)S(1)}, u32[]{:S(2)}, u32[]{:S(2)}) collective-permute-start(f32[2,168,512]{2,1,0:T(8,128)S(1)} %get-tuple-element.43), channel_id=1, source_target_pairs={{0,8},{8,0},{16,24},{24,16},{32,40},{40,32},{48,56},{56,48},{64,72... | collective-permute-start | bytes 2064392 | tf_op jit(solution)/shard_map/ppermute | solution.py:561
  16.1 13.8 %collective-permute-start.4 = (f32[2,168,512]{2,1,0:T(8,128)S(1)}, f32[2,168,512]{2,1,0:T(8,128)}, u32[]{:S(2)}, u32[]{:S(2)}) collective-permute-start(f32[2,168,512]{2,1,0:T(8,128)S(1)} %get-tuple-element.46), channel_id=1, source_target_pairs={{8,16},{24,32},{40,48},{56,64},{72,80},{88,96},{104,112},{120,128}... | collective-permute-start | bytes 2064392 | tf_op jit(solution)/shard_map/ppermute | solution.py:566
  20.2 19.0 %all-to-all-start = ((f32[64,1,128]{2,1,0:T(1,128)}), f32[64,1,128]{2,1,0:T(1,128)S(1)}, u32[]{:S(2)}, u32[]{:S(2)}) async-start(f32[64,1,128]{2,1,0:T(1,128)} %broadcast_in_dim.2), calls=%async_computation | async-start | bytes 65536 | tf_op jit(solution)/shard_map/all_to_all | solution.py:622
  29.9 0.9 %copy-start.6 = (f32[2,168,512]{2,1,0:T(8,128)}, f32[2,168,512]{2,1,0:T(8,128)S(1)}, u32[]{:S(2)}) copy-start(f32[2,168,512]{2,1,0:T(8,128)S(1)} %collective-permute-done.2.rc) | copy-start | bytes 2064388

commit v11 on v9

--- a/solution.py
+++ b/solution.py
@@ -307,7 +307,7 @@
 
         return lax.while_loop(lambda carry: carry[0] != 0, bit_step, (words[0, w], count))[1]
 
-    count = lax.fori_loop(0, 128, word_step, 0, unroll=8)
+    count = lax.fori_loop(0, 128, word_step, 0, unroll=32)
     found[0, 0] = count
     for k in range(GROUP - 1):
         found[0, count + 1 + k] = 0
@@ -613,8 +613,8 @@
         [part] * 5,
     )(u, a, v, rh, rg, u0p, a0p)
 
-    zc, zb, four = lax.optimization_barrier((zc, zb, four))
     rc = swap(zc, GZ, NZ_DEV, 0)
+    zb, four = lax.optimization_barrier((zb, four))
     rb = swap_open(zb, GZ, NZ_DEV)
     table = lax.all_to_all(jnp.broadcast_to(four, (64, 128)), ("yl", "z", "x"), 0, 0, tiled=True)
 

time: 42.3 us -> 42.3 us (level)
  transfers between devices with their start and end apart: 6 -> 6, of which waited for: 2 -> 1; matrix products, arithmetic and copies ran while one was open for 2% -> 2% of each run, Pallas kernels for 22% -> 22%
where the time goes in v11:
time: 42.3 us; the launch traced here: 42.1 us
  starting transfers between devices  22.2 us (52%)
  Pallas kernels  14.1 us (33%)
  waiting for transfers between devices  3.46 us (8%)
  local copies, waits for them, and re-layouts  1.52 us (4%)
  between operations  0.79 us (2%)
    all_to_all x1, starting transfers between devices, shards(): lax.all_to_all(jnp.broadcast_to(four, (64, 128)), ('yl', 'z', 'x'), 0, 0,...  9.66 us
    ppermute x4, starting transfers between devices, swap(): return lax.ppermute(value, axis, pairs)  9.11 us
    pallas_call x1, Pallas kernels, shards(): call(wave_step, (block,) * 2 + (block_hbm,) * 3 + (frame,), [anywhere()]...  5 us
    ppermute x1, starting transfers between devices, swap_open(): return lax.ppermute(value, axis, pairs + [(j, i) for i, j in pairs])  3.46 us
    all_to_all x1, waiting for transfers between devices, shards(): lax.all_to_all(jnp.broadcast_to(four, (64, 128)), ('yl', 'z', 'x'), 0, 0,...  3.45 us
    pallas_call x1, Pallas kernels, shards(): call(adjoint_step, (block,) * 3, [anywhere(), vmem()] + [anywhere()] * 6,...  2.92 us
    pallas_call x1, Pallas kernels, shards(): call(list_receivers, (jax.ShapeDtypeStruct((1, 128), jnp.int32), jax.Shap...  2.78 us
    pallas_call x1, Pallas kernels, shards(): call(pack_y, (f32(YROWS + 8, 128), f32(YROWS, 128), f32(1, 128)), [anywhe...  1.97 us
  transfers between devices with their start and end apart: 6, of which 1 were waited for; matrix products, arithmetic and copies ran while one was open for 2% of the time, Pallas kernels for 22%

profile of v11, /device:TPU:1, one launch (start us, length us, event | category | flops | bytes accessed | tf_op | source)
XLA Modules:
  0.0 42.1 jit_solution(17957796698171441111)
XLA Ops:
  0.6 0.0 copy-start.3
  0.6 0.0 copy-start.2
  0.7 0.0 copy-start.4
  0.7 0.0 copy-start
  0.7 0.0 copy-start.1
  0.7 2.0 %pack_y.1 = (f32[168,128]{1,0:T(8,128)S(1)}, f32[160,128]{1,0:T(8,128)S(1)}, f32[1,128]{1,0:T(1,128)S(1)}) custom-call(f32[4,32,512]{2,1,0:T(8,128)} %u.5, f32[4,32,512]{2,1,0:T(8,128)} %a.5, f32[4,32,512]{2,1,0:T(8,128)} %u1_.3, f32[4,32,512]{2,1,0:T(8,128)} %a1.1, f32[4,32,512]{2,1,0:T(8,128)} %v.7, f32[2,16]{1,0:T(2,128)} %obs.1), custom_call_target="tpu_custom_call" | custom-call | tf_op jit(solution)/shard_map/pack_y/pallas_call | solution.py:579
  2.7 3.8 %collective-permute-start = (f32[168,128]{1,0:T(8,128)S(1)}, f32[168,128]{1,0:T(8,128)S(1)}, u32[]{:S(2)}, u32[]{:S(2)}) collective-permute-start(f32[168,128]{1,0:T(8,128)S(1)} %get-tuple-element.33), channel_id=1, source_target_pairs={{0,1},{1,0},{2,3},{3,2},{4,5},{5,4},{6,7},{7,6},{8,9},{9,8},{10,11... | collective-permute-start | bytes 258056 | tf_op jit(solution)/shard_map/ppermute | solution.py:558
  6.5 2.3 %collective-permute-start.1 = (f32[160,128]{1,0:T(8,128)S(1)}, f32[160,128]{1,0:T(8,128)S(1)}, u32[]{:S(2)}, u32[]{:S(2)}) collective-permute-start(f32[160,128]{1,0:T(8,128)S(1)} %get-tuple-element.40), channel_id=1, source_target_pairs={{0,7},{1,2},{2,1},{3,4},{4,3},{5,6},{6,5},{7,0},{8,15},{9,10},{10,... | collective-permute-start | bytes 245768 | tf_op jit(solution)/shard_map/ppermute | solution.py:558
  8.8 0.0 copy-done.3
  8.8 0.0 copy-done.2
  8.8 0.0 copy-done.4
  8.8 0.0 copy-done
  8.8 0.0 copy-done.1
  8.8 1.0 %own_step.1 = (f32[4,32,512]{2,1,0:T(8,128)S(1)}, f32[4,32,512]{2,1,0:T(8,128)S(1)}) custom-call(f32[4,32,512]{2,1,0:T(8,128)S(1)} %copy-done.1, f32[4,32,512]{2,1,0:T(8,128)S(1)} %copy-done.2, f32[4,32,512]{2,1,0:T(8,128)S(1)} %copy-done.3, f32[4,32,512]{2,1,0:T(8,128)S(1)} %copy-done.4, f32[4,32,512]{2,1,0:T(8,128)S(1)} %copy-done), custom_call_target="tpu_custom_call" | custom-call | tf_op jit(solution)/shard_map/own_step/pallas_call | solution.py:606
  9.8 0.0 copy-done.5
  9.8 2.8 %list_receivers.1 = (s32[1,128]{1,0:T(1,128)S(1)}, s32[1,4224]{1,0:T(1,128)S(1)}) custom-call(s32[3,4096]{1,0:T(4,128)S(1)} %copy-done.5), custom_call_target="tpu_custom_call" | custom-call | tf_op jit(solution)/shard_map/list_receivers/pallas_call | solution.py:590
  12.6 0.0 collective-permute-done.rh
  12.6 1.3 %collective-permute-start.3 = (f32[1,128]{1,0:T(1,128)S(1)}, f32[1,128]{1,0:T(1,128)S(1)}, u32[]{:S(2)}, u32[]{:S(2)}) collective-permute-start(f32[1,128]{1,0:T(1,128)S(1)} %slice_add_fusion), channel_id=1, source_target_pairs={{0,8},{8,0},{1,9},{9,1},{2,10},{10,2},{3,11},{11,3},{4,12},{12,4},... | collective-permute-start | bytes 1544 | tf_op jit(solution)/shard_map/ppermute | solution.py:558
  13.9 0.0 collective-permute-done.1.rg
  13.9 0.5 %edge_step.1 = (f32[2,4,8,512]{3,2,1,0:T(8,128)S(1)}, f32[2,4,8,512]{3,2,1,0:T(8,128)S(1)}, f32[2,168,512]{2,1,0:T(8,128)S(1)}, f32[2,168,512]{2,1,0:T(8,128)S(1)}) custom-call(f32[4,32,512]{2,1,0:T(8,128)S(1)} %copy-done.1, f32[4,32,512]{2,1,0:T(8,128)S(1)} %copy-done.2, f32[4,32,512]{2,1,0:T(8,128)S(1)} %copy-done, ...), custom_call_target="tpu_custom_call" | custom-call | tf_op jit(solution)/shard_map/edge_step/pallas_call | solution.py:609
  14.4 1.7 %collective-permute-start.2 = (f32[2,168,512]{2,1,0:T(8,128)S(1)}, f32[2,168,512]{2,1,0:T(8,128)S(1)}, u32[]{:S(2)}, u32[]{:S(2)}) collective-permute-start(f32[2,168,512]{2,1,0:T(8,128)S(1)} %get-tuple-element.43), channel_id=1, source_target_pairs={{0,8},{8,0},{16,24},{24,16},{32,40},{40,32},{48,56},{56,48},{64,72... | collective-permute-start | bytes 2064392 | tf_op jit(solution)/shard_map/ppermute | solution.py:558
  16.1 0.0 collective-permute-done.3
  16.1 3.5 %collective-permute-start.4 = (f32[2,168,512]{2,1,0:T(8,128)S(1)}, f32[2,168,512]{2,1,0:T(8,128)}, u32[]{:S(2)}, u32[]{:S(2)}) collective-permute-start(f32[2,168,512]{2,1,0:T(8,128)S(1)} %get-tuple-element.46), channel_id=1, source_target_pairs={{8,16},{24,32},{40,48},{56,64},{72,80},{88,96},{104,112},{120,128}... | collective-permute-start | bytes 2064392 | tf_op jit(solution)/shard_map/ppermute | solution.py:563
  19.6 0.6 %broadcast_in_dim.2 = f32[64,1,128]{2,1,0:T(1,128)} broadcast(f32[128]{0:T(128)S(1)} %bitcast.3), dimensions={2} | broadcast | bytes 33280 | tf_op jit(solution)/shard_map/broadcast_in_dim | solution.py:619
  20.2 9.7 %all-to-all-start = ((f32[64,1,128]{2,1,0:T(1,128)}), f32[64,1,128]{2,1,0:T(1,128)S(1)}, u32[]{:S(2)}, u32[]{:S(2)}) async-start(f32[64,1,128]{2,1,0:T(1,128)} %broadcast_in_dim.2), calls=%async_computation | async-start | bytes 65536 | tf_op jit(solution)/shard_map/all_to_all | solution.py:619
  29.9 0.0 collective-permute-done.2.rc
  29.9 0.0 copy-start.6
  29.9 0.0 collective-permute-done.4.rb
  29.9 0.8 %copy-done.6 = f32[2,168,512]{2,1,0:T(8,128)} copy-done((f32[2,168,512]{2,1,0:T(8,128)}, f32[2,168,512]{2,1,0:T(8,128)S(1)}, u32[]{:S(2)}) %copy-start.6) | copy-done | bytes 688152
  30.7 5.0 %wave_step.1 = (f32[4,32,512]{2,1,0:T(8,128)}, f32[4,32,512]{2,1,0:T(8,128)}, f32[4,32,512]{2,1,0:T(8,128)}, f32[4,32,512]{2,1,0:T(8,128)}, f32[4,32,512]{2,1,0:T(8,128)}, /*index=5*/f32[8,48,512]{2,1,0:T(8,128)S(1)}) custom-call(f32[4,32,512]{2,1,0:T(8,128)} %u.5, f32[4,32,512]{2,1,0:T(8,128)} %a.5, f32[4,32,512]{2,1,0:T(8,128)} %u1_.3, f32[4,32,512]{2,1,0:T(8,128)} %v.7, ...), custom_call_target="tpu_custom_call" | custom-call | tf_op jit(solution)/shard_map/wave_step/pallas_call | solution.py:621
  35.7 3.4 %all-to-all-done = f32[64,1,128]{2,1,0:T(1,128)S(1)} async-done(((f32[64,1,128]{2,1,0:T(1,128)}), f32[64,1,128]{2,1,0:T(1,128)S(1)}, u32[]{:S(2)}, u32[]{:S(2)}) %all-to-all-start) | async-done | bytes 32800 | tf_op jit(solution)/shard_map/all_to_all | solution.py:619
  39.2 2.9 %adjoint_step.1 = (f32[4,32,512]{2,1,0:T(8,128)}, f32[4,32,512]{2,1,0:T(8,128)}, f32[4,32,512]{2,1,0:T(8,128)}) custom-call(f32[4,32,512]{2,1,0:T(8,128)} %v.7, f32[8,48,512]{2,1,0:T(8,128)S(1)} %get-tuple-element.51.a0p, f32[4,32,512]{2,1,0:T(8,128)} %get-tuple-element.52.w, f32[4,32,512]{2,1,0:T(8,128)} %get-tuple-element.53.gp, ...), custom_call_target="tpu_custom_call" | custom-call | tf_op jit(solution)/shard_map/adjoint_step/pallas_call | solution.py:633
  (3 shorter events, 0.0 us)
Async XLA Ops:
  0.6 8.2 %copy-start.3 = (f32[4,32,512]{2,1,0:T(8,128)S(1)}, f32[4,32,512]{2,1,0:T(8,128)}, u32[]{:S(2)}) copy-start(f32[4,32,512]{2,1,0:T(8,128)} %u1_.3) | copy-start | bytes 786436
  0.6 8.2 %copy-start.2 = (f32[4,32,512]{2,1,0:T(8,128)S(1)}, f32[4,32,512]{2,1,0:T(8,128)}, u32[]{:S(2)}) copy-start(f32[4,32,512]{2,1,0:T(8,128)} %a.5) | copy-start | bytes 786436
  0.7 8.2 %copy-start.4 = (f32[4,32,512]{2,1,0:T(8,128)S(1)}, f32[4,32,512]{2,1,0:T(8,128)}, u32[]{:S(2)}) copy-start(f32[4,32,512]{2,1,0:T(8,128)} %a1.1) | copy-start | bytes 786436
  0.7 8.2 %copy-start = (f32[4,32,512]{2,1,0:T(8,128)S(1)}, f32[4,32,512]{2,1,0:T(8,128)}, u32[]{:S(2)}) copy-start(f32[4,32,512]{2,1,0:T(8,128)} %v.7) | copy-start | bytes 786436
  0.7 8.1 %copy-start.1 = (f32[4,32,512]{2,1,0:T(8,128)S(1)}, f32[4,32,512]{2,1,0:T(8,128)}, u32[]{:S(2)}) copy-start(f32[4,32,512]{2,1,0:T(8,128)} %u.5) | copy-start | bytes 786436
  2.7 9.9 %collective-permute-start = (f32[168,128]{1,0:T(8,128)S(1)}, f32[168,128]{1,0:T(8,128)S(1)}, u32[]{:S(2)}, u32[]{:S(2)}) collective-permute-start(f32[168,128]{1,0:T(8,128)S(1)} %get-tuple-element.33), channel_id=1, source_target_pairs={{0,1},{1,0},{2,3},{3,2},{4,5},{5,4},{6,7},{7,6},{8,9},{9,8},{10,11... | collective-permute-start | bytes 258056 | tf_op jit(solution)/shard_map/ppermute | solution.py:558
  6.5 3.3 %copy-start.5 = (s32[3,4096]{1,0:T(4,128)S(1)}, s32[3,4096]{1,0:T(4,128)}, u32[]{:S(2)}) copy-start(s32[3,4096]{1,0:T(4,128)} %rec.1) | copy-start | bytes 147460
  6.5 7.4 %collective-permute-start.1 = (f32[160,128]{1,0:T(8,128)S(1)}, f32[160,128]{1,0:T(8,128)S(1)}, u32[]{:S(2)}, u32[]{:S(2)}) collective-permute-start(f32[160,128]{1,0:T(8,128)S(1)} %get-tuple-element.40), channel_id=1, source_target_pairs={{0,7},{1,2},{2,1},{3,4},{4,3},{5,6},{6,5},{7,0},{8,15},{9,10},{10,... | collective-permute-start | bytes 245768 | tf_op jit(solution)/shard_map/ppermute | solution.py:558
  12.6 3.5 %collective-permute-start.3 = (f32[1,128]{1,0:T(1,128)S(1)}, f32[1,128]{1,0:T(1,128)S(1)}, u32[]{:S(2)}, u32[]{:S(2)}) collective-permute-start(f32[1,128]{1,0:T(1,128)S(1)} %slice_add_fusion), channel_id=1, source_target_pairs={{0,8},{8,0},{1,9},{9,1},{2,10},{10,2},{3,11},{11,3},{4,12},{12,4},... | collective-permute-start | bytes 1544 | tf_op jit(solution)/shard_map/ppermute | solution.py:558
  14.4 15.5 %collective-permute-start.2 = (f32[2,168,512]{2,1,0:T(8,128)S(1)}, f32[2,168,512]{2,1,0:T(8,128)S(1)}, u32[]{:S(2)}, u32[]{:S(2)}) collective-permute-start(f32[2,168,512]{2,1,0:T(8,128)S(1)} %get-tuple-element.43), channel_id=1, source_target_pairs={{0,8},{8,0},{16,24},{24,16},{32,40},{40,32},{48,56},{56,48},{64,72... | collective-permute-start | bytes 2064392 | tf_op jit(solution)/shard_map/ppermute | solution.py:558
  16.1 13.8 %collective-permute-start.4 = (f32[2,168,512]{2,1,0:T(8,128)S(1)}, f32[2,168,512]{2,1,0:T(8,128)}, u32[]{:S(2)}, u32[]{:S(2)}) collective-permute-start(f32[2,168,512]{2,1,0:T(8,128)S(1)} %get-tuple-element.46), channel_id=1, source_target_pairs={{8,16},{24,32},{40,48},{56,64},{72,80},{88,96},{104,112},{120,128}... | collective-permute-start | bytes 2064392 | tf_op jit(solution)/shard_map/ppermute | solution.py:563
  20.2 19.0 %all-to-all-start = ((f32[64,1,128]{2,1,0:T(1,128)}), f32[64,1,128]{2,1,0:T(1,128)S(1)}, u32[]{:S(2)}, u32[]{:S(2)}) async-start(f32[64,1,128]{2,1,0:T(1,128)} %broadcast_in_dim.2), calls=%async_computation | async-start | bytes 65536 | tf_op jit(solution)/shard_map/all_to_all | solution.py:619
  29.9 0.9 %copy-start.6 = (f32[2,168,512]{2,1,0:T(8,128)}, f32[2,168,512]{2,1,0:T(8,128)S(1)}, u32[]{:S(2)}) copy-start(f32[2,168,512]{2,1,0:T(8,128)S(1)} %collective-permute-done.2.rc) | copy-start | bytes 2064388
